TPU v7x, 256 devices: a whole 4x4x8 slice. The times are simulated.
256 devices in a mesh: context: 16 (over z_lo, x), tensor: 16 (over z_hi, y, core).
Axes of the slice: x: 4, y: 4, z: 8 (z_hi: 2, z_lo: 4; z = z_hi * 4 + z_lo), core: 2. Of those that a mesh axis runs over, the one named last changes fastest.
Arguments:
- tokens: bfloat16 [32768, 4096], P(('context', 'tensor')), may hold values from -6 to 6
- norm_gain: bfloat16 [4096], replicated, may hold values from 0.5 to 1.5
- in_weight: bfloat16 [4096, 3, 4096], P(None, None, 'tensor'), may hold values from -0.09375 to 0.09375
- short_filter: bfloat16 [3, 3, 4096], P(None, None, 'tensor'), may hold values from -3.5 to 3.5
- long_filter: bfloat16 [256, 128], P('tensor'), may hold values from -0.5 to 0.5
- doc_start: int32 [32768], P('context'), may hold values from 0 to 32767, as said below
Outputs:
- layer_out: bfloat16 [32768, 4096], P(('context', 'tensor'))
Inputs may be any that keep to these rules, and one draw needn't show every extreme that they name: doc_start[0] = 0, and for t > 0 doc_start[t] is either doc_start[t - 1] or t, so documents are contiguous runs of positions; the last position begins a document.
All inputs are finite; a program needn't handle non-finite values.
Results may differ from a plain program's by a relative error of at most 0.0089.
Values may be sent and summed in bfloat16 or wider, within the bound.
No kernel may reach another device: no remote copies, remote signals or barrier semaphores. Data moves between devices by JAX's collectives and lax.ppermute only.
A program may use at most 128 MiB of HBM per device.

v0:
```python
import jax
import jax.numpy as jnp
from jax import lax
from jax.sharding import PartitionSpec as P


def from_behind(shard, axis, by):
    size = lax.axis_size(axis)
    pairs = [(i, i + by) for i in range(size) if 0 <= i + by < size]
    return lax.ppermute(shard, axis, pairs)


def banded(long_filter, span):
    groups = long_filter.shape[0]
    reversed_pad = jnp.concatenate(
        [long_filter[:, ::-1], jnp.zeros((groups, span), long_filter.dtype)], axis=1
    )
    tiled = jnp.tile(reversed_pad, (1, span))[:, : span * (2 * span - 1)]
    return tiled.reshape(groups, span, 2 * span - 1)


def short_mix(padded, positions, starts, filters):
    out_count = positions.shape[0]
    short_taps = filters.shape[1]
    summed = jnp.zeros((out_count,) + padded.shape[1:], jnp.float32)
    for lag_step in range(short_taps):
        begin = short_taps - 1 - lag_step
        rows_in = lax.slice_in_dim(padded, begin, begin + out_count, axis=0).astype(jnp.float32)
        kept_mask = (positions - lag_step >= starts)[:, None, None]
        summed = summed + jnp.where(
            kept_mask, filters[:, lag_step, :].astype(jnp.float32)[None] * rows_in, 0.0
        )
    return summed


def per_device(tokens, norm_gain, in_weight, short_filter, long_filter, doc_start):
    width = tokens.shape[1]
    channels = in_weight.shape[2]
    groups = long_filter.shape[0]
    span = long_filter.shape[1]
    share = channels // groups
    short_taps = short_filter.shape[1]
    float_tokens = tokens.astype(jnp.float32)
    scale_rows = lax.rsqrt(jnp.mean(float_tokens * float_tokens, axis=-1, keepdims=True) + 1e-06)
    normed = (float_tokens * scale_rows * norm_gain.astype(jnp.float32)[None]).astype(jnp.bfloat16)
    flat_weight = in_weight.reshape(width, 3 * channels)
    projected = jnp.dot(
        lax.all_gather(normed, "tensor", axis=0, tiled=True),
        flat_weight,
        preferred_element_type=jnp.float32,
    ).astype(jnp.bfloat16)
    length = projected.shape[0]
    projected = projected.reshape(length, 3, channels)
    starts = doc_start - lax.axis_index("context") * length
    local_rows = jnp.arange(length, dtype=jnp.int32)
    rim_rows = from_behind(projected[length - (short_taps - 1) :], "context", 1)
    padded = jnp.concatenate([rim_rows, projected], axis=0)
    mixed = short_mix(padded, local_rows, starts, short_filter)
    key_value = (mixed[:, 1] * mixed[:, 2]).astype(jnp.bfloat16)
    tail_rows = from_behind(key_value[length - (span - 1) :], "context", 1)
    query = mixed[:, 0]
    extended = jnp.concatenate([tail_rows, key_value], axis=0)
    blocks = length // span
    head_part = extended[:length].reshape(blocks, span, channels)
    rest_part = jnp.concatenate([extended[span:], jnp.zeros((1, channels), jnp.bfloat16)], axis=0)
    rest_part = rest_part.reshape(blocks, span, channels)[:, : span - 1]
    window = jnp.concatenate([head_part, rest_part], axis=1).reshape(
        blocks, 2 * span - 1, groups, share
    )
    inputs = (
        (jnp.arange(blocks, dtype=jnp.int32) * span)[:, None]
        + jnp.arange(2 * span - 1, dtype=jnp.int32)[None]
        - (span - 1)
    )
    block_starts = starts.reshape(blocks, span)
    kept_mask = inputs[:, None, :] >= block_starts[:, :, None]
    toeplitz = banded(long_filter, span)
    weights = jnp.where(kept_mask[:, None], toeplitz[None], jnp.zeros((), jnp.bfloat16))
    conv = jnp.einsum(
        "bgij,bjgc->bigc", weights, window, preferred_element_type=jnp.float32
    ).reshape(length, channels)
    gated = (query * conv).astype(jnp.bfloat16)
    returned = lax.all_to_all(gated, "tensor", split_axis=0, concat_axis=1, tiled=True)
    return (float_tokens + returned.astype(jnp.float32)).astype(jnp.bfloat16)


def solution(mesh):
    in_specs = (
        P(("context", "tensor"), None),
        P(),
        P(None, None, "tensor"),
        P(None, None, "tensor"),
        P("tensor", None),
        P("context"),
    )
    out_specs = P(("context", "tensor"), None)
    return jax.shard_map(
        per_device, mesh=mesh, in_specs=in_specs, out_specs=out_specs, check_vma=False
    )
```

profile of v0, /device:TPU:70, one launch (start us, length us, event | category | flops | bytes accessed | tf_op | source)
XLA Modules:
  0.0 295.7 jit_solution(7310383108310972181)
XLA Ops:
  7.2 1.5 fusion.6
  8.8 2.5 fusion.8
  11.3 8.8 %copy.11 = bf16[4096,3,256]{0,2,1:T(8,128)(2,1)} copy(bf16[4096,3,256]{2,0,1:T(8,128)(2,1)} %param.8) | data formatting | bytes 12582912 | tf_op args[2]
  21.4 163.9 %all-gather.2.cloned.1.call-done = bf16[2048,4096]{1,0:T(8,128)(2,1)} async-done(((bf16[128,4096]{1,0:T(8,128)(2,1)}), bf16[2048,4096]{1,0:T(8,128)(2,1)}) %all-gather.2.cloned.1.call-update) | async-done | bytes 16777232 | tf_op jit(solution)/shard_map/all_gather | solution.py:48
  185.3 18.2 %convolution_convert_fusion = bf16[2048,768]{1,0:T(8,128)(2,1)S(1)} fusion(bf16[2048,4096]{1,0:T(8,128)(2,1)} %all-gather.2.cloned.1.call-done, bf16[4096,768]{0,1:T(8,128)(2,1)} %bitcast.46), kind=kOutput, calls=%fused_computation.6 | convolution fusion | flops 12886474752 | bytes 26214400 | tf_op jit(solution)/shard_map/dot_general | solution.py:47
  203.5 1.6 copy-done.1
  205.3 1.9 collective-permute-start
  208.4 3.2 %copy.12 = bf16[2048,768]{0,1:T(8,128)(2,1)S(1)} copy(bf16[2048,768]{1,0:T(8,128)(2,1)} %copy-done.1) | data formatting | bytes 6291456 | tf_op jit(solution)/shard_map/convert_element_type | solution.py:51
  211.6 2.6 collective-permute-done
  214.2 5.0 %select_add_fusion = f32[2048,3,256]{0,2,1:T(8,128)S(1)} fusion(bf16[2048,3,256]{0,2,1:T(8,128)(2,1)S(1)} %bitcast.43, bf16[2,3,256]{0,2,1:T(8,128)(2,1)S(1)} %collective-permute-done, f32[3,256]{1,0:T(4,128)} %get-tuple-element.13, f32[3,256]{1,0:T(4,128)} %get-tuple-element.14, f32[3,256]{1,0:T(4,128)} %bitcast.56, pred[2048]{0:T(1024)(128)(4,1)} %get-tuple-element.9, ...), kind=kLoop, calls=%fused_computation.5 | loop fusion | flops 26738688 | bytes 9455616 | tf_op jit(solution)/shard_map/add | solution.py:30
  219.3 1.9 slice_bitcast_fusion
  221.2 4.5 %collective-permute-start.1 = (bf16[127,256]{0,1:T(8,128)(2,1)S(1)}, bf16[127,256]{0,1:T(8,128)(2,1)S(1)}, u32[]{:S(2)}, u32[]{:S(2)}) collective-permute-start(bf16[127,256]{0,1:T(8,128)(2,1)S(1)} %slice_bitcast_fusion.1), channel_id=1, source_target_pairs={{0,16},{16,32},{32,48},{48,64},{64,80},{80,96},{96,112},{112,128},... | collective-permute-start | bytes 195080 | tf_op jit(solution)/shard_map/ppermute | solution.py:10
  225.7 1.2 broadcast_compare_fusion
  227.7 4.3 %broadcast_in_dim.65 = bf16[16,128,255]{2,1,0:T(8,128)(2,1)} reshape(bf16[16,32640]{1,0:T(8,128)(2,1)S(1)} %slice.77) | data formatting | bytes 2088960 | tf_op jit(solution)/shard_map/jit(_where)/broadcast_in_dim | solution.py:78
  233.6 1.4 copy.27
  235.0 2.0 copy.28
  237.1 1.2 pad_maximum_fusion.1
  238.3 1.5 copy.16
  240.4 0.7 copy-done.2
  241.1 5.8 %fusion = f32[16,16,16,128]{3,2,1,0:T(8,128)S(1)} fusion(pred[16,128,255]{2,1,0:T(8,128)(4,1)} %broadcast_compare_fusion, bf16[16,128,255]{2,1,0:T(8,128)(2,1)S(1)} %copy-done.2, bf16[16,127,16,16]{1,3,2,0:T(8,128)(2,1)} %bitcast.54, bf16[16,128,16,16]{1,3,2,0:T(8,128)(2,1)S(1)} %copy.19), kind=kOutput, calls=%fused_computation | convolution fusion | flops 279920640 | bytes 5752832 | tf_op jit(solution)/shard_map/bgij,bjgc->bigc/dot_general | solution.py:79
  246.9 0.7 fusion.14
  247.6 36.4 %all_to_all.10 = bf16[16,128,256]{1,2,0:T(8,128)(2,1)S(1)} all-to-all(bf16[16,128,256]{1,2,0:T(8,128)(2,1)S(1)} %fusion.14), channel_id=1, replica_groups=mesh['context'=16,'tensor'=16] {'tensor'}, dimensions={0} | all-to-all | bytes 2097152 | tf_op jit(solution)/shard_map/all_to_all | solution.py:83
  284.2 1.8 copy.23
  286.0 2.8 fusion.9
  (40 shorter events, 6.7 us)
Async XLA Ops:
  6.5 178.7 %all-gather.2.cloned.1.call-start = ((), (), s32[]{:S(2)}) async-start(), calls=%async_computation.1 | async-start | bytes 17825792 | tf_op jit(solution)/shard_map/all_gather | solution.py:48
  11.3 8.8 %copy-start.5 = (bf16[3,3,256]{2,1,0:T(4,128)(2,1)S(1)}, bf16[3,3,256]{2,1,0:T(4,128)(2,1)}, u32[]{:S(2)}) copy-start(bf16[3,3,256]{2,1,0:T(4,128)(2,1)} %param.9) | copy-start | bytes 13828
  11.3 9.4 %copy-start.4 = (s32[2048]{0:T(1024)S(1)}, s32[2048]{0:T(1024)}, u32[]{:S(2)}) copy-start(s32[2048]{0:T(1024)} %param.11) | copy-start | bytes 24580
  203.5 1.6 copy-start.1
  205.3 9.0 %collective-permute-start = (bf16[2,3,256]{0,2,1:T(8,128)(2,1)S(1)}, bf16[2,3,256]{0,2,1:T(8,128)(2,1)S(1)}, u32[]{:S(2)}, u32[]{:S(2)}) collective-permute-start(bf16[2,3,256]{0,2,1:T(8,128)(2,1)S(1)} %bitcast.55), channel_id=1, source_target_pairs={{0,16},{16,32},{32,48},{48,64},{64,80},{80,96},{96,112},{112,128},... | collective-permute-start | bytes 9224 | tf_op jit(solution)/shard_map/ppermute | solution.py:10
  219.2 6.5 %copy-start.3 = (s32[16,128]{1,0:T(8,128)S(1)}, s32[16,128]{1,0:T(8,128)}, u32[]{:S(2)}) copy-start(s32[16,128]{1,0:T(8,128)} %subtract_bitcast_fusion) | copy-start | bytes 24580
  219.2 7.6 %copy-start.6 = (bf16[16,128]{1,0:T(8,128)(2,1)S(1)}, bf16[16,128]{1,0:T(8,128)(2,1)}, u32[]{:S(2)}) copy-start(bf16[16,128]{1,0:T(8,128)(2,1)} %param.10) | copy-start | bytes 12292
  221.2 15.8 %collective-permute-start.1 = (bf16[127,256]{0,1:T(8,128)(2,1)S(1)}, bf16[127,256]{0,1:T(8,128)(2,1)S(1)}, u32[]{:S(2)}, u32[]{:S(2)}) collective-permute-start(bf16[127,256]{0,1:T(8,128)(2,1)S(1)} %slice_bitcast_fusion.1), channel_id=1, source_target_pairs={{0,16},{16,32},{32,48},{48,64},{64,80},{80,96},{96,112},{112,128},... | collective-permute-start | bytes 195080 | tf_op jit(solution)/shard_map/ppermute | solution.py:10
  239.8 1.2 copy-start.2
  284.0 2.0 copy-start
Sparse Core Ops, SparseCore 0:
  11.4 173.7 all-gather.1
where the time goes:
time: 296 us
  waiting for transfers between devices  167 us (56%)
  blocking collectives  36.4 us (12%)
  local copies, waits for them, and re-layouts  29.7 us (10%)
  matrix products  24 us (8%)
  other arithmetic  19 us (6%)
  between operations  13.6 us (5%)
  starting transfers between devices  6.41 us (2%)
    all_gather x1, waiting for transfers between devices, per_device(): lax.all_gather(normed, 'tensor', axis=0, tiled=True)  164 us
    all_to_all x1, blocking collectives, per_device(): lax.all_to_all(gated, 'tensor', split_axis=0, concat_axis=1, tiled=True)  36.4 us
    dot_general x1, matrix products, per_device(): jnp.dot(lax.all_gather(normed, 'tensor', axis=0, tiled=True), flat_weight...  18.2 us
    unnamed x21, local copies, waits for them, and re-layouts  16.5 us
    ppermute x2, starting transfers between devices, from_behind(): return lax.ppermute(shard, axis, pairs)  6.41 us
  transfers between devices with their start and end apart: 3, of which 2 were waited for; matrix products, arithmetic and copies ran while one was open for 9% of the time, Pallas kernels for 0%

commit v1 on v0

v1 whole, which is shorter than its diff:
```python
import functools

import jax
import jax.numpy as jnp
from jax import lax
from jax.experimental import pallas as pl
from jax.experimental.pallas import tpu as pltpu
from jax.sharding import Mesh
from jax.sharding import PartitionSpec as P

AXES = ("z_lo", "x", "z_hi", "y", "core")
SPAN = 128
RIM = 16


def swap(value, axis):
    return lax.ppermute(value, axis, [(0, 1), (1, 0)])


def banded(long_filter):
    groups, span = long_filter.shape
    period = 3 * span
    row = jnp.concatenate([long_filter, jnp.zeros((groups, period - span), long_filter.dtype)], axis=1)
    tiled = jnp.tile(row, (1, 2 * span))[:, : 2 * span * (period - 1)]
    skewed = tiled.reshape(groups, 2 * span, period - 1)
    return skewed[:, :, span : 2 * span]


def gather_tokens(normed):
    rows, width = normed.shape
    y, core = lax.axis_index("y"), lax.axis_index("core")
    size = lax.axis_size("y")
    sib = swap(normed, "core")
    first = jnp.where(core == 0, normed, sib)
    second = jnp.where(core == 0, sib, normed)
    pair = jnp.concatenate([first, second], axis=0)
    ring = [
        (2 * i + c, 2 * ((i + (1 if c == 0 else -1)) % size) + c) for i in range(size) for c in range(2)
    ]
    near = lax.ppermute(pair, ("y", "core"), ring)
    near_half = lax.dynamic_slice_in_dim(near, core * rows, rows, 0)
    far = lax.ppermute(near_half, ("y", "core"), ring)
    near_sib = swap(near, "core")
    far_sib = swap(far, "core")
    sign = 1 - 2 * core
    full = jnp.zeros((2 * size * rows, width), normed.dtype)
    put = lambda full, value, at: lax.dynamic_update_slice_in_dim(full, value, at * rows, 0)
    full = put(full, pair, 2 * y)
    full = put(full, near, 2 * ((y - sign + size) % size))
    full = put(full, near_sib, 2 * ((y + sign + size) % size))
    full = put(full, far, 2 * ((y + 2) % size) + core)
    full = put(full, far_sib, 2 * ((y + 2) % size) + 1 - core)
    return full


def mix_conv_kernel(
    flags, proj, halo, short, band, start_col, start_row, out, key_value_t, query, conv_t
):
    length, channels = out.shape
    groups = band.shape[0]
    share = channels // groups
    blocks = length // SPAN
    taps = short.shape[0] // 3
    key_value_t[:, 0:SPAN] = halo[0:SPAN, :].astype(jnp.float32).T.astype(jnp.bfloat16)
    for b in range(blocks):
        rows = slice(b * SPAN, (b + 1) * SPAN)
        starts = start_col[rows, :]
        places = b * SPAN + lax.broadcasted_iota(jnp.int32, (SPAN, 1), 0)
        mixed = []
        for m in range(3):
            cols = slice(m * channels, (m + 1) * channels)
            if b == 0:
                before = halo[SPAN + m * RIM : SPAN + (m + 1) * RIM, :]
            else:
                before = proj[b * SPAN - RIM : b * SPAN, cols]
            both = jnp.concatenate([before, proj[rows, cols]], axis=0).astype(jnp.float32)
            total = None
            for s in range(taps):
                term = short[m * taps + s : m * taps + s + 1, :] * both[RIM - s : RIM - s + SPAN]
                term = jnp.where(places - s >= starts, term, 0.0)
                total = term if total is None else total + term
            mixed.append(total)
        query[rows, :] = mixed[0]
        key_value_t[:, (b + 1) * SPAN : (b + 2) * SPAN] = (mixed[1] * mixed[2]).T.astype(jnp.bfloat16)
    for g in range(groups):
        rows = slice(g * share, (g + 1) * share)
        windows = jnp.concatenate(
            [key_value_t[rows, b * SPAN : (b + 2) * SPAN] for b in range(blocks)], axis=0
        )
        sums = jnp.dot(windows, band[g], preferred_element_type=jnp.float32)
        for b in range(blocks):
            conv_t[rows, b * SPAN : (b + 1) * SPAN] = sums[b * share : (b + 1) * share]
    for b in range(blocks):

        @pl.when(flags[b] > 0)
        def _(b=b):
            inputs = (b - 1) * SPAN + lax.broadcasted_iota(jnp.int32, (2 * SPAN, SPAN), 0)
            kept = (inputs >= start_row[:, b * SPAN : (b + 1) * SPAN])

            def one_group(g, _):
                rows = pl.ds(pl.multiple_of(g * share, share), share)
                weights = jnp.where(kept, band[g].astype(jnp.float32), 0.0).astype(jnp.bfloat16)
                conv_t[rows, b * SPAN : (b + 1) * SPAN] = jnp.dot(
                    key_value_t[rows, b * SPAN : (b + 2) * SPAN],
                    weights,
                    preferred_element_type=jnp.float32,
                )
                return 0

            lax.fori_loop(0, groups, one_group, 0, unroll=4)

    for b in range(blocks):
        rows = slice(b * SPAN, (b + 1) * SPAN)
        out[rows, :] = (query[rows, :] * conv_t[:, b * SPAN : (b + 1) * SPAN].T).astype(out.dtype)


def mix_conv(proj, halo, short, band, starts):
    length = proj.shape[0]
    channels = proj.shape[1] // 3
    blocks = length // SPAN
    last = starts.reshape(blocks, SPAN)[:, -1]
    flags = (last > jnp.arange(blocks, dtype=jnp.int32) * SPAN - (SPAN - 1)).astype(jnp.int32)
    vmem = pl.BlockSpec(memory_space=pltpu.VMEM)
    return pl.pallas_call(
        mix_conv_kernel,
        out_shape=jax.ShapeDtypeStruct((length, channels), jnp.bfloat16),
        in_specs=[pl.BlockSpec(memory_space=pltpu.SMEM)] + [vmem] * 6,
        out_specs=vmem,
        scratch_shapes=[
            pltpu.VMEM((channels, length + SPAN), jnp.bfloat16),
            pltpu.VMEM((length, channels), jnp.float32),
            pltpu.VMEM((channels, length), jnp.float32),
        ],
        compiler_params=pltpu.CompilerParams(vmem_limit_bytes=24 << 20),
        cost_estimate=pl.CostEstimate(flops=10_000_000_000, bytes_accessed=4_000_000, transcendentals=0),
    )(flags, proj, halo, short, band, starts[:, None], starts[None, :])


def tail_of(proj, short, starts):
    length = proj.shape[0]
    channels = proj.shape[1] // 3
    taps = short.shape[0] // 3
    places = jnp.arange(length - SPAN, length, dtype=jnp.int32)
    mixed = []
    for m in (1, 2):
        total = jnp.zeros((SPAN, channels), jnp.float32)
        for s in range(taps):
            rows = proj[length - SPAN - s : length - s, m * channels : (m + 1) * channels].astype(jnp.float32)
            kept = (places - s >= starts[length - SPAN :])[:, None]
            total = total + jnp.where(kept, short[m * taps + s][None] * rows, 0.0)
        mixed.append(total)
    key_value = (mixed[0] * mixed[1]).astype(jnp.bfloat16)
    rims = [proj[length - RIM :, m * channels : (m + 1) * channels] for m in range(3)]
    return jnp.concatenate([key_value, *rims], axis=0)


def per_device(tokens, norm_gain, in_weight, short_filter, long_filter, doc_start):
    rows, width = tokens.shape
    channels = in_weight.shape[2]
    groups, span = long_filter.shape
    taps = short_filter.shape[1]
    z_lo, x, z_hi = lax.axis_index("z_lo"), lax.axis_index("x"), lax.axis_index("z_hi")
    contexts = lax.axis_size("z_lo") * lax.axis_size("x")
    context = z_lo * lax.axis_size("x") + x
    length = rows * lax.axis_size("y") * lax.axis_size("core")
    starts = lax.dynamic_slice_in_dim(doc_start, z_hi * length, length, 0)
    starts = starts - (context * lax.axis_size("z_hi") + z_hi) * length

    deep = width // contexts
    piece = lax.dynamic_slice_in_dim(in_weight, context * deep, deep, 0).reshape(deep, 3 * channels)
    piece = swap(piece, "z_hi")
    other_weight = lax.all_gather(piece, ("z_lo", "x"), axis=0, tiled=True)

    float_tokens = tokens.astype(jnp.float32)
    scale_rows = lax.rsqrt(jnp.mean(float_tokens * float_tokens, axis=-1, keepdims=True) + 1e-06)
    normed = (float_tokens * scale_rows * norm_gain.astype(jnp.float32)[None]).astype(jnp.bfloat16)
    gathered = gather_tokens(normed)

    small = jnp.concatenate(
        [short_filter.reshape(3 * taps, channels), long_filter.reshape(-1, channels)], axis=0
    )
    small = swap(small, "z_hi")
    other_short, other_long = small[: 3 * taps], small[3 * taps :].reshape(groups, span)

    next_half = [(i, i + 1) for i in range(contexts * lax.axis_size("z_hi") - 1)]

    def project(weight, short):
        projected = jnp.dot(gathered, weight, preferred_element_type=jnp.float32).astype(jnp.bfloat16)
        return projected, lax.ppermute(tail_of(projected, short, starts), ("z_lo", "x", "z_hi"), next_half)

    def finish(projected, halo, short, long):
        gated = mix_conv(projected, halo, short, banded(long), starts)
        return lax.all_to_all(gated, ("y", "core"), split_axis=0, concat_axis=1, tiled=True)

    own_short = short_filter.reshape(3 * taps, channels).astype(jnp.float32)
    other_short = other_short.astype(jnp.float32)
    own_projected, other_halo = project(in_weight.reshape(width, 3 * channels), own_short)
    other_projected, own_halo = project(other_weight, other_short)
    own = finish(own_projected, own_halo, own_short, long_filter)
    other = finish(other_projected, other_halo, other_short, other_long)
    left = jnp.where(z_hi == 0, own, other)
    right = jnp.where(z_hi == 0, other, own)
    gated = jnp.concatenate([left, right], axis=1)
    return (float_tokens + gated.astype(jnp.float32)).astype(jnp.bfloat16)


def solution(mesh):
    fine = Mesh(mesh.devices.reshape(4, 4, 2, 4, 2), AXES)
    context, tensor = ("z_lo", "x"), ("z_hi", "y", "core")
    in_specs = (
        P(context + tensor, None),
        P(),
        P(None, None, tensor),
        P(None, None, tensor),
        P(tensor, None),
        P(context),
    )
    return jax.shard_map(
        per_device, mesh=fine, in_specs=in_specs, out_specs=P(context + tensor, None), check_vma=False
    )
```

time: 296 us -> 214 us (0.72)
  the two profiles are of different devices: /device:TPU:70 before, /device:TPU:1 now
where the time goes in v1:
time: 214 us; the launch traced here: 212 us
  starting transfers between devices  64.8 us (30%)
  local copies, waits for them, and re-layouts  62.1 us (29%)
  waiting for transfers between devices  33.6 us (16%)
  matrix products  20.2 us (9%)
  between operations  13.8 us (6%)
  Pallas kernels  12.3 us (6%)
  other arithmetic  5.52 us (3%)
    ppermute x5, starting transfers between devices, swap(): return lax.ppermute(value, axis, [(0, 1), (1, 0)])  24.2 us
    reshape x2, local copies, waits for them, and re-layouts, banded(): skewed = tiled.reshape(groups, 2 * span, period - 1)  21.2 us
    dot_general x2, matrix products, project(): jnp.dot(gathered, weight, preferred_element_type=jnp.float32)  20.2 us
    all_to_all x2, starting transfers between devices, finish(): lax.all_to_all(gated, ('y', 'core'), split_axis=0, concat_axis=1, tiled=T...  19.2 us
    ppermute x2, starting transfers between devices, project(): lax.ppermute(tail_of(projected, short, starts), ('z_lo', 'x', 'z_hi'), ne...  17.1 us
    unnamed x27, local copies, waits for them, and re-layouts  15.8 us
    pallas_call x2, Pallas kernels, mix_conv(): pl.pallas_call(mix_conv_kernel, out_shape=jax.ShapeDtypeStruct((length, c...  12.3 us
    all_to_all x2, waiting for transfers between devices, finish(): lax.all_to_all(gated, ('y', 'core'), split_axis=0, concat_axis=1, tiled=T...  11.4 us
  transfers between devices with their start and end apart: 12, of which 5 were waited for; matrix products, arithmetic and copies ran while one was open for 35% of the time, Pallas kernels for 6%

profile of v1, /device:TPU:1, one launch (start us, length us, event | category | flops | bytes accessed | tf_op | source)
XLA Modules:
  0.0 212.3 jit_solution(8204453973743429106)
XLA Ops:
  6.5 8.7 %copy.15 = bf16[4096,3,256]{0,2,1:T(8,128)(2,1)} copy(bf16[4096,3,256]{2,0,1:T(8,128)(2,1)} %param.8) | data formatting | bytes 12582912 | tf_op args[2]
  16.3 7.8 %collective-permute-start.6 = (bf16[256,768]{0,1:T(8,128)(2,1)S(1)}, bf16[256,768]{0,1:T(8,128)(2,1)S(1)}, u32[]{:S(2)}, u32[]{:S(2)}) collective-permute-start(bf16[256,768]{0,1:T(8,128)(2,1)S(1)} %bitcast.48), channel_id=1, source_target_pairs={{0,8},{8,0},{1,9},{9,1},{2,10},{10,2},{3,11},{11,3},{4,12},{12,4},... | collective-permute-start | bytes 1179656 | tf_op jit(solution)/shard_map/ppermute | solution.py:17
  24.4 9.0 %collective-permute-done.6 = bf16[256,768]{0,1:T(8,128)(2,1)S(1)} collective-permute-done((bf16[256,768]{0,1:T(8,128)(2,1)S(1)}, bf16[256,768]{0,1:T(8,128)(2,1)S(1)}, u32[]{:S(2)}, u32[]{:S(2)}) %collective-permute-start.6) | collective-permute-done | bytes 393248 | tf_op jit(solution)/shard_map/ppermute | solution.py:17
  36.5 2.3 %collective-permute-done = bf16[128,4096]{1,0:T(8,128)(2,1)S(1)} collective-permute-done((bf16[128,4096]{1,0:T(8,128)(2,1)S(1)}, bf16[128,4096]{1,0:T(8,128)(2,1)S(1)}, u32[]{:S(2)}, u32[]{:S(2)}) %collective-permute-start) | collective-permute-done | bytes 1048608 | tf_op jit(solution)/shard_map/ppermute | solution.py:17
  40.2 4.3 %broadcast_in_dim.85 = bf16[1024,4096]{1,0:T(8,128)(2,1)} broadcast(bf16[]{:T(256)} %constant.73.clone.1), dimensions={} | broadcast | bytes 8388610 | tf_op jit(solution)/shard_map/broadcast_in_dim | solution.py:46
  46.4 2.8 %collective-permute-start.1 = (bf16[256,4096]{1,0:T(8,128)(2,1)S(1)}, bf16[256,4096]{1,0:T(8,128)(2,1)}, u32[]{:S(2)}, u32[]{:S(2)}) collective-permute-start(bf16[256,4096]{1,0:T(8,128)(2,1)S(1)} %get-tuple-element.5), channel_id=1, source_target_pairs={{0,2},{1,7},{2,4},{3,1},{4,6},{5,3},{6,0},{7,5},{8,10},{9,15},{10,... | collective-permute-start | bytes 6291464 | tf_op jit(solution)/shard_map/ppermute | solution.py:40
  49.2 12.1 %collective-permute-start.5 = (bf16[17,256]{1,0:T(8,128)(2,1)S(1)}, bf16[17,256]{1,0:T(8,128)(2,1)S(1)}, u32[]{:S(2)}, u32[]{:S(2)}) collective-permute-start(bf16[17,256]{1,0:T(8,128)(2,1)S(1)} %pad_maximum_fusion.3), channel_id=1, source_target_pairs={{0,8},{8,0},{1,9},{9,1},{2,10},{10,2},{3,11},{11,3},{4,12},{12,4},... | collective-permute-start | bytes 26120 | tf_op jit(solution)/shard_map/ppermute | solution.py:17
  61.3 10.8 %collective-permute-done.1 = bf16[256,4096]{1,0:T(8,128)(2,1)} collective-permute-done((bf16[256,4096]{1,0:T(8,128)(2,1)S(1)}, bf16[256,4096]{1,0:T(8,128)(2,1)}, u32[]{:S(2)}, u32[]{:S(2)}) %collective-permute-start.1) | collective-permute-done | bytes 2097184 | tf_op jit(solution)/shard_map/ppermute | solution.py:40
  72.1 2.0 collective-permute-start.2
  74.1 2.3 %constant_dynamic-slice_fusion.1 = bf16[128,4096]{1,0:T(8,128)(2,1)} fusion(bf16[256,4096]{1,0:T(8,128)(2,1)} %collective-permute-done.1, s32[]{:T(128)S(6)} %select_n.124), kind=kLoop, calls=%fused_computation.26 | loop fusion | bytes 2097156 | tf_op jit(solution)/shard_map/dynamic_slice | solution.py:41
  82.4 10.6 %reshape.61 = bf16[16,256,383]{2,1,0:T(8,128)(2,1)} reshape(bf16[16,98048]{1,0:T(8,128)(2,1)} %slice.180) | data formatting | bytes 6275072 | tf_op jit(solution)/shard_map/reshape | solution.py:25
  98.4 10.6 %reshape.63 = bf16[16,256,383]{2,1,0:T(8,128)(2,1)} reshape(bf16[16,98048]{1,0:T(8,128)(2,1)} %slice.198) | data formatting | bytes 6275072 | tf_op jit(solution)/shard_map/reshape | solution.py:25
  110.7 3.3 %constant_dynamic-update-slice_fusion.3 = bf16[1024,4096]{1,0:T(8,128)(2,1)} fusion(bf16[1024,4096]{1,0:T(8,128)(2,1)} %get-tuple-element.6, bf16[256,4096]{1,0:T(8,128)(2,1)} %collective-permute-done.1, s32[]{:T(128)S(6)} %select_n.121), kind=kLoop, calls=%fused_computation.28 | loop fusion | bytes 4194308 | tf_op jit(solution)/shard_map/dynamic_update_slice | solution.py:47
  114.0 3.3 %constant_dynamic-update-slice_fusion.2 = bf16[1024,4096]{1,0:T(8,128)(2,1)} fusion(bf16[1024,4096]{1,0:T(8,128)(2,1)} %constant_dynamic-update-slice_fusion.3, bf16[256,4096]{1,0:T(8,128)(2,1)} %collective-permute-done.2, s32[]{:T(128)S(6)} %select_n.123), kind=kLoop, calls=%fused_computation.27 | loop fusion | bytes 4194308 | tf_op jit(solution)/shard_map/dynamic_update_slice | solution.py:47
  117.4 2.3 %constant_dynamic-update-slice_fusion.1 = bf16[1024,4096]{1,0:T(8,128)(2,1)} fusion(bf16[1024,4096]{1,0:T(8,128)(2,1)} %constant_dynamic-update-slice_fusion.2, bf16[128,4096]{1,0:T(8,128)(2,1)} %collective-permute-done.3, s32[]{:T(128)S(6)} %select_n.126), kind=kLoop, calls=%fused_computation.25 | loop fusion | bytes 2097156 | tf_op jit(solution)/shard_map/dynamic_update_slice | solution.py:47
  120.8 9.2 %convolution_convert_fusion.1.proj = bf16[1024,768]{1,0:T(8,128)(2,1)S(1)} fusion(bf16[1024,4096]{1,0:T(8,128)(2,1)} %constant_dynamic-update-slice_fusion, bf16[4096,768]{0,1:T(8,128)(2,1)S(1)} %bitcast.45), kind=kOutput, calls=%fused_computation.9 | convolution fusion | flops 6443237376 | bytes 16252928 | tf_op jit(solution)/shard_map/dot_general | solution.py:188
  131.3 13.9 %collective-permute-start.8 = (bf16[176,256]{1,0:T(8,128)(2,1)S(1)}, bf16[176,256]{1,0:T(8,128)(2,1)S(1)}, u32[]{:S(2)}, u32[]{:S(2)}) collective-permute-start(bf16[176,256]{1,0:T(8,128)(2,1)S(1)} %pad_maximum_fusion.2), channel_id=1, source_target_pairs={{0,8},{8,16},{16,24},{24,32},{32,40},{40,48},{48,56},{56,64},{64,7... | collective-permute-start | bytes 270344 | tf_op jit(solution)/shard_map/ppermute | solution.py:189
  145.3 11.0 %convolution_convert_fusion.proj = bf16[1024,768]{1,0:T(8,128)(2,1)S(1)} fusion(bf16[1024,4096]{1,0:T(8,128)(2,1)} %constant_dynamic-update-slice_fusion, bf16[4096,768]{0,1:T(8,128)(2,1)} %all-gather.2.cloned.1.call-done), kind=kOutput, calls=%fused_computation.8 | convolution fusion | flops 6443237376 | bytes 16252928 | tf_op jit(solution)/shard_map/dot_general | solution.py:188
  156.5 3.2 %collective-permute-start.7 = (bf16[176,256]{1,0:T(8,128)(2,1)S(1)}, bf16[176,256]{1,0:T(8,128)(2,1)S(1)}, u32[]{:S(2)}, u32[]{:S(2)}) collective-permute-start(bf16[176,256]{1,0:T(8,128)(2,1)S(1)} %pad_maximum_fusion.1), channel_id=1, source_target_pairs={{0,8},{8,16},{16,24},{24,32},{32,40},{40,48},{48,56},{56,64},{64,7... | collective-permute-start | bytes 270344 | tf_op jit(solution)/shard_map/ppermute | solution.py:189
  159.7 6.1 %shard_map.65 = bf16[1024,256]{1,0:T(8,128)(2,1)} custom-call(s32[8]{0:T(128)S(1)} %compare_convert_fusion.flags, bf16[1024,768]{1,0:T(8,128)(2,1)S(1)} %convolution_convert_fusion.proj, bf16[176,256]{1,0:T(8,128)(2,1)S(1)} %collective-permute-done.8.halo, f32[9,256]{1,0:T(8,128)S(1)} %slice_convert_fusion.short, bf16[16,256,128]{2,1,0:T(8,128)(2,1)S(1)} %slice.199.band, ...), custom_call_target="tpu_custom_call" | custom-call | flops 10000000000 | bytes 4000000 | tf_op jit(solution)/shard_map/pallas_call | solution.py:124
  165.9 14.9 %all-to-all-start.1 = ((bf16[8,128,256]{2,1,0:T(8,128)(2,1)}), bf16[8,128,256]{2,1,0:T(8,128)(2,1)S(1)}, u32[]{:S(2)}, u32[]{:S(2)}) async-start(bf16[8,128,256]{2,1,0:T(8,128)(2,1)} %bitcast.18), calls=%async_computation.1 | async-start | bytes 1048576 | tf_op jit(solution)/shard_map/all_to_all | solution.py:193
  182.2 6.1 %shard_map.64 = bf16[1024,256]{1,0:T(8,128)(2,1)} custom-call(s32[8]{0:T(128)S(1)} %compare_convert_fusion.flags, bf16[1024,768]{1,0:T(8,128)(2,1)S(1)} %copy-done.1, bf16[176,256]{1,0:T(8,128)(2,1)S(1)} %collective-permute-done.7.halo, f32[9,256]{1,0:T(8,128)S(1)} %convert_element_type.87.short, bf16[16,256,128]{2,1,0:T(8,128)(2,1)S(1)} %slice.181.band, ...), custom_call_target="tpu_custom_call" | custom-call | flops 10000000000 | bytes 4000000 | tf_op jit(solution)/shard_map/pallas_call | solution.py:124
  190.2 4.3 %all-to-all-start = ((bf16[8,128,256]{2,1,0:T(8,128)(2,1)}), bf16[8,128,256]{2,1,0:T(8,128)(2,1)S(1)}, u32[]{:S(2)}, u32[]{:S(2)}) async-start(bf16[8,128,256]{2,1,0:T(8,128)(2,1)} %bitcast.11), calls=%async_computation | async-start | bytes 1048576 | tf_op jit(solution)/shard_map/all_to_all | solution.py:193
  194.5 9.5 %all-to-all-done = bf16[8,128,256]{2,1,0:T(8,128)(2,1)S(1)} async-done(((bf16[8,128,256]{2,1,0:T(8,128)(2,1)}), bf16[8,128,256]{2,1,0:T(8,128)(2,1)S(1)}, u32[]{:S(2)}, u32[]{:S(2)}) %all-to-all-start) | async-done | bytes 524320 | tf_op jit(solution)/shard_map/all_to_all | solution.py:193
  (81 shorter events, 28.0 us)
Async XLA Ops:
  6.5 138.8 %all-gather.2.cloned.1.call-start = ((), (), s32[]{:S(2)}) async-start(), calls=%async_computation.2 | async-start | bytes 6684672 | tf_op jit(solution)/shard_map/all_gather | solution.py:172
  6.5 17.6 %copy-start.7 = (bf16[4096]{0:T(1024)(128)(2,1)S(1)}, bf16[4096]{0:T(1024)(128)(2,1)}, u32[]{:S(2)}) copy-start(bf16[4096]{0:T(1024)(128)(2,1)} %param.7) | copy-start | bytes 24580
  6.5 17.6 %copy-start.2 = (bf16[128,4096]{1,0:T(8,128)(2,1)S(1)}, bf16[128,4096]{1,0:T(8,128)(2,1)}, u32[]{:S(2)}) copy-start(bf16[128,4096]{1,0:T(8,128)(2,1)} %param.6) | copy-start | bytes 3145732
  16.3 17.1 %collective-permute-start.6 = (bf16[256,768]{0,1:T(8,128)(2,1)S(1)}, bf16[256,768]{0,1:T(8,128)(2,1)S(1)}, u32[]{:S(2)}, u32[]{:S(2)}) collective-permute-start(bf16[256,768]{0,1:T(8,128)(2,1)S(1)} %bitcast.48), channel_id=1, source_target_pairs={{0,8},{8,0},{1,9},{9,1},{2,10},{10,2},{3,11},{11,3},{4,12},{12,4},... | collective-permute-start | bytes 1179656 | tf_op jit(solution)/shard_map/ppermute | solution.py:17
  24.1 10.1 %copy-start.5 = (f32[4096]{0:T(1024)}, f32[4096]{0:T(1024)S(1)}, u32[]{:S(2)}) copy-start(f32[4096]{0:T(1024)S(1)} %convert_element_type.75) | copy-start | bytes 49156
  33.4 0.8 copy-start.4
  34.5 4.3 %collective-permute-start = (bf16[128,4096]{1,0:T(8,128)(2,1)S(1)}, bf16[128,4096]{1,0:T(8,128)(2,1)S(1)}, u32[]{:S(2)}, u32[]{:S(2)}) collective-permute-start(bf16[128,4096]{1,0:T(8,128)(2,1)S(1)} %fusion.2), channel_id=1, source_target_pairs={{0,1},{1,0},{2,3},{3,2},{4,5},{5,4},{6,7},{7,6},{8,9},{9,8},{10,11... | collective-permute-start | bytes 3145736 | tf_op jit(solution)/shard_map/ppermute | solution.py:17
  44.5 4.6 %copy-start.9 = (bf16[3,3,256]{2,1,0:T(4,128)(2,1)S(1)}, bf16[3,3,256]{2,1,0:T(4,128)(2,1)}, u32[]{:S(2)}) copy-start(bf16[3,3,256]{2,1,0:T(4,128)(2,1)} %param.9) | copy-start | bytes 13828
  44.5 4.7 %copy-start.6 = (bf16[16,128]{1,0:T(8,128)(2,1)S(1)}, bf16[16,128]{1,0:T(8,128)(2,1)}, u32[]{:S(2)}) copy-start(bf16[16,128]{1,0:T(8,128)(2,1)} %param.10) | copy-start | bytes 12292
  44.5 16.8 %copy-start.8 = (s32[2048]{0:T(1024)S(1)}, s32[2048]{0:T(1024)}, u32[]{:S(2)}) copy-start(s32[2048]{0:T(1024)} %param.11) | copy-start | bytes 24580
  46.4 25.7 %collective-permute-start.1 = (bf16[256,4096]{1,0:T(8,128)(2,1)S(1)}, bf16[256,4096]{1,0:T(8,128)(2,1)}, u32[]{:S(2)}, u32[]{:S(2)}) collective-permute-start(bf16[256,4096]{1,0:T(8,128)(2,1)S(1)} %get-tuple-element.5), channel_id=1, source_target_pairs={{0,2},{1,7},{2,4},{3,1},{4,6},{5,3},{6,0},{7,5},{8,10},{9,15},{10,... | collective-permute-start | bytes 6291464 | tf_op jit(solution)/shard_map/ppermute | solution.py:40
  49.2 45.2 %collective-permute-start.5 = (bf16[17,256]{1,0:T(8,128)(2,1)S(1)}, bf16[17,256]{1,0:T(8,128)(2,1)S(1)}, u32[]{:S(2)}, u32[]{:S(2)}) collective-permute-start(bf16[17,256]{1,0:T(8,128)(2,1)S(1)} %pad_maximum_fusion.3), channel_id=1, source_target_pairs={{0,8},{8,0},{1,9},{9,1},{2,10},{10,2},{3,11},{11,3},{4,12},{12,4},... | collective-permute-start | bytes 26120 | tf_op jit(solution)/shard_map/ppermute | solution.py:17
  72.1 41.9 %collective-permute-start.2 = (bf16[256,4096]{1,0:T(8,128)(2,1)}, bf16[256,4096]{1,0:T(8,128)(2,1)}, u32[]{:S(2)}, u32[]{:S(2)}) collective-permute-start(bf16[256,4096]{1,0:T(8,128)(2,1)} %collective-permute-done.1), channel_id=1, source_target_pairs={{0,1},{1,0},{2,3},{3,2},{4,5},{5,4},{6,7},{7,6},{8,9},{9,8},{10,11... | collective-permute-start | bytes 6291464 | tf_op jit(solution)/shard_map/ppermute | solution.py:17
  76.4 34.0 %collective-permute-start.3 = (bf16[128,4096]{1,0:T(8,128)(2,1)}, bf16[128,4096]{1,0:T(8,128)(2,1)}, u32[]{:S(2)}, u32[]{:S(2)}) collective-permute-start(bf16[128,4096]{1,0:T(8,128)(2,1)} %constant_dynamic-slice_fusion.1), channel_id=1, source_target_pairs={{0,2},{1,7},{2,4},{3,1},{4,6},{5,3},{6,0},{7,5},{8,10},{9,15},{10,... | collective-permute-start | bytes 3145736 | tf_op jit(solution)/shard_map/ppermute | solution.py:42
  110.4 9.3 %collective-permute-start.4 = (bf16[128,4096]{1,0:T(8,128)(2,1)}, bf16[128,4096]{1,0:T(8,128)(2,1)S(1)}, u32[]{:S(2)}, u32[]{:S(2)}) collective-permute-start(bf16[128,4096]{1,0:T(8,128)(2,1)} %collective-permute-done.3), channel_id=1, source_target_pairs={{0,1},{1,0},{2,3},{3,2},{4,5},{5,4},{6,7},{7,6},{8,9},{9,8},{10,11... | collective-permute-start | bytes 3145736 | tf_op jit(solution)/shard_map/ppermute | solution.py:17
  110.7 10.1 %slice-start = ((s8[6291456]{0:T(1024)(128)(4,1)}), s8[4194304]{0:T(1024)(128)(4,1)S(1)}, s32[]{:S(2)}) async-start(s8[6291456]{0:T(1024)(128)(4,1)} %bitcast.43), calls=%async_computation.3 | async-start | bytes 8388608
  114.0 6.8 %slice-start.1 = ((s8[6291456]{0:T(1024)(128)(4,1)}), s8[2097152]{0:T(1024)(128)(4,1)S(1)}, s32[]{:S(2)}) async-start(s8[6291456]{0:T(1024)(128)(4,1)} %bitcast.43), calls=%async_computation.4 | async-start | bytes 4194304
  130.2 1.2 copy-start
  131.3 28.4 %collective-permute-start.8 = (bf16[176,256]{1,0:T(8,128)(2,1)S(1)}, bf16[176,256]{1,0:T(8,128)(2,1)S(1)}, u32[]{:S(2)}, u32[]{:S(2)}) collective-permute-start(bf16[176,256]{1,0:T(8,128)(2,1)S(1)} %pad_maximum_fusion.2), channel_id=1, source_target_pairs={{0,8},{8,16},{16,24},{24,32},{32,40},{40,48},{48,56},{56,64},{64,7... | collective-permute-start | bytes 270344 | tf_op jit(solution)/shard_map/ppermute | solution.py:189
  156.5 24.3 %collective-permute-start.7 = (bf16[176,256]{1,0:T(8,128)(2,1)S(1)}, bf16[176,256]{1,0:T(8,128)(2,1)S(1)}, u32[]{:S(2)}, u32[]{:S(2)}) collective-permute-start(bf16[176,256]{1,0:T(8,128)(2,1)S(1)} %pad_maximum_fusion.1), channel_id=1, source_target_pairs={{0,8},{8,16},{16,24},{24,32},{32,40},{40,48},{48,56},{56,64},{64,7... | collective-permute-start | bytes 270344 | tf_op jit(solution)/shard_map/ppermute | solution.py:189
  165.9 24.4 %all-to-all-start.1 = ((bf16[8,128,256]{2,1,0:T(8,128)(2,1)}), bf16[8,128,256]{2,1,0:T(8,128)(2,1)S(1)}, u32[]{:S(2)}, u32[]{:S(2)}) async-start(bf16[8,128,256]{2,1,0:T(8,128)(2,1)} %bitcast.18), calls=%async_computation.1 | async-start | bytes 1048576 | tf_op jit(solution)/shard_map/all_to_all | solution.py:193
  180.8 1.4 copy-start.1
  188.3 15.9 %copy-start.3 = (bf16[128,4096]{1,0:T(8,128)(2,1)S(1)}, bf16[128,4096]{1,0:T(8,128)(2,1)}, u32[]{:S(2)}) copy-start(bf16[128,4096]{1,0:T(8,128)(2,1)} %param.6) | copy-start | bytes 3145732
  190.2 13.8 %all-to-all-start = ((bf16[8,128,256]{2,1,0:T(8,128)(2,1)}), bf16[8,128,256]{2,1,0:T(8,128)(2,1)S(1)}, u32[]{:S(2)}, u32[]{:S(2)}) async-start(bf16[8,128,256]{2,1,0:T(8,128)(2,1)} %bitcast.11), calls=%async_computation | async-start | bytes 1048576 | tf_op jit(solution)/shard_map/all_to_all | solution.py:193
Sparse Core Ops, SparseCore 0:
  34.3 107.3 all-gather.1

commit v2 on v1

--- a/solution.py
+++ b/solution.py
@@ -17,40 +17,135 @@
     return lax.ppermute(value, axis, [(0, 1), (1, 0)])
 
 
+def shift(value, axis, by):
+    size = lax.axis_size(axis)
+    return lax.ppermute(value, axis, [(i, (i + by) % size) for i in range(size)])
+
+
+def fan(axis):
+    size = lax.axis_size(axis)
+    return [(2 * i + c, 2 * ((i + 1 - 2 * c) % size) + c) for i in range(size) for c in range(2)]
+
+
+def band_kernel(taps, band):
+    groups, span = taps.shape
+    for g in range(groups):
+        row = jnp.concatenate([taps[g : g + 1, :], jnp.zeros((1, span), jnp.float32)], axis=1)
+        rows = jnp.broadcast_to(row, (2 * span, 2 * span))
+        moved = pltpu.roll(rows, 0, axis=1, stride=1, stride_axis=0)
+        band[g] = moved[:, span:].astype(band.dtype)
+
+
 def banded(long_filter):
     groups, span = long_filter.shape
-    period = 3 * span
-    row = jnp.concatenate([long_filter, jnp.zeros((groups, period - span), long_filter.dtype)], axis=1)
-    tiled = jnp.tile(row, (1, 2 * span))[:, : 2 * span * (period - 1)]
-    skewed = tiled.reshape(groups, 2 * span, period - 1)
-    return skewed[:, :, span : 2 * span]
+    vmem = pl.BlockSpec(memory_space=pltpu.VMEM)
+    return pl.pallas_call(
+        band_kernel,
+        out_shape=jax.ShapeDtypeStruct((groups, 2 * span, span), jnp.bfloat16),
+        in_specs=[vmem],
+        out_specs=vmem,
+        compiler_params=pltpu.CompilerParams(vmem_limit_bytes=16 << 20),
+        cost_estimate=pl.CostEstimate(flops=2_000_000_000, bytes_accessed=1_000_000, transcendentals=0),
+    )(long_filter.astype(jnp.float32))
+
+
+def place(pieces, at, rows):
+    width = pieces[0].shape[1]
+    counts = [piece.shape[0] // rows for piece in pieces]
+    firsts = [sum(counts[:n]) for n in range(len(pieces))]
+
+    def kernel(at, *refs):
+        del at
+        step = pl.program_id(0)
+        for n, (first, count) in enumerate(zip(firsts, counts)):
+
+            @pl.when(jnp.logical_and(step >= first, step < first + count))
+            def _(n=n):
+                refs[-1][...] = refs[n][...]
+
+    def pick(first, count):
+        return pl.BlockSpec((rows, width), lambda step, at: (jnp.clip(step - first, 0, count - 1), 0))
+
+    spec = pltpu.PrefetchScalarGridSpec(
+        num_scalar_prefetch=1,
+        grid=(sum(counts),),
+        in_specs=[pick(first, count) for first, count in zip(firsts, counts)],
+        out_specs=pl.BlockSpec((rows, width), lambda step, at: (at[step], 0)),
+    )
+    return pl.pallas_call(
+        kernel,
+        out_shape=jax.ShapeDtypeStruct((sum(counts) * rows, width), pieces[0].dtype),
+        grid_spec=spec,
+        compiler_params=pltpu.CompilerParams(vmem_limit_bytes=24 << 20),
+        cost_estimate=pl.CostEstimate(flops=0, bytes_accessed=16_000_000, transcendentals=0),
+    )(jnp.stack(at).astype(jnp.int32), *pieces)
 
 
 def gather_tokens(normed):
-    rows, width = normed.shape
+    rows = normed.shape[0]
     y, core = lax.axis_index("y"), lax.axis_index("core")
     size = lax.axis_size("y")
     sib = swap(normed, "core")
-    first = jnp.where(core == 0, normed, sib)
-    second = jnp.where(core == 0, sib, normed)
-    pair = jnp.concatenate([first, second], axis=0)
-    ring = [
-        (2 * i + c, 2 * ((i + (1 if c == 0 else -1)) % size) + c) for i in range(size) for c in range(2)
-    ]
-    near = lax.ppermute(pair, ("y", "core"), ring)
+    pair = jnp.concatenate([jnp.where(core == 0, normed, sib), jnp.where(core == 0, sib, normed)], axis=0)
+    near = lax.ppermute(pair, ("y", "core"), fan("y"))
     near_half = lax.dynamic_slice_in_dim(near, core * rows, rows, 0)
-    far = lax.ppermute(near_half, ("y", "core"), ring)
+    far = lax.ppermute(near_half, ("y", "core"), fan("y"))
     near_sib = swap(near, "core")
     far_sib = swap(far, "core")
     sign = 1 - 2 * core
-    full = jnp.zeros((2 * size * rows, width), normed.dtype)
-    put = lambda full, value, at: lax.dynamic_update_slice_in_dim(full, value, at * rows, 0)
-    full = put(full, pair, 2 * y)
-    full = put(full, near, 2 * ((y - sign + size) % size))
-    full = put(full, near_sib, 2 * ((y + sign + size) % size))
-    full = put(full, far, 2 * ((y + 2) % size) + core)
-    full = put(full, far_sib, 2 * ((y + 2) % size) + 1 - core)
-    return full
+    at = [2 * a + c for a in (y, (y - sign + size) % size, (y + sign + size) % size) for c in range(2)]
+    at += [2 * ((y + 2) % size) + core, 2 * ((y + 2) % size) + 1 - core]
+    return place([pair, near, near_sib, far, far_sib], at, rows)
+
+
+def spread_columns(piece):
+    up, down = shift(piece, "z_lo", 1), shift(piece, "z_lo", -1)
+    late, up, down = lax.optimization_barrier((piece, up, down))
+    return (0, piece), (1, up), (-1, down), (2, shift(late, "z_lo", 2))
+
+
+def spread_rows(by, mine):
+    z_lo, x, core = lax.axis_index("z_lo"), lax.axis_index("x"), lax.axis_index("core")
+    depth, size = lax.axis_size("z_lo"), lax.axis_size("x")
+    below, above = shift(mine, "x", 1), shift(mine, "x", -1)
+    far = lax.ppermute(jnp.where(core == 0, below, above), ("x", "core"), fan("x"))
+    first = (z_lo - by + depth) % depth * size
+    places = [first + x, first + (x + size - 1) % size, first + (x + 1) % size, first + (x + 2) % size]
+    return [mine, below, above, far], places
+
+
+def add_product_kernel(count, places, *refs):
+    del places
+    lefts, rights, rest = refs[:count], refs[count : 2 * count], refs[2 * count :]
+    total = rest[0][...] if len(rest) == 2 else None
+    for left, right in zip(lefts, rights):
+        term = jnp.dot(left[...], right[...], preferred_element_type=jnp.float32)
+        total = term if total is None else total + term
+    rest[-1][...] = total.astype(rest[-1].dtype)
+
+
+def add_product(left, pieces, places, total, dtype):
+    length = left.shape[0]
+    deep, wide = pieces[0].shape
+    rows = 256
+    count = len(pieces)
+    spec = pltpu.PrefetchScalarGridSpec(
+        num_scalar_prefetch=1,
+        grid=(length // rows,),
+        in_specs=[pl.BlockSpec((rows, deep), lambda r, at, n=n: (r, at[n])) for n in range(count)]
+        + [pl.BlockSpec((deep, wide), lambda r, at: (0, 0)) for _ in range(count)]
+        + ([] if total is None else [pl.BlockSpec((rows, wide), lambda r, at: (r, 0))]),
+        out_specs=pl.BlockSpec((rows, wide), lambda r, at: (r, 0)),
+    )
+    return pl.pallas_call(
+        functools.partial(add_product_kernel, count),
+        out_shape=jax.ShapeDtypeStruct((length, wide), dtype),
+        grid_spec=spec,
+        compiler_params=pltpu.CompilerParams(vmem_limit_bytes=24 << 20),
+        cost_estimate=pl.CostEstimate(
+            flops=2 * length * deep * wide * count, bytes_accessed=8_000_000, transcendentals=0
+        ),
+    )(jnp.stack(places).astype(jnp.int32), *[left] * count, *pieces, *([] if total is None else [total]))
 
 
 def mix_conv_kernel(
@@ -168,13 +263,15 @@
 
     deep = width // contexts
     piece = lax.dynamic_slice_in_dim(in_weight, context * deep, deep, 0).reshape(deep, 3 * channels)
+    piece, tokens = lax.optimization_barrier((piece, tokens))
     piece = swap(piece, "z_hi")
-    other_weight = lax.all_gather(piece, ("z_lo", "x"), axis=0, tiled=True)
 
     float_tokens = tokens.astype(jnp.float32)
     scale_rows = lax.rsqrt(jnp.mean(float_tokens * float_tokens, axis=-1, keepdims=True) + 1e-06)
     normed = (float_tokens * scale_rows * norm_gain.astype(jnp.float32)[None]).astype(jnp.bfloat16)
+    in_weight, normed = lax.optimization_barrier((in_weight, normed))
     gathered = gather_tokens(normed)
+    columns = spread_columns(piece)
 
     small = jnp.concatenate(
         [short_filter.reshape(3 * taps, channels), long_filter.reshape(-1, channels)], axis=0
@@ -184,9 +281,8 @@
 
     next_half = [(i, i + 1) for i in range(contexts * lax.axis_size("z_hi") - 1)]
 
-    def project(weight, short):
-        projected = jnp.dot(gathered, weight, preferred_element_type=jnp.float32).astype(jnp.bfloat16)
-        return projected, lax.ppermute(tail_of(projected, short, starts), ("z_lo", "x", "z_hi"), next_half)
+    def halo_of(projected, short):
+        return lax.ppermute(tail_of(projected, short, starts), ("z_lo", "x", "z_hi"), next_half)
 
     def finish(projected, halo, short, long):
         gated = mix_conv(projected, halo, short, banded(long), starts)
@@ -194,8 +290,20 @@
 
     own_short = short_filter.reshape(3 * taps, channels).astype(jnp.float32)
     other_short = other_short.astype(jnp.float32)
-    own_projected, other_halo = project(in_weight.reshape(width, 3 * channels), own_short)
-    other_projected, own_halo = project(other_weight, other_short)
+    own_projected = jnp.dot(
+        gathered, in_weight.reshape(width, 3 * channels), preferred_element_type=jnp.float32
+    ).astype(jnp.bfloat16)
+    other_halo = halo_of(own_projected, own_short)
+    other_projected = None
+    for n, (by, mine) in enumerate(columns):
+        last = n == len(columns) - 1
+        if last:
+            mine, own_projected = lax.optimization_barrier((mine, own_projected))
+        pieces, places = spread_rows(by, mine)
+        other_projected = add_product(
+            gathered, pieces, places, other_projected, jnp.bfloat16 if last else jnp.float32
+        )
+    own_halo = halo_of(other_projected, other_short)
     own = finish(own_projected, own_halo, own_short, long_filter)
     other = finish(other_projected, other_halo, other_short, other_long)
     left = jnp.where(z_hi == 0, own, other)

time: 214 us -> 188 us (0.88)
  local copies, waits for them, and re-layouts: 62.1 us -> 14.7 us
  waiting for transfers between devices: 33.6 us -> 59.2 us
  Pallas kernels: 12.3 us -> 36.4 us
  matrix products: 20.2 us -> 6.7 us
  between operations: 13.8 us -> 0.56 us
    ppermute x4 -> x19, waiting for transfers between devices: 10.8 us -> 44.5 us  [the longest x11 28.8 us: shift(): lax.ppermute(value, axis, [(i, (i + by) % size) for i in range(size)])]
    pallas_call x0 -> x7, Pallas kernels: none -> 22.9 us  [the longest x4 16.2 us: add_product(): pl.pallas_call(functools.partial(add_product_kernel, count), out_shape=ja...]
    reshape x3 -> x0, local copies, waits for them, and re-layouts: 21.2 us -> none  [the longest x2 21.2 us: banded(): skewed = tiled.reshape(groups, 2 * span, period - 1)]
    ppermute x4 -> x19, starting transfers between devices: 21.5 us -> 39 us  [the longest x11 16.9 us: shift(): lax.ppermute(value, axis, [(i, (i + by) % size) for i in range(size)])]
    unnamed x27 -> x23, local copies, waits for them, and re-layouts: 15.8 us -> 0.27 us
    dot_general x2 -> x1, matrix products: 20.2 us -> 6.7 us  [per_device(): jnp.dot(gathered, in_weight.reshape(width, 3 * channels), preferred_eleme...]
    ppermute x5, starting transfers between devices: 24.2 us -> 12.7 us  [swap(): return lax.ppermute(value, axis, [(0, 1), (1, 0)])]
    dynamic_update_slice x4 -> x0, local copies, waits for them, and re-layouts: 10.1 us -> none  [gather_tokens(): lax.dynamic_update_slice_in_dim(full, value, at * rows, 0)]
  transfers between devices with their start and end apart: 12 -> 26, of which waited for: 5 -> 11; matrix products, arithmetic and copies ran while one was open for 35% -> 11% of each run, Pallas kernels for 6% -> 20%
where the time goes in v2:
time: 188 us; the launch traced here: 186 us
  starting transfers between devices  64 us (34%)
  waiting for transfers between devices  59.2 us (31%)
  Pallas kernels  36.4 us (19%)
  local copies, waits for them, and re-layouts  14.7 us (8%)
  matrix products  6.7 us (4%)
  other arithmetic  4.15 us (2%)
    ppermute x11, waiting for transfers between devices, shift(): lax.ppermute(value, axis, [(i, (i + by) % size) for i in range(size)])  28.8 us
    ppermute x11, starting transfers between devices, shift(): lax.ppermute(value, axis, [(i, (i + by) % size) for i in range(size)])  16.9 us
    pallas_call x4, Pallas kernels, add_product(): pl.pallas_call(functools.partial(add_product_kernel, count), out_shape=ja...  16.2 us
    ppermute x1, waiting for transfers between devices, gather_tokens(): near = lax.ppermute(pair, ('y', 'core'), fan('y'))  15.7 us
    ppermute x2, starting transfers between devices, halo_of(): lax.ppermute(tail_of(projected, short, starts), ('z_lo', 'x', 'z_hi'), ne...  14.8 us
    pallas_call x2, Pallas kernels, mix_conv(): pl.pallas_call(mix_conv_kernel, out_shape=jax.ShapeDtypeStruct((length, c...  13.4 us
    ppermute x5, starting transfers between devices, swap(): return lax.ppermute(value, axis, [(0, 1), (1, 0)])  12.7 us
    all_to_all x2, waiting for transfers between devices, finish(): lax.all_to_all(gated, ('y', 'core'), split_axis=0, concat_axis=1, tiled=T...  12.4 us
  transfers between devices with their start and end apart: 26, of which 11 were waited for; matrix products, arithmetic and copies ran while one was open for 11% of the time, Pallas kernels for 20%

profile of v2, /device:TPU:1, one launch (start us, length us, event | category | flops | bytes accessed | tf_op | source)
XLA Modules:
  0.0 185.8 jit_solution(18110664156518036912)
XLA Ops:
  2.0 3.3 %collective-permute-start.4 = (bf16[128,4096]{1,0:T(8,128)(2,1)S(1)}, bf16[128,4096]{1,0:T(8,128)(2,1)S(1)}, u32[]{:S(2)}, u32[]{:S(2)}) collective-permute-start(bf16[128,4096]{1,0:T(8,128)(2,1)S(1)} %fusion.2), channel_id=1, source_target_pairs={{0,1},{1,0},{2,3},{3,2},{4,5},{5,4},{6,7},{7,6},{8,9},{9,8},{10,11... | collective-permute-start | bytes 3145736 | tf_op jit(solution)/shard_map/ppermute | solution.py:17
  10.0 6.9 %collective-permute-start = (bf16[256,768]{1,0:T(8,128)(2,1)}, bf16[256,768]{1,0:T(8,128)(2,1)}, u32[]{:S(2)}, u32[]{:S(2)}) collective-permute-start(bf16[256,768]{1,0:T(8,128)(2,1)} %copy.18), channel_id=1, source_target_pairs={{0,8},{8,0},{1,9},{9,1},{2,10},{10,2},{3,11},{11,3},{4,12},{12,4},... | collective-permute-start | bytes 1179656 | tf_op jit(solution)/shard_map/ppermute | solution.py:17
  17.6 15.7 %collective-permute-done.5.refs_1_ = bf16[256,4096]{1,0:T(8,128)(2,1)} collective-permute-done((bf16[256,4096]{1,0:T(8,128)(2,1)S(1)}, bf16[256,4096]{1,0:T(8,128)(2,1)}, u32[]{:S(2)}, u32[]{:S(2)}) %collective-permute-start.5) | collective-permute-done | bytes 2097184 | tf_op jit(solution)/shard_map/ppermute | solution.py:90
  38.4 8.7 %copy.19 = bf16[4096,3,256]{0,2,1:T(8,128)(2,1)} copy(bf16[4096,3,256]{2,0,1:T(8,128)(2,1)} %param.8) | data formatting | bytes 12582912 | tf_op jit(solution)/shard_map/optimization_barrier | solution.py:272
  49.5 2.7 %collective-permute-start.2 = (bf16[256,768]{1,0:T(8,128)(2,1)}, bf16[256,768]{1,0:T(8,128)(2,1)}, u32[]{:S(2)}, u32[]{:S(2)}) collective-permute-start(bf16[256,768]{1,0:T(8,128)(2,1)} %collective-permute-done.refs_4_), channel_id=1, source_target_pairs={{0,192},{64,0},{128,64},{192,128},{1,193},{65,1},{129,65},{193,129... | collective-permute-start | bytes 1179656 | tf_op jit(solution)/shard_map/ppermute | solution.py:22
  53.4 8.1 %collective-permute-done.1.refs_4_ = bf16[256,768]{1,0:T(8,128)(2,1)} collective-permute-done((bf16[256,768]{1,0:T(8,128)(2,1)}, bf16[256,768]{1,0:T(8,128)(2,1)}, u32[]{:S(2)}, u32[]{:S(2)}) %collective-permute-start.1) | collective-permute-done | bytes 393248 | tf_op jit(solution)/shard_map/ppermute | solution.py:22
  64.0 4.4 %collective-permute-done.2.refs_4_ = bf16[256,768]{1,0:T(8,128)(2,1)} collective-permute-done((bf16[256,768]{1,0:T(8,128)(2,1)}, bf16[256,768]{1,0:T(8,128)(2,1)}, u32[]{:S(2)}, u32[]{:S(2)}) %collective-permute-start.2) | collective-permute-done | bytes 393248 | tf_op jit(solution)/shard_map/ppermute | solution.py:22
  73.5 5.5 %collective-permute-done.16.refs_5_ = bf16[256,768]{1,0:T(8,128)(2,1)S(1)} collective-permute-done((bf16[256,768]{1,0:T(8,128)(2,1)}, bf16[256,768]{1,0:T(8,128)(2,1)S(1)}, u32[]{:S(2)}, u32[]{:S(2)}) %collective-permute-start.16) | collective-permute-done | bytes 393248 | tf_op jit(solution)/shard_map/ppermute | solution.py:22
  82.4 2.7 %collective-permute-start.21 = (bf16[256,768]{1,0:T(8,128)(2,1)S(1)}, bf16[256,768]{1,0:T(8,128)(2,1)S(1)}, u32[]{:S(2)}, u32[]{:S(2)}) collective-permute-start(bf16[256,768]{1,0:T(8,128)(2,1)S(1)} %broadcast_select_fusion.2), channel_id=1, source_target_pairs={{0,16},{1,49},{16,32},{17,1},{32,48},{33,17},{48,0},{49,33},{2,18}... | collective-permute-start | bytes 1179656 | tf_op jit(solution)/shard_map/ppermute | solution.py:111
  91.1 6.3 %shard_map.64.refs_0_.refs_1_.refs_2_.refs_3_ = bf16[1024,4096]{1,0:T(8,128)(2,1)S(1)} custom-call(s32[8]{0:T(128)S(1)} %stack.95.at, bf16[256,4096]{1,0:T(8,128)(2,1)S(1)} %pad_maximum_fusion.refs_0_, bf16[256,4096]{1,0:T(8,128)(2,1)} %collective-permute-done.5.refs_1_, bf16[256,4096]{1,0:T(8,128)(2,1)} %collective-permute-done.6.refs_2_, ...), custom_call_target="tpu_custom_call" | custom-call | bytes 16000000 | tf_op jit(solution)/shard_map/pallas_call | solution.py:75
  97.4 6.7 %convolution_convert_fusion.proj = bf16[1024,768]{1,0:T(8,128)(2,1)S(1)} fusion(bf16[1024,4096]{1,0:T(8,128)(2,1)S(1)} %shard_map.64.refs_0_.refs_1_.refs_2_.refs_3_, bf16[4096,768]{0,1:T(8,128)(2,1)S(1)} %bitcast.59), kind=kOutput, calls=%fused_computation.8 | convolution fusion | flops 6443237376 | bytes 16252928 | tf_op jit(solution)/shard_map/dot_general | solution.py:293
  108.4 5.0 %collective-permute-done.10.refs_5_ = bf16[256,768]{1,0:T(8,128)(2,1)S(1)} collective-permute-done((bf16[256,768]{1,0:T(8,128)(2,1)S(1)}, bf16[256,768]{1,0:T(8,128)(2,1)S(1)}, u32[]{:S(2)}, u32[]{:S(2)}) %collective-permute-start.10) | collective-permute-done | bytes 393248 | tf_op jit(solution)/shard_map/ppermute | solution.py:22
  113.4 8.4 %collective-permute-start.23 = (bf16[176,256]{1,0:T(8,128)(2,1)S(1)}, bf16[176,256]{1,0:T(8,128)(2,1)S(1)}, u32[]{:S(2)}, u32[]{:S(2)}) collective-permute-start(bf16[176,256]{1,0:T(8,128)(2,1)S(1)} %pad_maximum_fusion.2), channel_id=1, source_target_pairs={{0,8},{8,16},{16,24},{24,32},{32,40},{40,48},{48,56},{56,64},{64,7... | collective-permute-start | bytes 270344 | tf_op jit(solution)/shard_map/ppermute | solution.py:285
  122.3 4.3 %shard_map.65.refs_8_ = f32[1024,768]{1,0:T(8,128)S(1)} custom-call(s32[4]{0:T(128)S(1)} %pad_add_fusion.3.places, bf16[1024,4096]{1,0:T(8,128)(2,1)S(1)} %shard_map.64.refs_0_.refs_1_.refs_2_.refs_3_, bf16[1024,4096]{1,0:T(8,128)(2,1)S(1)} %shard_map.64.refs_0_.refs_1_.refs_2_.refs_3_, bf16[1024,4096]{1,0:T(8,128)(2,1)S(1)} %shard_map.64.refs_0_.refs_1_.refs_2_.refs_3_, ...), custom_call_target="tpu_custom_call" | custom-call | flops 1610612736 | bytes 8000000 | tf_op jit(solution)/shard_map/pallas_call | solution.py:140
  126.5 4.3 %shard_map.66.refs_8_ = f32[1024,768]{1,0:T(8,128)S(1)} custom-call(s32[4]{0:T(128)S(1)} %pad_add_fusion.2.places, bf16[1024,4096]{1,0:T(8,128)(2,1)S(1)} %shard_map.64.refs_0_.refs_1_.refs_2_.refs_3_, bf16[1024,4096]{1,0:T(8,128)(2,1)S(1)} %shard_map.64.refs_0_.refs_1_.refs_2_.refs_3_, bf16[1024,4096]{1,0:T(8,128)(2,1)S(1)} %shard_map.64.refs_0_.refs_1_.refs_2_.refs_3_, ...), custom_call_target="tpu_custom_call" | custom-call | flops 1610612736 | bytes 8000000 | tf_op jit(solution)/shard_map/pallas_call | solution.py:140
  130.9 4.3 %shard_map.67.refs_8_ = f32[1024,768]{1,0:T(8,128)S(1)} custom-call(s32[4]{0:T(128)S(1)} %pad_add_fusion.1.places, bf16[1024,4096]{1,0:T(8,128)(2,1)S(1)} %shard_map.64.refs_0_.refs_1_.refs_2_.refs_3_, bf16[1024,4096]{1,0:T(8,128)(2,1)S(1)} %shard_map.64.refs_0_.refs_1_.refs_2_.refs_3_, bf16[1024,4096]{1,0:T(8,128)(2,1)S(1)} %shard_map.64.refs_0_.refs_1_.refs_2_.refs_3_, ...), custom_call_target="tpu_custom_call" | custom-call | flops 1610612736 | bytes 8000000 | tf_op jit(solution)/shard_map/pallas_call | solution.py:140
  135.2 3.3 %shard_map.68.proj = bf16[1024,768]{1,0:T(8,128)(2,1)S(1)} custom-call(s32[4]{0:T(128)S(1)} %pad_add_fusion.places, bf16[1024,4096]{1,0:T(8,128)(2,1)S(1)} %shard_map.64.refs_0_.refs_1_.refs_2_.refs_3_, bf16[1024,4096]{1,0:T(8,128)(2,1)S(1)} %shard_map.64.refs_0_.refs_1_.refs_2_.refs_3_, bf16[1024,4096]{1,0:T(8,128)(2,1)S(1)} %shard_map.64.refs_0_.refs_1_.refs_2_.refs_3_, ...), custom_call_target="tpu_custom_call" | custom-call | flops 1610612736 | bytes 8000000 | tf_op jit(solution)/shard_map/pallas_call | solution.py:140
  138.8 6.3 %collective-permute-start.22 = (bf16[176,256]{1,0:T(8,128)(2,1)S(1)}, bf16[176,256]{1,0:T(8,128)(2,1)S(1)}, u32[]{:S(2)}, u32[]{:S(2)}) collective-permute-start(bf16[176,256]{1,0:T(8,128)(2,1)S(1)} %pad_maximum_fusion.1), channel_id=1, source_target_pairs={{0,8},{8,16},{16,24},{24,32},{32,40},{40,48},{48,56},{56,64},{64,7... | collective-permute-start | bytes 270344 | tf_op jit(solution)/shard_map/ppermute | solution.py:285
  145.1 6.7 %shard_map.72 = bf16[1024,256]{1,0:T(8,128)(2,1)} custom-call(s32[8]{0:T(128)S(1)} %compare_convert_fusion.flags, bf16[1024,768]{1,0:T(8,128)(2,1)S(1)} %shard_map.68.proj, bf16[176,256]{1,0:T(8,128)(2,1)S(1)} %collective-permute-done.23.halo, f32[9,256]{1,0:T(8,128)S(1)} %slice_convert_fusion.short, bf16[16,256,128]{2,1,0:T(8,128)(2,1)S(1)} %shard_map.71.band, ...), custom_call_target="tpu_custom_call" | custom-call | flops 10000000000 | bytes 4000000 | tf_op jit(solution)/shard_map/pallas_call | solution.py:219
  151.9 8.1 %all-to-all-start.1 = ((bf16[8,128,256]{2,1,0:T(8,128)(2,1)}), bf16[8,128,256]{2,1,0:T(8,128)(2,1)}, u32[]{:S(2)}, u32[]{:S(2)}) async-start(bf16[8,128,256]{2,1,0:T(8,128)(2,1)} %bitcast.42), calls=%async_computation.1 | async-start | bytes 1048576 | tf_op jit(solution)/shard_map/all_to_all | solution.py:289
  160.0 6.7 %shard_map.70 = bf16[1024,256]{1,0:T(8,128)(2,1)} custom-call(s32[8]{0:T(128)S(1)} %compare_convert_fusion.flags, bf16[1024,768]{1,0:T(8,128)(2,1)S(1)} %convolution_convert_fusion.proj, bf16[176,256]{1,0:T(8,128)(2,1)S(1)} %collective-permute-done.22.halo, f32[9,256]{1,0:T(8,128)S(1)} %convert_element_type.91.short, bf16[16,256,128]{2,1,0:T(8,128)(2,1)S(1)} %copy-done.2, ...), custom_call_target="tpu_custom_call" | custom-call | flops 10000000000 | bytes 4000000 | tf_op jit(solution)/shard_map/pallas_call | solution.py:219
  166.7 2.9 %all-to-all-done.1 = bf16[8,128,256]{2,1,0:T(8,128)(2,1)} async-done(((bf16[8,128,256]{2,1,0:T(8,128)(2,1)}), bf16[8,128,256]{2,1,0:T(8,128)(2,1)}, u32[]{:S(2)}, u32[]{:S(2)}) %all-to-all-start.1) | async-done | bytes 524320 | tf_op jit(solution)/shard_map/all_to_all | solution.py:289
  169.6 4.3 %all-to-all-start = ((bf16[8,128,256]{2,1,0:T(8,128)(2,1)}), bf16[8,128,256]{2,1,0:T(8,128)(2,1)S(1)}, u32[]{:S(2)}, u32[]{:S(2)}) async-start(bf16[8,128,256]{2,1,0:T(8,128)(2,1)} %bitcast.35), calls=%async_computation | async-start | bytes 1048576 | tf_op jit(solution)/shard_map/all_to_all | solution.py:289
  173.8 9.5 %all-to-all-done = bf16[8,128,256]{2,1,0:T(8,128)(2,1)S(1)} async-done(((bf16[8,128,256]{2,1,0:T(8,128)(2,1)}), bf16[8,128,256]{2,1,0:T(8,128)(2,1)S(1)}, u32[]{:S(2)}, u32[]{:S(2)}) %all-to-all-start) | async-done | bytes 524320 | tf_op jit(solution)/shard_map/all_to_all | solution.py:289
  (107 shorter events, 40.1 us)
Async XLA Ops:
  7.9 25.4 %collective-permute-start.5 = (bf16[256,4096]{1,0:T(8,128)(2,1)S(1)}, bf16[256,4096]{1,0:T(8,128)(2,1)}, u32[]{:S(2)}, u32[]{:S(2)}) collective-permute-start(bf16[256,4096]{1,0:T(8,128)(2,1)S(1)} %pad_maximum_fusion.refs_0_), channel_id=1, source_target_pairs={{0,2},{1,7},{2,4},{3,1},{4,6},{5,3},{6,0},{7,5},{8,10},{9,15},{10,... | collective-permute-start | bytes 6291464 | tf_op jit(solution)/shard_map/ppermute | solution.py:90
  10.0 38.3 %collective-permute-start = (bf16[256,768]{1,0:T(8,128)(2,1)}, bf16[256,768]{1,0:T(8,128)(2,1)}, u32[]{:S(2)}, u32[]{:S(2)}) collective-permute-start(bf16[256,768]{1,0:T(8,128)(2,1)} %copy.18), channel_id=1, source_target_pairs={{0,8},{8,0},{1,9},{9,1},{2,10},{10,2},{3,11},{11,3},{4,12},{12,4},... | collective-permute-start | bytes 1179656 | tf_op jit(solution)/shard_map/ppermute | solution.py:17
  16.9 35.3 %collective-permute-start.9 = (bf16[17,256]{1,0:T(8,128)(2,1)S(1)}, bf16[17,256]{1,0:T(8,128)(2,1)S(1)}, u32[]{:S(2)}, u32[]{:S(2)}) collective-permute-start(bf16[17,256]{1,0:T(8,128)(2,1)S(1)} %pad_maximum_fusion.3), channel_id=1, source_target_pairs={{0,8},{8,0},{1,9},{9,1},{2,10},{10,2},{3,11},{11,3},{4,12},{12,4},... | collective-permute-start | bytes 26120 | tf_op jit(solution)/shard_map/ppermute | solution.py:17
  35.6 34.0 %collective-permute-start.7 = (bf16[128,4096]{1,0:T(8,128)(2,1)}, bf16[128,4096]{1,0:T(8,128)(2,1)}, u32[]{:S(2)}, u32[]{:S(2)}) collective-permute-start(bf16[128,4096]{1,0:T(8,128)(2,1)} %constant_dynamic-slice_fusion), channel_id=1, source_target_pairs={{0,2},{1,7},{2,4},{3,1},{4,6},{5,3},{6,0},{7,5},{8,10},{9,15},{10,... | collective-permute-start | bytes 3145736 | tf_op jit(solution)/shard_map/ppermute | solution.py:92
  37.6 53.5 %collective-permute-start.6 = (bf16[256,4096]{1,0:T(8,128)(2,1)}, bf16[256,4096]{1,0:T(8,128)(2,1)}, u32[]{:S(2)}, u32[]{:S(2)}) collective-permute-start(bf16[256,4096]{1,0:T(8,128)(2,1)} %collective-permute-done.5.refs_1_), channel_id=1, source_target_pairs={{0,1},{1,0},{2,3},{3,2},{4,5},{5,4},{6,7},{7,6},{8,9},{9,8},{10,11... | collective-permute-start | bytes 6291464 | tf_op jit(solution)/shard_map/ppermute | solution.py:17
  48.2 13.3 %collective-permute-start.1 = (bf16[256,768]{1,0:T(8,128)(2,1)}, bf16[256,768]{1,0:T(8,128)(2,1)}, u32[]{:S(2)}, u32[]{:S(2)}) collective-permute-start(bf16[256,768]{1,0:T(8,128)(2,1)} %collective-permute-done.refs_4_), channel_id=1, source_target_pairs={{0,64},{64,128},{128,192},{192,0},{1,65},{65,129},{129,193},{193,1... | collective-permute-start | bytes 1179656 | tf_op jit(solution)/shard_map/ppermute | solution.py:22
  49.5 18.9 %collective-permute-start.2 = (bf16[256,768]{1,0:T(8,128)(2,1)}, bf16[256,768]{1,0:T(8,128)(2,1)}, u32[]{:S(2)}, u32[]{:S(2)}) collective-permute-start(bf16[256,768]{1,0:T(8,128)(2,1)} %collective-permute-done.refs_4_), channel_id=1, source_target_pairs={{0,192},{64,0},{128,64},{192,128},{1,193},{65,1},{129,65},{193,129... | collective-permute-start | bytes 1179656 | tf_op jit(solution)/shard_map/ppermute | solution.py:22
  52.2 19.2 %collective-permute-start.19 = (bf16[256,768]{1,0:T(8,128)(2,1)}, bf16[256,768]{1,0:T(8,128)(2,1)S(1)}, u32[]{:S(2)}, u32[]{:S(2)}) collective-permute-start(bf16[256,768]{1,0:T(8,128)(2,1)} %collective-permute-done.refs_4_), channel_id=1, source_target_pairs={{0,16},{16,32},{32,48},{48,0},{1,17},{17,33},{33,49},{49,1},{2,18}... | collective-permute-start | bytes 1179656 | tf_op jit(solution)/shard_map/ppermute | solution.py:22
  61.5 11.6 %collective-permute-start.20 = (bf16[256,768]{1,0:T(8,128)(2,1)}, bf16[256,768]{1,0:T(8,128)(2,1)S(1)}, u32[]{:S(2)}, u32[]{:S(2)}) collective-permute-start(bf16[256,768]{1,0:T(8,128)(2,1)} %collective-permute-done.refs_4_), channel_id=1, source_target_pairs={{0,48},{16,0},{32,16},{48,32},{1,49},{17,1},{33,17},{49,33},{2,50}... | collective-permute-start | bytes 1179656 | tf_op jit(solution)/shard_map/ppermute | solution.py:22
  68.4 10.5 %collective-permute-start.16 = (bf16[256,768]{1,0:T(8,128)(2,1)}, bf16[256,768]{1,0:T(8,128)(2,1)S(1)}, u32[]{:S(2)}, u32[]{:S(2)}) collective-permute-start(bf16[256,768]{1,0:T(8,128)(2,1)} %collective-permute-done.1.refs_4_), channel_id=1, source_target_pairs={{0,16},{16,32},{32,48},{48,0},{1,17},{17,33},{33,49},{49,1},{2,18}... | collective-permute-start | bytes 1179656 | tf_op jit(solution)/shard_map/ppermute | solution.py:22
  69.6 20.6 %collective-permute-start.8 = (bf16[128,4096]{1,0:T(8,128)(2,1)}, bf16[128,4096]{1,0:T(8,128)(2,1)}, u32[]{:S(2)}, u32[]{:S(2)}) collective-permute-start(bf16[128,4096]{1,0:T(8,128)(2,1)} %collective-permute-done.7.refs_3_), channel_id=1, source_target_pairs={{0,1},{1,0},{2,3},{3,2},{4,5},{5,4},{6,7},{7,6},{8,9},{9,8},{10,11... | collective-permute-start | bytes 3145736 | tf_op jit(solution)/shard_map/ppermute | solution.py:17
  71.4 11.0 %collective-permute-start.17 = (bf16[256,768]{1,0:T(8,128)(2,1)}, bf16[256,768]{1,0:T(8,128)(2,1)S(1)}, u32[]{:S(2)}, u32[]{:S(2)}) collective-permute-start(bf16[256,768]{1,0:T(8,128)(2,1)} %collective-permute-done.1.refs_4_), channel_id=1, source_target_pairs={{0,48},{16,0},{32,16},{48,32},{1,49},{17,1},{33,17},{49,33},{2,50}... | collective-permute-start | bytes 1179656 | tf_op jit(solution)/shard_map/ppermute | solution.py:22
  73.2 14.2 %collective-permute-start.13 = (bf16[256,768]{1,0:T(8,128)(2,1)}, bf16[256,768]{1,0:T(8,128)(2,1)S(1)}, u32[]{:S(2)}, u32[]{:S(2)}) collective-permute-start(bf16[256,768]{1,0:T(8,128)(2,1)} %collective-permute-done.2.refs_4_), channel_id=1, source_target_pairs={{0,16},{16,32},{32,48},{48,0},{1,17},{17,33},{33,49},{49,1},{2,18}... | collective-permute-start | bytes 1179656 | tf_op jit(solution)/shard_map/ppermute | solution.py:22
  79.0 10.7 %collective-permute-start.14 = (bf16[256,768]{1,0:T(8,128)(2,1)}, bf16[256,768]{1,0:T(8,128)(2,1)S(1)}, u32[]{:S(2)}, u32[]{:S(2)}) collective-permute-start(bf16[256,768]{1,0:T(8,128)(2,1)} %collective-permute-done.2.refs_4_), channel_id=1, source_target_pairs={{0,48},{16,0},{32,16},{48,32},{1,49},{17,1},{33,17},{49,33},{2,50}... | collective-permute-start | bytes 1179656 | tf_op jit(solution)/shard_map/ppermute | solution.py:22
  82.4 39.8 %collective-permute-start.21 = (bf16[256,768]{1,0:T(8,128)(2,1)S(1)}, bf16[256,768]{1,0:T(8,128)(2,1)S(1)}, u32[]{:S(2)}, u32[]{:S(2)}) collective-permute-start(bf16[256,768]{1,0:T(8,128)(2,1)S(1)} %broadcast_select_fusion.2), channel_id=1, source_target_pairs={{0,16},{1,49},{16,32},{17,1},{32,48},{33,17},{48,0},{49,33},{2,18}... | collective-permute-start | bytes 1179656 | tf_op jit(solution)/shard_map/ppermute | solution.py:111
  87.4 18.2 %collective-permute-start.3 = (bf16[256,768]{1,0:T(8,128)(2,1)}, bf16[256,768]{1,0:T(8,128)(2,1)S(1)}, u32[]{:S(2)}, u32[]{:S(2)}) collective-permute-start(bf16[256,768]{1,0:T(8,128)(2,1)} %collective-permute-done.refs_4_), channel_id=1, source_target_pairs={{0,128},{64,192},{128,0},{192,64},{1,129},{65,193},{129,1},{193,65... | collective-permute-start | bytes 1179656 | tf_op jit(solution)/shard_map/ppermute | solution.py:22
  89.6 36.9 %collective-permute-start.18 = (bf16[256,768]{1,0:T(8,128)(2,1)S(1)}, bf16[256,768]{1,0:T(8,128)(2,1)S(1)}, u32[]{:S(2)}, u32[]{:S(2)}) collective-permute-start(bf16[256,768]{1,0:T(8,128)(2,1)S(1)} %broadcast_select_fusion.3), channel_id=1, source_target_pairs={{0,16},{1,49},{16,32},{17,1},{32,48},{33,17},{48,0},{49,33},{2,18}... | collective-permute-start | bytes 1179656 | tf_op jit(solution)/shard_map/ppermute | solution.py:111
  90.2 40.6 %collective-permute-start.15 = (bf16[256,768]{1,0:T(8,128)(2,1)S(1)}, bf16[256,768]{1,0:T(8,128)(2,1)S(1)}, u32[]{:S(2)}, u32[]{:S(2)}) collective-permute-start(bf16[256,768]{1,0:T(8,128)(2,1)S(1)} %broadcast_select_fusion.4), channel_id=1, source_target_pairs={{0,16},{1,49},{16,32},{17,1},{32,48},{33,17},{48,0},{49,33},{2,18}... | collective-permute-start | bytes 1179656 | tf_op jit(solution)/shard_map/ppermute | solution.py:111
  105.6 16.3 %collective-permute-start.11 = (bf16[256,768]{1,0:T(8,128)(2,1)S(1)}, bf16[256,768]{1,0:T(8,128)(2,1)S(1)}, u32[]{:S(2)}, u32[]{:S(2)}) collective-permute-start(bf16[256,768]{1,0:T(8,128)(2,1)S(1)} %collective-permute-done.3.refs_4_), channel_id=1, source_target_pairs={{0,48},{16,0},{32,16},{48,32},{1,49},{17,1},{33,17},{49,33},{2,50}... | collective-permute-start | bytes 1179656 | tf_op jit(solution)/shard_map/ppermute | solution.py:22
  113.4 31.7 %collective-permute-start.23 = (bf16[176,256]{1,0:T(8,128)(2,1)S(1)}, bf16[176,256]{1,0:T(8,128)(2,1)S(1)}, u32[]{:S(2)}, u32[]{:S(2)}) collective-permute-start(bf16[176,256]{1,0:T(8,128)(2,1)S(1)} %pad_maximum_fusion.2), channel_id=1, source_target_pairs={{0,8},{8,16},{16,24},{24,32},{32,40},{40,48},{48,56},{56,64},{64,7... | collective-permute-start | bytes 270344 | tf_op jit(solution)/shard_map/ppermute | solution.py:285
  121.9 13.3 %collective-permute-start.12 = (bf16[256,768]{1,0:T(8,128)(2,1)S(1)}, bf16[256,768]{1,0:T(8,128)(2,1)S(1)}, u32[]{:S(2)}, u32[]{:S(2)}) collective-permute-start(bf16[256,768]{1,0:T(8,128)(2,1)S(1)} %broadcast_select_fusion.5), channel_id=1, source_target_pairs={{0,16},{1,49},{16,32},{17,1},{32,48},{33,17},{48,0},{49,33},{2,18}... | collective-permute-start | bytes 1179656 | tf_op jit(solution)/shard_map/ppermute | solution.py:111
  138.8 21.2 %collective-permute-start.22 = (bf16[176,256]{1,0:T(8,128)(2,1)S(1)}, bf16[176,256]{1,0:T(8,128)(2,1)S(1)}, u32[]{:S(2)}, u32[]{:S(2)}) collective-permute-start(bf16[176,256]{1,0:T(8,128)(2,1)S(1)} %pad_maximum_fusion.1), channel_id=1, source_target_pairs={{0,8},{8,16},{16,24},{24,32},{32,40},{40,48},{48,56},{56,64},{64,7... | collective-permute-start | bytes 270344 | tf_op jit(solution)/shard_map/ppermute | solution.py:285
  151.9 17.7 %all-to-all-start.1 = ((bf16[8,128,256]{2,1,0:T(8,128)(2,1)}), bf16[8,128,256]{2,1,0:T(8,128)(2,1)}, u32[]{:S(2)}, u32[]{:S(2)}) async-start(bf16[8,128,256]{2,1,0:T(8,128)(2,1)} %bitcast.42), calls=%async_computation.1 | async-start | bytes 1048576 | tf_op jit(solution)/shard_map/all_to_all | solution.py:289
  169.6 13.8 %all-to-all-start = ((bf16[8,128,256]{2,1,0:T(8,128)(2,1)}), bf16[8,128,256]{2,1,0:T(8,128)(2,1)S(1)}, u32[]{:S(2)}, u32[]{:S(2)}) async-start(bf16[8,128,256]{2,1,0:T(8,128)(2,1)} %bitcast.35), calls=%async_computation | async-start | bytes 1048576 | tf_op jit(solution)/shard_map/all_to_all | solution.py:289
  (13 other events, 123.4 us)

commit v3 on v2

--- a/solution.py
+++ b/solution.py
@@ -49,69 +49,22 @@
     )(long_filter.astype(jnp.float32))
 
 
-def place(pieces, at, rows):
-    width = pieces[0].shape[1]
-    counts = [piece.shape[0] // rows for piece in pieces]
-    firsts = [sum(counts[:n]) for n in range(len(pieces))]
-
-    def kernel(at, *refs):
-        del at
-        step = pl.program_id(0)
-        for n, (first, count) in enumerate(zip(firsts, counts)):
-
-            @pl.when(jnp.logical_and(step >= first, step < first + count))
-            def _(n=n):
-                refs[-1][...] = refs[n][...]
-
-    def pick(first, count):
-        return pl.BlockSpec((rows, width), lambda step, at: (jnp.clip(step - first, 0, count - 1), 0))
-
-    spec = pltpu.PrefetchScalarGridSpec(
-        num_scalar_prefetch=1,
-        grid=(sum(counts),),
-        in_specs=[pick(first, count) for first, count in zip(firsts, counts)],
-        out_specs=pl.BlockSpec((rows, width), lambda step, at: (at[step], 0)),
-    )
-    return pl.pallas_call(
-        kernel,
-        out_shape=jax.ShapeDtypeStruct((sum(counts) * rows, width), pieces[0].dtype),
-        grid_spec=spec,
-        compiler_params=pltpu.CompilerParams(vmem_limit_bytes=24 << 20),
-        cost_estimate=pl.CostEstimate(flops=0, bytes_accessed=16_000_000, transcendentals=0),
-    )(jnp.stack(at).astype(jnp.int32), *pieces)
-
-
-def gather_tokens(normed):
-    rows = normed.shape[0]
-    y, core = lax.axis_index("y"), lax.axis_index("core")
-    size = lax.axis_size("y")
-    sib = swap(normed, "core")
-    pair = jnp.concatenate([jnp.where(core == 0, normed, sib), jnp.where(core == 0, sib, normed)], axis=0)
-    near = lax.ppermute(pair, ("y", "core"), fan("y"))
-    near_half = lax.dynamic_slice_in_dim(near, core * rows, rows, 0)
-    far = lax.ppermute(near_half, ("y", "core"), fan("y"))
-    near_sib = swap(near, "core")
-    far_sib = swap(far, "core")
-    sign = 1 - 2 * core
-    at = [2 * a + c for a in (y, (y - sign + size) % size, (y + sign + size) % size) for c in range(2)]
-    at += [2 * ((y + 2) % size) + core, 2 * ((y + 2) % size) + 1 - core]
-    return place([pair, near, near_sib, far, far_sib], at, rows)
-
-
 def spread_columns(piece):
     up, down = shift(piece, "z_lo", 1), shift(piece, "z_lo", -1)
     late, up, down = lax.optimization_barrier((piece, up, down))
     return (0, piece), (1, up), (-1, down), (2, shift(late, "z_lo", 2))
 
 
-def spread_rows(by, mine):
-    z_lo, x, core = lax.axis_index("z_lo"), lax.axis_index("x"), lax.axis_index("core")
+def spread_rows(mine):
+    below, above = shift(mine, "x", 1), shift(mine, "x", -1)
+    return below, above, jnp.where(lax.axis_index("core") == 0, below, above)
+
+
+def places_of(by):
+    z_lo, x = lax.axis_index("z_lo"), lax.axis_index("x")
     depth, size = lax.axis_size("z_lo"), lax.axis_size("x")
-    below, above = shift(mine, "x", 1), shift(mine, "x", -1)
-    far = lax.ppermute(jnp.where(core == 0, below, above), ("x", "core"), fan("x"))
     first = (z_lo - by + depth) % depth * size
-    places = [first + x, first + (x + size - 1) % size, first + (x + 1) % size, first + (x + 2) % size]
-    return [mine, below, above, far], places
+    return [first + x, first + (x + size - 1) % size, first + (x + 1) % size, first + (x + 2) % size]
 
 
 def add_product_kernel(count, places, *refs):
@@ -270,7 +223,9 @@
     scale_rows = lax.rsqrt(jnp.mean(float_tokens * float_tokens, axis=-1, keepdims=True) + 1e-06)
     normed = (float_tokens * scale_rows * norm_gain.astype(jnp.float32)[None]).astype(jnp.bfloat16)
     in_weight, normed = lax.optimization_barrier((in_weight, normed))
-    gathered = gather_tokens(normed)
+    gathered = lax.all_gather(normed, ("y", "core"), axis=0, tiled=True)
+    weight_t = in_weight.transpose(1, 2, 0).reshape(3 * channels, width)
+    piece, weight_t = lax.optimization_barrier((piece, weight_t))
     columns = spread_columns(piece)
 
     small = jnp.concatenate(
@@ -290,19 +245,24 @@
 
     own_short = short_filter.reshape(3 * taps, channels).astype(jnp.float32)
     other_short = other_short.astype(jnp.float32)
-    own_projected = jnp.dot(
-        gathered, in_weight.reshape(width, 3 * channels), preferred_element_type=jnp.float32
+    own_projected = lax.dot_general(
+        gathered, weight_t, (((1,), (1,)), ((), ())), preferred_element_type=jnp.float32
     ).astype(jnp.bfloat16)
+    rows_of = [spread_rows(mine) for _, mine in columns]
+    other_projected = None
+    for n, ((by, mine), (below, above, onward)) in enumerate(zip(columns, rows_of)):
+        last = n == len(columns) - 1
+        if n == len(columns) - 2:
+            onward, own_projected = lax.optimization_barrier((onward, own_projected))
+        far = lax.ppermute(onward, ("x", "core"), fan("x"))
+        other_projected = add_product(
+            gathered,
+            [mine, below, above, far],
+            places_of(by),
+            other_projected,
+            jnp.bfloat16 if last else jnp.float32,
+        )
     other_halo = halo_of(own_projected, own_short)
-    other_projected = None
-    for n, (by, mine) in enumerate(columns):
-        last = n == len(columns) - 1
-        if last:
-            mine, own_projected = lax.optimization_barrier((mine, own_projected))
-        pieces, places = spread_rows(by, mine)
-        other_projected = add_product(
-            gathered, pieces, places, other_projected, jnp.bfloat16 if last else jnp.float32
-        )
     own_halo = halo_of(other_projected, other_short)
     own = finish(own_projected, own_halo, own_short, long_filter)
     other = finish(other_projected, other_halo, other_short, other_long)

time: 188 us -> 178 us (0.947); the launches traced: 186 us -> 178 us
  starting transfers between devices: 64 us -> 48.2 us
  between operations: 0.56 us -> 14.3 us
  waiting for transfers between devices: 59.2 us -> 49.7 us
  other arithmetic: 4.15 us -> 11.8 us
  Pallas kernels: 36.4 us -> 29.9 us
  matrix products: 6.7 us -> 11.1 us
    ppermute x6 -> x4, waiting for transfers between devices: 15.7 us -> 0.01 us  [per_device(): far = lax.ppermute(onward, ('x', 'core'), fan('x'))]
    ppermute x11, waiting for transfers between devices: 28.8 us -> 37.3 us  [shift(): lax.ppermute(value, axis, [(i, (i + by) % size) for i in range(size)])]
    pallas_call x1 -> x0, Pallas kernels: 6.26 us -> none  [place(): pl.pallas_call(kernel, out_shape=jax.ShapeDtypeStruct((sum(counts) * rows...]
    ppermute x5 -> x2, starting transfers between devices: 12.7 us -> 7.94 us  [swap(): return lax.ppermute(value, axis, [(0, 1), (1, 0)])]
    dot_general x1, matrix products: 6.7 us -> 11.1 us  [per_device(): lax.dot_general(gathered, weight_t, (((1,), (1,)), ((), ())), preferred_e...]
    ppermute x2, starting transfers between devices: 14.8 us -> 10.5 us  [halo_of(): lax.ppermute(tail_of(projected, short, starts), ('z_lo', 'x', 'z_hi'), ne...]
    ppermute x6 -> x4, starting transfers between devices: 7.38 us -> 3.69 us  [per_device(): far = lax.ppermute(onward, ('x', 'core'), fan('x'))]
    select_n x5 -> x4, other arithmetic: 0.33 us -> 3.19 us  [spread_rows(): return (below, above, jnp.where(lax.axis_index('core') == 0, below, above))]
  transfers between devices with their start and end apart: 26 -> 22, of which waited for: 11 -> 7; matrix products, arithmetic and copies ran while one was open for 11% -> 17% of each run, Pallas kernels for 20% -> 17%
where the time goes in v3:
time: 178 us
  waiting for transfers between devices  49.7 us (28%)
  starting transfers between devices  48.2 us (27%)
  Pallas kernels  29.9 us (17%)
  between operations  14.3 us (8%)
  local copies, waits for them, and re-layouts  13.1 us (7%)
  other arithmetic  11.8 us (7%)
  matrix products  11.1 us (6%)
    ppermute x11, waiting for transfers between devices, shift(): lax.ppermute(value, axis, [(i, (i + by) % size) for i in range(size)])  37.3 us
    pallas_call x4, Pallas kernels, add_product(): pl.pallas_call(functools.partial(add_product_kernel, count), out_shape=ja...  16.1 us
    ppermute x11, starting transfers between devices, shift(): lax.ppermute(value, axis, [(i, (i + by) % size) for i in range(size)])  14.1 us
    pallas_call x2, Pallas kernels, mix_conv(): pl.pallas_call(mix_conv_kernel, out_shape=jax.ShapeDtypeStruct((length, c...  13.3 us
    all_to_all x2, waiting for transfers between devices, finish(): lax.all_to_all(gated, ('y', 'core'), split_axis=0, concat_axis=1, tiled=T...  12.4 us
    all_to_all x2, starting transfers between devices, finish(): lax.all_to_all(gated, ('y', 'core'), split_axis=0, concat_axis=1, tiled=T...  12 us
    dot_general x1, matrix products, per_device(): lax.dot_general(gathered, weight_t, (((1,), (1,)), ((), ())), preferred_e...  11.1 us
    ppermute x2, starting transfers between devices, halo_of(): lax.ppermute(tail_of(projected, short, starts), ('z_lo', 'x', 'z_hi'), ne...  10.5 us
  transfers between devices with their start and end apart: 22, of which 7 were waited for; matrix products, arithmetic and copies ran while one was open for 17% of the time, Pallas kernels for 17%

profile of v3, /device:TPU:1, one launch (start us, length us, event | category | flops | bytes accessed | tf_op | source)
XLA Modules:
  0.0 178.0 jit_solution(6363857008101870662)
XLA Ops:
  9.7 7.8 %collective-permute-start = (bf16[256,768]{1,0:T(8,128)(2,1)S(1)}, bf16[256,768]{1,0:T(8,128)(2,1)S(1)}, u32[]{:S(2)}, u32[]{:S(2)}) collective-permute-start(bf16[256,768]{1,0:T(8,128)(2,1)S(1)} %copy.18), channel_id=1, source_target_pairs={{0,8},{8,0},{1,9},{9,1},{2,10},{10,2},{3,11},{11,3},{4,12},{12,4},... | collective-permute-start | bytes 1179656 | tf_op jit(solution)/shard_map/ppermute | solution.py:17
  23.1 8.8 %copy.19 = bf16[4096,3,256]{0,2,1:T(8,128)(2,1)} copy(bf16[4096,3,256]{2,0,1:T(8,128)(2,1)} %param.8) | data formatting | bytes 12582912 | tf_op jit(solution)/shard_map/optimization_barrier | solution.py:225
  33.0 3.2 %collective-permute-start.1 = (bf16[256,768]{1,0:T(8,128)(2,1)S(1)}, bf16[256,768]{1,0:T(8,128)(2,1)S(1)}, u32[]{:S(2)}, u32[]{:S(2)}) collective-permute-start(bf16[256,768]{1,0:T(8,128)(2,1)S(1)} %collective-permute-done.refs_4_), channel_id=1, source_target_pairs={{0,64},{64,128},{128,192},{192,0},{1,65},{65,129},{129,193},{193,1... | collective-permute-start | bytes 1179656 | tf_op jit(solution)/shard_map/ppermute | solution.py:22
  39.6 3.7 %collective-permute-done.1.refs_4_ = bf16[256,768]{1,0:T(8,128)(2,1)S(1)} collective-permute-done((bf16[256,768]{1,0:T(8,128)(2,1)S(1)}, bf16[256,768]{1,0:T(8,128)(2,1)S(1)}, u32[]{:S(2)}, u32[]{:S(2)}) %collective-permute-start.1) | collective-permute-done | bytes 393248 | tf_op jit(solution)/shard_map/ppermute | solution.py:22
  43.3 11.1 %collective-permute-done.2.refs_4_ = bf16[256,768]{1,0:T(8,128)(2,1)S(1)} collective-permute-done((bf16[256,768]{1,0:T(8,128)(2,1)S(1)}, bf16[256,768]{1,0:T(8,128)(2,1)S(1)}, u32[]{:S(2)}, u32[]{:S(2)}) %collective-permute-start.2) | collective-permute-done | bytes 393248 | tf_op jit(solution)/shard_map/ppermute | solution.py:22
  57.4 2.6 %collective-permute-start.4 = (bf16[256,768]{1,0:T(8,128)(2,1)S(1)}, bf16[256,768]{1,0:T(8,128)(2,1)S(1)}, u32[]{:S(2)}, u32[]{:S(2)}) collective-permute-start(bf16[256,768]{1,0:T(8,128)(2,1)S(1)} %collective-permute-done.2.refs_4_), channel_id=1, source_target_pairs={{0,48},{16,0},{32,16},{48,32},{1,49},{17,1},{33,17},{49,33},{2,50}... | collective-permute-start | bytes 1179656 | tf_op jit(solution)/shard_map/ppermute | solution.py:22
  60.9 4.9 %collective-permute-done.11.refs_5_ = bf16[256,768]{1,0:T(8,128)(2,1)S(1)} collective-permute-done((bf16[256,768]{1,0:T(8,128)(2,1)S(1)}, bf16[256,768]{1,0:T(8,128)(2,1)S(1)}, u32[]{:S(2)}, u32[]{:S(2)}) %collective-permute-start.11) | collective-permute-done | bytes 393248 | tf_op jit(solution)/shard_map/ppermute | solution.py:22
  67.1 10.4 %collective-permute-done.6.refs_4_ = bf16[256,768]{1,0:T(8,128)(2,1)S(1)} collective-permute-done((bf16[256,768]{1,0:T(8,128)(2,1)S(1)}, bf16[256,768]{1,0:T(8,128)(2,1)S(1)}, u32[]{:S(2)}, u32[]{:S(2)}) %collective-permute-start.6) | collective-permute-done | bytes 393248 | tf_op jit(solution)/shard_map/ppermute | solution.py:22
  77.5 2.7 %collective-permute-start.8 = (bf16[256,768]{1,0:T(8,128)(2,1)S(1)}, bf16[256,768]{1,0:T(8,128)(2,1)S(1)}, u32[]{:S(2)}, u32[]{:S(2)}) collective-permute-start(bf16[256,768]{1,0:T(8,128)(2,1)S(1)} %collective-permute-done.6.refs_4_), channel_id=1, source_target_pairs={{0,48},{16,0},{32,16},{48,32},{1,49},{17,1},{33,17},{49,33},{2,50}... | collective-permute-start | bytes 1179656 | tf_op jit(solution)/shard_map/ppermute | solution.py:22
  81.7 7.2 %collective-permute-done.7.refs_5_ = bf16[256,768]{1,0:T(8,128)(2,1)S(1)} collective-permute-done((bf16[256,768]{1,0:T(8,128)(2,1)S(1)}, bf16[256,768]{1,0:T(8,128)(2,1)S(1)}, u32[]{:S(2)}, u32[]{:S(2)}) %collective-permute-start.7) | collective-permute-done | bytes 393248 | tf_op jit(solution)/shard_map/ppermute | solution.py:22
  89.7 2.4 %collective-permute-start.9 = (bf16[256,768]{1,0:T(8,128)(2,1)}, bf16[256,768]{1,0:T(8,128)(2,1)}, u32[]{:S(2)}, u32[]{:S(2)}) collective-permute-start(bf16[256,768]{1,0:T(8,128)(2,1)} %broadcast_select_fusion.2), channel_id=1, source_target_pairs={{0,16},{1,49},{16,32},{17,1},{32,48},{33,17},{48,0},{49,33},{2,18}... | collective-permute-start | bytes 1179656 | tf_op jit(solution)/shard_map/ppermute | solution.py:257
  92.2 11.1 %convolution_convert_fusion.proj = bf16[1024,768]{1,0:T(8,128)(2,1)S(1)} fusion(bf16[1024,4096]{1,0:T(8,128)(2,1)} %all-gather.2.cloned.1.call-done.refs_0_.refs_1_.refs_2_.refs_3_, bf16[768,4096]{1,0:T(8,128)(2,1)} %bitcast.51), kind=kOutput, calls=%fused_computation.7 | convolution fusion | flops 6443237376 | bytes 16252928 | tf_op jit(solution)/shard_map/dot_general | solution.py:248
  103.7 7.3 %collective-permute-start.18 = (bf16[176,256]{1,0:T(8,128)(2,1)S(1)}, bf16[176,256]{1,0:T(8,128)(2,1)S(1)}, u32[]{:S(2)}, u32[]{:S(2)}) collective-permute-start(bf16[176,256]{1,0:T(8,128)(2,1)S(1)} %pad_maximum_fusion.1), channel_id=1, source_target_pairs={{0,8},{8,16},{16,24},{24,32},{32,40},{40,48},{48,56},{56,64},{64,7... | collective-permute-start | bytes 270344 | tf_op jit(solution)/shard_map/ppermute | solution.py:240
  111.0 4.3 %shard_map.64.refs_8_ = f32[1024,768]{1,0:T(8,128)S(1)} custom-call(s32[4]{0:T(128)S(1)} %copy-done.13, bf16[1024,4096]{1,0:T(8,128)(2,1)S(1)} %copy-done, bf16[1024,4096]{1,0:T(8,128)(2,1)S(1)} %copy-done, bf16[1024,4096]{1,0:T(8,128)(2,1)S(1)} %copy-done, bf16[1024,4096]{1,0:T(8,128)(2,1)S(1)} %copy-done, ...), custom_call_target="tpu_custom_call" | custom-call | flops 1610612736 | bytes 8000000 | tf_op jit(solution)/shard_map/pallas_call | solution.py:93
  115.4 4.3 %shard_map.65.refs_8_ = f32[1024,768]{1,0:T(8,128)S(1)} custom-call(s32[4]{0:T(128)S(1)} %copy-done.14, bf16[1024,4096]{1,0:T(8,128)(2,1)S(1)} %copy-done, bf16[1024,4096]{1,0:T(8,128)(2,1)S(1)} %copy-done, bf16[1024,4096]{1,0:T(8,128)(2,1)S(1)} %copy-done, bf16[1024,4096]{1,0:T(8,128)(2,1)S(1)} %copy-done, bf16[256,768]{1,0:T(8,128)(2,1)S(1)} %copy-done.5, ...), custom_call_target="tpu_custom_call" | custom-call | flops 1610612736 | bytes 8000000 | tf_op jit(solution)/shard_map/pallas_call | solution.py:93
  119.7 3.3 %shard_map.66.refs_8_ = f32[1024,768]{1,0:T(8,128)S(1)} custom-call(s32[4]{0:T(128)S(1)} %copy-done.16, bf16[1024,4096]{1,0:T(8,128)(2,1)S(1)} %copy-done, bf16[1024,4096]{1,0:T(8,128)(2,1)S(1)} %copy-done, bf16[1024,4096]{1,0:T(8,128)(2,1)S(1)} %copy-done, bf16[1024,4096]{1,0:T(8,128)(2,1)S(1)} %copy-done, bf16[256,768]{1,0:T(8,128)(2,1)S(1)} %copy-done.3, ...), custom_call_target="tpu_custom_call" | custom-call | flops 1610612736 | bytes 8000000 | tf_op jit(solution)/shard_map/pallas_call | solution.py:93
  123.2 4.3 %shard_map.67.proj = bf16[1024,768]{1,0:T(8,128)(2,1)S(1)} custom-call(s32[4]{0:T(128)S(1)} %copy-done.15, bf16[1024,4096]{1,0:T(8,128)(2,1)S(1)} %copy-done, bf16[1024,4096]{1,0:T(8,128)(2,1)S(1)} %copy-done, bf16[1024,4096]{1,0:T(8,128)(2,1)S(1)} %copy-done, bf16[1024,4096]{1,0:T(8,128)(2,1)S(1)} %copy-done, bf16[256,768]{1,0:T(8,128)(2,1)S(1)} %copy-done.7, ...), custom_call_target="tpu_custom_call" | custom-call | flops 1610612736 | bytes 8000000 | tf_op jit(solution)/shard_map/pallas_call | solution.py:93
  127.7 3.2 %collective-permute-start.17 = (bf16[176,256]{1,0:T(8,128)(2,1)S(1)}, bf16[176,256]{1,0:T(8,128)(2,1)S(1)}, u32[]{:S(2)}, u32[]{:S(2)}) collective-permute-start(bf16[176,256]{1,0:T(8,128)(2,1)S(1)} %pad_maximum_fusion), channel_id=1, source_target_pairs={{0,8},{8,16},{16,24},{24,32},{32,40},{40,48},{48,56},{56,64},{64,7... | collective-permute-start | bytes 270344 | tf_op jit(solution)/shard_map/ppermute | solution.py:240
  131.0 6.6 %shard_map.71 = bf16[1024,256]{1,0:T(8,128)(2,1)} custom-call(s32[8]{0:T(128)S(1)} %copy-done.17, bf16[1024,768]{1,0:T(8,128)(2,1)S(1)} %shard_map.67.proj, bf16[176,256]{1,0:T(8,128)(2,1)S(1)} %collective-permute-done.18.halo, f32[9,256]{1,0:T(8,128)S(1)} %slice_convert_fusion.short, bf16[16,256,128]{2,1,0:T(8,128)(2,1)S(1)} %copy-done.21, ...), custom_call_target="tpu_custom_call" | custom-call | flops 10000000000 | bytes 4000000 | tf_op jit(solution)/shard_map/pallas_call | solution.py:172
  137.6 7.8 %all-to-all-start.1 = ((bf16[8,128,256]{2,1,0:T(8,128)(2,1)}), bf16[8,128,256]{2,1,0:T(8,128)(2,1)}, u32[]{:S(2)}, u32[]{:S(2)}) async-start(bf16[8,128,256]{2,1,0:T(8,128)(2,1)} %bitcast.35), calls=%async_computation.1 | async-start | bytes 1048576 | tf_op jit(solution)/shard_map/all_to_all | solution.py:244
  145.4 6.7 %shard_map.69 = bf16[1024,256]{1,0:T(8,128)(2,1)} custom-call(s32[8]{0:T(128)S(1)} %copy-done.17, bf16[1024,768]{1,0:T(8,128)(2,1)S(1)} %copy-done.9, bf16[176,256]{1,0:T(8,128)(2,1)S(1)} %collective-permute-done.17.halo, f32[9,256]{1,0:T(8,128)S(1)} %copy-done.12, bf16[16,256,128]{2,1,0:T(8,128)(2,1)S(1)} %copy-done.19, s32[1024,1]{1,0:T(8,128)S(1)} %copy-done.1, ...), custom_call_target="tpu_custom_call" | custom-call | flops 10000000000 | bytes 4000000 | tf_op jit(solution)/shard_map/pallas_call | solution.py:172
  152.1 2.9 %all-to-all-done.1 = bf16[8,128,256]{2,1,0:T(8,128)(2,1)} async-done(((bf16[8,128,256]{2,1,0:T(8,128)(2,1)}), bf16[8,128,256]{2,1,0:T(8,128)(2,1)}, u32[]{:S(2)}, u32[]{:S(2)}) %all-to-all-start.1) | async-done | bytes 524320 | tf_op jit(solution)/shard_map/all_to_all | solution.py:244
  155.0 4.3 %all-to-all-start = ((bf16[8,128,256]{2,1,0:T(8,128)(2,1)}), bf16[8,128,256]{2,1,0:T(8,128)(2,1)S(1)}, u32[]{:S(2)}, u32[]{:S(2)}) async-start(bf16[8,128,256]{2,1,0:T(8,128)(2,1)} %bitcast.28), calls=%async_computation | async-start | bytes 1048576 | tf_op jit(solution)/shard_map/all_to_all | solution.py:244
  159.2 9.5 %all-to-all-done = bf16[8,128,256]{2,1,0:T(8,128)(2,1)S(1)} async-done(((bf16[8,128,256]{2,1,0:T(8,128)(2,1)}), bf16[8,128,256]{2,1,0:T(8,128)(2,1)S(1)}, u32[]{:S(2)}, u32[]{:S(2)}) %all-to-all-start) | async-done | bytes 524320 | tf_op jit(solution)/shard_map/all_to_all | solution.py:244
  (160 shorter events, 23.5 us)
Async XLA Ops:
  6.5 85.5 %all-gather.2.cloned.1.call-start = ((), (), s32[]{:S(2)}) async-start(), calls=%async_computation.2 | async-start | bytes 9437184 | tf_op jit(solution)/shard_map/all_gather | solution.py:226
  9.7 23.2 %collective-permute-start = (bf16[256,768]{1,0:T(8,128)(2,1)S(1)}, bf16[256,768]{1,0:T(8,128)(2,1)S(1)}, u32[]{:S(2)}, u32[]{:S(2)}) collective-permute-start(bf16[256,768]{1,0:T(8,128)(2,1)S(1)} %copy.18), channel_id=1, source_target_pairs={{0,8},{8,0},{1,9},{9,1},{2,10},{10,2},{3,11},{11,3},{4,12},{12,4},... | collective-permute-start | bytes 1179656 | tf_op jit(solution)/shard_map/ppermute | solution.py:17
  17.6 15.4 %collective-permute-start.5 = (bf16[17,256]{1,0:T(8,128)(2,1)S(1)}, bf16[17,256]{1,0:T(8,128)(2,1)S(1)}, u32[]{:S(2)}, u32[]{:S(2)}) collective-permute-start(bf16[17,256]{1,0:T(8,128)(2,1)S(1)} %pad_maximum_fusion.2), channel_id=1, source_target_pairs={{0,8},{8,0},{1,9},{9,1},{2,10},{10,2},{3,11},{11,3},{4,12},{12,4},... | collective-permute-start | bytes 26120 | tf_op jit(solution)/shard_map/ppermute | solution.py:17
  33.0 10.3 %collective-permute-start.1 = (bf16[256,768]{1,0:T(8,128)(2,1)S(1)}, bf16[256,768]{1,0:T(8,128)(2,1)S(1)}, u32[]{:S(2)}, u32[]{:S(2)}) collective-permute-start(bf16[256,768]{1,0:T(8,128)(2,1)S(1)} %collective-permute-done.refs_4_), channel_id=1, source_target_pairs={{0,64},{64,128},{128,192},{192,0},{1,65},{65,129},{129,193},{193,1... | collective-permute-start | bytes 1179656 | tf_op jit(solution)/shard_map/ppermute | solution.py:22
  36.2 18.2 %collective-permute-start.2 = (bf16[256,768]{1,0:T(8,128)(2,1)S(1)}, bf16[256,768]{1,0:T(8,128)(2,1)S(1)}, u32[]{:S(2)}, u32[]{:S(2)}) collective-permute-start(bf16[256,768]{1,0:T(8,128)(2,1)S(1)} %collective-permute-done.refs_4_), channel_id=1, source_target_pairs={{0,192},{64,0},{128,64},{192,128},{1,193},{65,1},{129,65},{193,129... | collective-permute-start | bytes 1179656 | tf_op jit(solution)/shard_map/ppermute | solution.py:22
  36.3 21.0 %collective-permute-start.14 = (bf16[256,768]{1,0:T(8,128)(2,1)S(1)}, bf16[256,768]{1,0:T(8,128)(2,1)S(1)}, u32[]{:S(2)}, u32[]{:S(2)}) collective-permute-start(bf16[256,768]{1,0:T(8,128)(2,1)S(1)} %collective-permute-done.refs_4_), channel_id=1, source_target_pairs={{0,16},{16,32},{32,48},{48,0},{1,17},{17,33},{33,49},{49,1},{2,18}... | collective-permute-start | bytes 1179656 | tf_op jit(solution)/shard_map/ppermute | solution.py:22
  37.5 19.9 %collective-permute-start.15 = (bf16[256,768]{1,0:T(8,128)(2,1)S(1)}, bf16[256,768]{1,0:T(8,128)(2,1)S(1)}, u32[]{:S(2)}, u32[]{:S(2)}) collective-permute-start(bf16[256,768]{1,0:T(8,128)(2,1)S(1)} %collective-permute-done.refs_4_), channel_id=1, source_target_pairs={{0,48},{16,0},{32,16},{48,32},{1,49},{17,1},{33,17},{49,33},{2,50}... | collective-permute-start | bytes 1179656 | tf_op jit(solution)/shard_map/ppermute | solution.py:22
  54.4 11.5 %collective-permute-start.11 = (bf16[256,768]{1,0:T(8,128)(2,1)S(1)}, bf16[256,768]{1,0:T(8,128)(2,1)S(1)}, u32[]{:S(2)}, u32[]{:S(2)}) collective-permute-start(bf16[256,768]{1,0:T(8,128)(2,1)S(1)} %collective-permute-done.1.refs_4_), channel_id=1, source_target_pairs={{0,16},{16,32},{32,48},{48,0},{1,17},{17,33},{33,49},{49,1},{2,18}... | collective-permute-start | bytes 1179656 | tf_op jit(solution)/shard_map/ppermute | solution.py:22
  55.5 21.9 %collective-permute-start.12 = (bf16[256,768]{1,0:T(8,128)(2,1)S(1)}, bf16[256,768]{1,0:T(8,128)(2,1)S(1)}, u32[]{:S(2)}, u32[]{:S(2)}) collective-permute-start(bf16[256,768]{1,0:T(8,128)(2,1)S(1)} %collective-permute-done.1.refs_4_), channel_id=1, source_target_pairs={{0,48},{16,0},{32,16},{48,32},{1,49},{17,1},{33,17},{49,33},{2,50}... | collective-permute-start | bytes 1179656 | tf_op jit(solution)/shard_map/ppermute | solution.py:22
  57.1 20.4 %collective-permute-start.6 = (bf16[256,768]{1,0:T(8,128)(2,1)S(1)}, bf16[256,768]{1,0:T(8,128)(2,1)S(1)}, u32[]{:S(2)}, u32[]{:S(2)}) collective-permute-start(bf16[256,768]{1,0:T(8,128)(2,1)S(1)} %collective-permute-done.refs_4_), channel_id=1, source_target_pairs={{0,128},{64,192},{128,0},{192,64},{1,129},{65,193},{129,1},{193,65... | collective-permute-start | bytes 1179656 | tf_op jit(solution)/shard_map/ppermute | solution.py:22
  57.3 32.4 %copy-start.20 = (bf16[16,256,128]{2,1,0:T(8,128)(2,1)}, bf16[16,256,128]{2,1,0:T(8,128)(2,1)S(1)}, u32[]{:S(2)}) copy-start(bf16[16,256,128]{2,1,0:T(8,128)(2,1)S(1)} %shard_map.70.band) | copy-start | bytes 3145732
  57.3 23.6 %collective-permute-start.3 = (bf16[256,768]{1,0:T(8,128)(2,1)S(1)}, bf16[256,768]{1,0:T(8,128)(2,1)S(1)}, u32[]{:S(2)}, u32[]{:S(2)}) collective-permute-start(bf16[256,768]{1,0:T(8,128)(2,1)S(1)} %collective-permute-done.2.refs_4_), channel_id=1, source_target_pairs={{0,16},{16,32},{32,48},{48,0},{1,17},{17,33},{33,49},{49,1},{2,18}... | collective-permute-start | bytes 1179656 | tf_op jit(solution)/shard_map/ppermute | solution.py:22
  57.4 23.5 %collective-permute-start.4 = (bf16[256,768]{1,0:T(8,128)(2,1)S(1)}, bf16[256,768]{1,0:T(8,128)(2,1)S(1)}, u32[]{:S(2)}, u32[]{:S(2)}) collective-permute-start(bf16[256,768]{1,0:T(8,128)(2,1)S(1)} %collective-permute-done.2.refs_4_), channel_id=1, source_target_pairs={{0,48},{16,0},{32,16},{48,32},{1,49},{17,1},{33,17},{49,33},{2,50}... | collective-permute-start | bytes 1179656 | tf_op jit(solution)/shard_map/ppermute | solution.py:22
  65.8 45.2 %collective-permute-start.16 = (bf16[256,768]{1,0:T(8,128)(2,1)}, bf16[256,768]{1,0:T(8,128)(2,1)}, u32[]{:S(2)}, u32[]{:S(2)}) collective-permute-start(bf16[256,768]{1,0:T(8,128)(2,1)} %broadcast_select_fusion), channel_id=1, source_target_pairs={{0,16},{1,49},{16,32},{17,1},{32,48},{33,17},{48,0},{49,33},{2,18}... | collective-permute-start | bytes 1179656 | tf_op jit(solution)/shard_map/ppermute | solution.py:257
  77.5 11.5 %collective-permute-start.7 = (bf16[256,768]{1,0:T(8,128)(2,1)S(1)}, bf16[256,768]{1,0:T(8,128)(2,1)S(1)}, u32[]{:S(2)}, u32[]{:S(2)}) collective-permute-start(bf16[256,768]{1,0:T(8,128)(2,1)S(1)} %collective-permute-done.6.refs_4_), channel_id=1, source_target_pairs={{0,16},{16,32},{32,48},{48,0},{1,17},{17,33},{33,49},{49,1},{2,18}... | collective-permute-start | bytes 1179656 | tf_op jit(solution)/shard_map/ppermute | solution.py:22
  77.5 11.4 %collective-permute-start.8 = (bf16[256,768]{1,0:T(8,128)(2,1)S(1)}, bf16[256,768]{1,0:T(8,128)(2,1)S(1)}, u32[]{:S(2)}, u32[]{:S(2)}) collective-permute-start(bf16[256,768]{1,0:T(8,128)(2,1)S(1)} %collective-permute-done.6.refs_4_), channel_id=1, source_target_pairs={{0,48},{16,0},{32,16},{48,32},{1,49},{17,1},{33,17},{49,33},{2,50}... | collective-permute-start | bytes 1179656 | tf_op jit(solution)/shard_map/ppermute | solution.py:22
  80.9 34.4 %collective-permute-start.13 = (bf16[256,768]{1,0:T(8,128)(2,1)}, bf16[256,768]{1,0:T(8,128)(2,1)}, u32[]{:S(2)}, u32[]{:S(2)}) collective-permute-start(bf16[256,768]{1,0:T(8,128)(2,1)} %broadcast_select_fusion.1), channel_id=1, source_target_pairs={{0,16},{1,49},{16,32},{17,1},{32,48},{33,17},{48,0},{49,33},{2,18}... | collective-permute-start | bytes 1179656 | tf_op jit(solution)/shard_map/ppermute | solution.py:257
  89.7 33.4 %collective-permute-start.9 = (bf16[256,768]{1,0:T(8,128)(2,1)}, bf16[256,768]{1,0:T(8,128)(2,1)}, u32[]{:S(2)}, u32[]{:S(2)}) collective-permute-start(bf16[256,768]{1,0:T(8,128)(2,1)} %broadcast_select_fusion.2), channel_id=1, source_target_pairs={{0,16},{1,49},{16,32},{17,1},{32,48},{33,17},{48,0},{49,33},{2,18}... | collective-permute-start | bytes 1179656 | tf_op jit(solution)/shard_map/ppermute | solution.py:257
  92.1 18.9 %copy-start = (bf16[1024,4096]{1,0:T(8,128)(2,1)S(1)}, bf16[1024,4096]{1,0:T(8,128)(2,1)}, u32[]{:S(2)}) copy-start(bf16[1024,4096]{1,0:T(8,128)(2,1)} %all-gather.2.cloned.1.call-done.refs_0_.refs_1_.refs_2_.refs_3_) | copy-start | bytes 25165828
  103.3 16.4 %collective-permute-start.10 = (bf16[256,768]{1,0:T(8,128)(2,1)S(1)}, bf16[256,768]{1,0:T(8,128)(2,1)S(1)}, u32[]{:S(2)}, u32[]{:S(2)}) collective-permute-start(bf16[256,768]{1,0:T(8,128)(2,1)S(1)} %copy-done.24), channel_id=1, source_target_pairs={{0,16},{1,49},{16,32},{17,1},{32,48},{33,17},{48,0},{49,33},{2,18}... | collective-permute-start | bytes 1179656 | tf_op jit(solution)/shard_map/ppermute | solution.py:257
  103.7 27.2 %collective-permute-start.18 = (bf16[176,256]{1,0:T(8,128)(2,1)S(1)}, bf16[176,256]{1,0:T(8,128)(2,1)S(1)}, u32[]{:S(2)}, u32[]{:S(2)}) collective-permute-start(bf16[176,256]{1,0:T(8,128)(2,1)S(1)} %pad_maximum_fusion.1), channel_id=1, source_target_pairs={{0,8},{8,16},{16,24},{24,32},{32,40},{40,48},{48,56},{56,64},{64,7... | collective-permute-start | bytes 270344 | tf_op jit(solution)/shard_map/ppermute | solution.py:240
  127.7 17.7 %collective-permute-start.17 = (bf16[176,256]{1,0:T(8,128)(2,1)S(1)}, bf16[176,256]{1,0:T(8,128)(2,1)S(1)}, u32[]{:S(2)}, u32[]{:S(2)}) collective-permute-start(bf16[176,256]{1,0:T(8,128)(2,1)S(1)} %pad_maximum_fusion), channel_id=1, source_target_pairs={{0,8},{8,16},{16,24},{24,32},{32,40},{40,48},{48,56},{56,64},{64,7... | collective-permute-start | bytes 270344 | tf_op jit(solution)/shard_map/ppermute | solution.py:240
  137.6 17.4 %all-to-all-start.1 = ((bf16[8,128,256]{2,1,0:T(8,128)(2,1)}), bf16[8,128,256]{2,1,0:T(8,128)(2,1)}, u32[]{:S(2)}, u32[]{:S(2)}) async-start(bf16[8,128,256]{2,1,0:T(8,128)(2,1)} %bitcast.35), calls=%async_computation.1 | async-start | bytes 1048576 | tf_op jit(solution)/shard_map/all_to_all | solution.py:244
  155.0 13.8 %all-to-all-start = ((bf16[8,128,256]{2,1,0:T(8,128)(2,1)}), bf16[8,128,256]{2,1,0:T(8,128)(2,1)S(1)}, u32[]{:S(2)}, u32[]{:S(2)}) async-start(bf16[8,128,256]{2,1,0:T(8,128)(2,1)} %bitcast.28), calls=%async_computation | async-start | bytes 1048576 | tf_op jit(solution)/shard_map/all_to_all | solution.py:244
  (42 other events, 381.7 us)
Sparse Core Ops, SparseCore 0:
  9.7 56.5 all-gather.1

commit v4 on v3

--- a/solution.py
+++ b/solution.py
@@ -49,10 +49,35 @@
     )(long_filter.astype(jnp.float32))
 
 
-def spread_columns(piece):
-    up, down = shift(piece, "z_lo", 1), shift(piece, "z_lo", -1)
-    late, up, down = lax.optimization_barrier((piece, up, down))
-    return (0, piece), (1, up), (-1, down), (2, shift(late, "z_lo", 2))
+def across(value, by):
+    size = lax.axis_size("z_lo")
+    pairs = [(2 * i + h, 2 * ((i + by) % size) + 1 - h) for i in range(size) for h in range(2)]
+    return lax.ppermute(value, ("z_lo", "z_hi"), pairs)
+
+
+def ring(value, by):
+    size = lax.axis_size("z_lo")
+    pairs = []
+    for i in range(size):
+        for h in range(2):
+            to = (h * size + i + by) % (2 * size)
+            pairs.append((2 * i + h, 2 * (to % size) + to // size))
+    return lax.ppermute(value, ("z_lo", "z_hi"), pairs)
+
+
+def spread_columns(piece, ends):
+    z_lo = lax.axis_index("z_lo")
+    size = lax.axis_size("z_lo")
+    top, bottom = z_lo == size - 1, z_lo == 0
+    up = ring(jnp.where(top, ends[0], piece), 1)
+    down = ring(jnp.where(bottom, ends[0], piece), -1)
+    pairs = []
+    for h in range(2):
+        pairs += [(2 * 1 + h, 2 * 2 + h), (2 * 2 + h, 2 * 1 + h)]
+        pairs += [(2 * 0 + h, 2 * 3 + 1 - h), (2 * 3 + h, 2 * 0 + 1 - h)]
+    onward = jnp.where(jnp.logical_or(top, bottom), ends[1], jnp.where(z_lo == 1, up, down))
+    opposite = lax.ppermute(onward, ("z_lo", "z_hi"), pairs)
+    return (0, piece), (1, up), (-1, down), (2, opposite)
 
 
 def spread_rows(mine):
@@ -70,17 +95,18 @@
 def add_product_kernel(count, places, *refs):
     del places
     lefts, rights, rest = refs[:count], refs[count : 2 * count], refs[2 * count :]
-    total = rest[0][...] if len(rest) == 2 else None
-    for left, right in zip(lefts, rights):
-        term = jnp.dot(left[...], right[...], preferred_element_type=jnp.float32)
-        total = term if total is None else total + term
+    left = jnp.concatenate([ref[...] for ref in lefts], axis=1)
+    right = jnp.concatenate([ref[...] for ref in rights], axis=0)
+    total = jnp.dot(left, right, preferred_element_type=jnp.float32)
+    if len(rest) == 2:
+        total = total + rest[0][...]
     rest[-1][...] = total.astype(rest[-1].dtype)
 
 
 def add_product(left, pieces, places, total, dtype):
     length = left.shape[0]
     deep, wide = pieces[0].shape
-    rows = 256
+    rows = 512
     count = len(pieces)
     spec = pltpu.PrefetchScalarGridSpec(
         num_scalar_prefetch=1,
@@ -94,7 +120,7 @@
         functools.partial(add_product_kernel, count),
         out_shape=jax.ShapeDtypeStruct((length, wide), dtype),
         grid_spec=spec,
-        compiler_params=pltpu.CompilerParams(vmem_limit_bytes=24 << 20),
+        compiler_params=pltpu.CompilerParams(vmem_limit_bytes=40 << 20),
         cost_estimate=pl.CostEstimate(
             flops=2 * length * deep * wide * count, bytes_accessed=8_000_000, transcendentals=0
         ),
@@ -102,8 +128,9 @@
 
 
 def mix_conv_kernel(
-    flags, proj, halo, short, band, start_col, start_row, out, key_value_t, query, conv_t
+    flags, proj, halo, short, band, start_col, start_row, into, out, key_value_t, query, conv_t
 ):
+    del into
     length, channels = out.shape
     groups = band.shape[0]
     share = channels // groups
@@ -162,26 +189,38 @@
         out[rows, :] = (query[rows, :] * conv_t[:, b * SPAN : (b + 1) * SPAN].T).astype(out.dtype)
 
 
-def mix_conv(proj, halo, short, band, starts):
-    length = proj.shape[0]
-    channels = proj.shape[1] // 3
-    blocks = length // SPAN
+def mix_conv(proj, halo, short, band, starts, rows, into, side):
+    length, channels = proj.shape[0], proj.shape[1] // 3
+    blocks = rows // SPAN
+    starts = starts[:rows]
     last = starts.reshape(blocks, SPAN)[:, -1]
     flags = (last > jnp.arange(blocks, dtype=jnp.int32) * SPAN - (SPAN - 1)).astype(jnp.int32)
-    vmem = pl.BlockSpec(memory_space=pltpu.VMEM)
+    given = [flags, proj, halo, short, band, starts[:, None], starts[None, :]]
+    in_specs = [pl.BlockSpec(memory_space=pltpu.SMEM), pl.BlockSpec((rows, 3 * channels), lambda n: (0, 0))]
+    in_specs += [pl.BlockSpec(memory_space=pltpu.VMEM)] * 5
+    body = mix_conv_kernel
+    aliases = {}
+    if into is None:
+        body = lambda *refs: mix_conv_kernel(*refs[:7], None, *refs[7:])
+    else:
+        aliases = {len(given): 0}
+        given.append(into)
+        in_specs.append(pl.BlockSpec(memory_space=pl.ANY))
     return pl.pallas_call(
-        mix_conv_kernel,
-        out_shape=jax.ShapeDtypeStruct((length, channels), jnp.bfloat16),
-        in_specs=[pl.BlockSpec(memory_space=pltpu.SMEM)] + [vmem] * 6,
-        out_specs=vmem,
+        body,
+        out_shape=jax.ShapeDtypeStruct((length, 2 * channels), jnp.bfloat16),
+        grid=(1,),
+        in_specs=in_specs,
+        out_specs=pl.BlockSpec((rows, channels), lambda n: (0, side)),
         scratch_shapes=[
-            pltpu.VMEM((channels, length + SPAN), jnp.bfloat16),
-            pltpu.VMEM((length, channels), jnp.float32),
-            pltpu.VMEM((channels, length), jnp.float32),
+            pltpu.VMEM((channels, rows + SPAN), jnp.bfloat16),
+            pltpu.VMEM((rows, channels), jnp.float32),
+            pltpu.VMEM((channels, rows), jnp.float32),
         ],
+        input_output_aliases=aliases,
         compiler_params=pltpu.CompilerParams(vmem_limit_bytes=24 << 20),
-        cost_estimate=pl.CostEstimate(flops=10_000_000_000, bytes_accessed=4_000_000, transcendentals=0),
-    )(flags, proj, halo, short, band, starts[:, None], starts[None, :])
+        cost_estimate=pl.CostEstimate(flops=rows * 6_000_000, bytes_accessed=4_000_000, transcendentals=0),
+    )(*given)
 
 
 def tail_of(proj, short, starts):
@@ -215,9 +254,15 @@
     starts = starts - (context * lax.axis_size("z_hi") + z_hi) * length
 
     deep = width // contexts
-    piece = lax.dynamic_slice_in_dim(in_weight, context * deep, deep, 0).reshape(deep, 3 * channels)
-    piece, tokens = lax.optimization_barrier((piece, tokens))
-    piece = swap(piece, "z_hi")
+    depth = lax.axis_size("z_lo")
+
+    def cut(quarter):
+        first = (quarter * lax.axis_size("x") + x) * deep
+        return lax.dynamic_slice_in_dim(in_weight, first, deep, 0).reshape(deep, 3 * channels)
+
+    piece, tokens = lax.optimization_barrier((cut((z_lo + 2) % depth), tokens))
+    piece = across(piece, 2)
+    top = z_lo == depth - 1
 
     float_tokens = tokens.astype(jnp.float32)
     scale_rows = lax.rsqrt(jnp.mean(float_tokens * float_tokens, axis=-1, keepdims=True) + 1e-06)
@@ -226,7 +271,9 @@
     gathered = lax.all_gather(normed, ("y", "core"), axis=0, tiled=True)
     weight_t = in_weight.transpose(1, 2, 0).reshape(3 * channels, width)
     piece, weight_t = lax.optimization_barrier((piece, weight_t))
-    columns = spread_columns(piece)
+    ends = cut(jnp.where(top, depth - 1, 0)), cut(jnp.where(top, depth - 2, 1))
+    piece, *ends = lax.optimization_barrier((piece, *ends))
+    columns = spread_columns(piece, ends)
 
     small = jnp.concatenate(
         [short_filter.reshape(3 * taps, channels), long_filter.reshape(-1, channels)], axis=0
@@ -238,10 +285,6 @@
 
     def halo_of(projected, short):
         return lax.ppermute(tail_of(projected, short, starts), ("z_lo", "x", "z_hi"), next_half)
-
-    def finish(projected, halo, short, long):
-        gated = mix_conv(projected, halo, short, banded(long), starts)
-        return lax.all_to_all(gated, ("y", "core"), split_axis=0, concat_axis=1, tiled=True)
 
     own_short = short_filter.reshape(3 * taps, channels).astype(jnp.float32)
     other_short = other_short.astype(jnp.float32)
@@ -249,23 +292,27 @@
         gathered, weight_t, (((1,), (1,)), ((), ())), preferred_element_type=jnp.float32
     ).astype(jnp.bfloat16)
     rows_of = [spread_rows(mine) for _, mine in columns]
-    other_projected = None
-    for n, ((by, mine), (below, above, onward)) in enumerate(zip(columns, rows_of)):
-        last = n == len(columns) - 1
-        if n == len(columns) - 2:
-            onward, own_projected = lax.optimization_barrier((onward, own_projected))
-        far = lax.ppermute(onward, ("x", "core"), fan("x"))
-        other_projected = add_product(
-            gathered,
-            [mine, below, above, far],
-            places_of(by),
-            other_projected,
-            jnp.bfloat16 if last else jnp.float32,
-        )
+    onwards = [onward for _, _, onward in rows_of]
+    onwards[1], onwards[2], own_projected = lax.optimization_barrier((onwards[1], onwards[2], own_projected))
+    pieces, places = [], []
+    for (by, mine), (below, above, _), onward in zip(columns, rows_of, onwards):
+        pieces += [mine, below, above, lax.ppermute(onward, ("x", "core"), fan("x"))]
+        places += places_of(by)
+    half = len(pieces) // 2
+    first_sum = add_product(gathered, pieces[:half], places[:half], None, jnp.float32)
+    first_sum, own_projected = lax.optimization_barrier((first_sum, own_projected))
     other_halo = halo_of(own_projected, own_short)
+    own_band, other_band = banded(long_filter), banded(other_long)
+    nothing = jnp.zeros((SPAN + 3 * RIM, channels), jnp.bfloat16)
+    gated = mix_conv(own_projected, nothing, own_short, own_band, starts, length, None, 0)
+    first_sum, gated = lax.optimization_barrier((first_sum, gated))
+    other_projected = add_product(gathered, pieces[half:], places[half:], first_sum, jnp.bfloat16)
     own_halo = halo_of(other_projected, other_short)
-    own = finish(own_projected, own_halo, own_short, long_filter)
-    other = finish(other_projected, other_halo, other_short, other_long)
+    gated = mix_conv(other_projected, other_halo, other_short, other_band, starts, length, gated, 1)
+    gated = mix_conv(own_projected, own_halo, own_short, own_band, starts, 2 * SPAN, gated, 0)
+    returned = lax.all_to_all(gated, ("y", "core"), split_axis=0, concat_axis=1, tiled=True)
+    returned = returned.reshape(rows, -1, 2, channels)
+    own, other = returned[:, :, 0].reshape(rows, -1), returned[:, :, 1].reshape(rows, -1)
     left = jnp.where(z_hi == 0, own, other)
     right = jnp.where(z_hi == 0, other, own)
     gated = jnp.concatenate([left, right], axis=1)

time: 178 us -> 166 us (0.933)
  waiting for transfers between devices: 49.7 us -> 30.8 us
  local copies, waits for them, and re-layouts: 13.1 us -> 21.8 us
  Pallas kernels: 29.9 us -> 33.5 us
  other arithmetic: 11.8 us -> 9.17 us
  starting transfers between devices: 48.2 us -> 46.1 us
    ppermute x11 -> x8, waiting for transfers between devices: 37.3 us -> 6.34 us  [shift(): lax.ppermute(value, axis, [(i, (i + by) % size) for i in range(size)])]
    ppermute x4 -> x8, starting transfers between devices: 3.69 us -> 16.2 us  [the longest x1 6.94 us: across(): return lax.ppermute(value, ('z_lo', 'z_hi'), pairs)]
    ppermute x4 -> x8, waiting for transfers between devices: 0.01 us -> 9.29 us  [the longest x2 6.93 us: ring(): return lax.ppermute(value, ('z_lo', 'z_hi'), pairs)]
    pallas_call x2 -> x3, Pallas kernels: 13.3 us -> 20.5 us  [mix_conv(): pl.pallas_call(body, out_shape=jax.ShapeDtypeStruct((length, 2 * channels...]
    ppermute x2 -> x1, starting transfers between devices: 7.94 us -> 1 us  [swap(): return lax.ppermute(value, axis, [(0, 1), (1, 0)])]
    ppermute x2, starting transfers between devices: 10.5 us -> 5.31 us  [halo_of(): lax.ppermute(tail_of(projected, short, starts), ('z_lo', 'x', 'z_hi'), ne...]
    pallas_call x4 -> x2, Pallas kernels: 16.1 us -> 12.6 us  [add_product(): pl.pallas_call(functools.partial(add_product_kernel, count), out_shape=ja...]
    ppermute x11 -> x8, starting transfers between devices: 14.1 us -> 10.7 us  [shift(): lax.ppermute(value, axis, [(i, (i + by) % size) for i in range(size)])]
  transfers between devices with their start and end apart: 22 -> 21, of which waited for: 7 -> 6; matrix products, arithmetic and copies ran while one was open for 17% -> 19% of each run, Pallas kernels for 17% -> 18%
where the time goes in v4:
time: 166 us; the launch traced here: 167 us
  starting transfers between devices  46.1 us (28%)
  Pallas kernels  33.5 us (20%)
  waiting for transfers between devices  30.8 us (19%)
  local copies, waits for them, and re-layouts  21.8 us (13%)
  between operations  14.2 us (9%)
  matrix products  11 us (7%)
  other arithmetic  9.17 us (6%)
    pallas_call x3, Pallas kernels, mix_conv(): pl.pallas_call(body, out_shape=jax.ShapeDtypeStruct((length, 2 * channels...  20.5 us
    all_to_all x1, waiting for transfers between devices, per_device(): lax.all_to_all(gated, ('y', 'core'), split_axis=0, concat_axis=1, tiled=T...  15.1 us
    all_to_all x1, starting transfers between devices, per_device(): lax.all_to_all(gated, ('y', 'core'), split_axis=0, concat_axis=1, tiled=T...  12.9 us
    pallas_call x2, Pallas kernels, add_product(): pl.pallas_call(functools.partial(add_product_kernel, count), out_shape=ja...  12.6 us
    dot_general x1, matrix products, per_device(): lax.dot_general(gathered, weight_t, (((1,), (1,)), ((), ())), preferred_e...  11 us
    ppermute x8, starting transfers between devices, shift(): lax.ppermute(value, axis, [(i, (i + by) % size) for i in range(size)])  10.7 us
    optimization_barrier x1, local copies, waits for them, and re-layouts, per_device(): in_weight, normed = lax.optimization_barrier((in_weight, normed))  8.75 us
    ppermute x1, starting transfers between devices, across(): return lax.ppermute(value, ('z_lo', 'z_hi'), pairs)  6.94 us
  transfers between devices with their start and end apart: 21, of which 6 were waited for; matrix products, arithmetic and copies ran while one was open for 19% of the time, Pallas kernels for 18%

profile of v4, /device:TPU:1, one launch (start us, length us, event | category | flops | bytes accessed | tf_op | source)
XLA Modules:
  0.0 166.5 jit_solution(11149133513327388469)
XLA Ops:
  9.7 6.9 %collective-permute-start = (bf16[256,768]{1,0:T(8,128)(2,1)S(1)}, bf16[256,768]{1,0:T(8,128)(2,1)S(1)}, u32[]{:S(2)}, u32[]{:S(2)}) collective-permute-start(bf16[256,768]{1,0:T(8,128)(2,1)S(1)} %copy.28), channel_id=1, source_target_pairs={{0,136},{8,128},{64,200},{72,192},{128,8},{136,0},{192,72},{200,64... | collective-permute-start | bytes 1179656 | tf_op jit(solution)/shard_map/ppermute | solution.py:55
  18.3 8.8 %copy.29 = bf16[4096,3,256]{0,2,1:T(8,128)(2,1)} copy(bf16[4096,3,256]{2,0,1:T(8,128)(2,1)} %param.8) | data formatting | bytes 12582912 | tf_op jit(solution)/shard_map/optimization_barrier | solution.py:270
  35.6 3.2 %collective-permute-start.7 = (bf16[256,768]{1,0:T(8,128)(2,1)S(1)}, bf16[256,768]{1,0:T(8,128)(2,1)S(1)}, u32[]{:S(2)}, u32[]{:S(2)}) collective-permute-start(bf16[256,768]{1,0:T(8,128)(2,1)S(1)} %get-tuple-element.49), channel_id=1, source_target_pairs={{0,200},{8,192},{64,0},{72,8},{128,64},{136,72},{192,128},{200,136... | collective-permute-start | bytes 1179656 | tf_op jit(solution)/shard_map/ppermute | solution.py:65
  42.2 3.7 %collective-permute-done.7.refs_8_ = bf16[256,768]{1,0:T(8,128)(2,1)S(1)} collective-permute-done((bf16[256,768]{1,0:T(8,128)(2,1)S(1)}, bf16[256,768]{1,0:T(8,128)(2,1)S(1)}, u32[]{:S(2)}, u32[]{:S(2)}) %collective-permute-start.7) | collective-permute-done | bytes 393248 | tf_op jit(solution)/shard_map/ppermute | solution.py:65
  45.9 3.2 %collective-permute-done.4.refs_12_ = bf16[256,768]{1,0:T(8,128)(2,1)S(1)} collective-permute-done((bf16[256,768]{1,0:T(8,128)(2,1)S(1)}, bf16[256,768]{1,0:T(8,128)(2,1)S(1)}, u32[]{:S(2)}, u32[]{:S(2)}) %collective-permute-start.4) | collective-permute-done | bytes 393248 | tf_op jit(solution)/shard_map/ppermute | solution.py:65
  50.8 1.5 collective-permute-start.9
  53.0 2.7 %collective-permute-start.6 = (bf16[256,768]{1,0:T(8,128)(2,1)S(1)}, bf16[256,768]{1,0:T(8,128)(2,1)S(1)}, u32[]{:S(2)}, u32[]{:S(2)}) collective-permute-start(bf16[256,768]{1,0:T(8,128)(2,1)S(1)} %collective-permute-done.4.refs_12_), channel_id=1, source_target_pairs={{0,48},{16,0},{32,16},{48,32},{1,49},{17,1},{33,17},{49,33},{2,50}... | collective-permute-start | bytes 1179656 | tf_op jit(solution)/shard_map/ppermute | solution.py:22
  56.5 2.7 %collective-permute-done.8.refs_9_ = bf16[256,768]{1,0:T(8,128)(2,1)S(1)} collective-permute-done((bf16[256,768]{1,0:T(8,128)(2,1)S(1)}, bf16[256,768]{1,0:T(8,128)(2,1)S(1)}, u32[]{:S(2)}, u32[]{:S(2)}) %collective-permute-start.8) | collective-permute-done | bytes 393248 | tf_op jit(solution)/shard_map/ppermute | solution.py:22
  60.7 2.5 %collective-permute-start.15 = (bf16[256,768]{1,0:T(8,128)(2,1)}, bf16[256,768]{1,0:T(8,128)(2,1)S(1)}, u32[]{:S(2)}, u32[]{:S(2)}) collective-permute-start(bf16[256,768]{1,0:T(8,128)(2,1)} %collective-permute-done.13.refs_12_), channel_id=1, source_target_pairs={{0,48},{16,0},{32,16},{48,32},{1,49},{17,1},{33,17},{49,33},{2,50}... | collective-permute-start | bytes 1179656 | tf_op jit(solution)/shard_map/ppermute | solution.py:22
  63.9 3.6 %collective-permute-done.5.refs_13_ = bf16[256,768]{1,0:T(8,128)(2,1)S(1)} collective-permute-done((bf16[256,768]{1,0:T(8,128)(2,1)S(1)}, bf16[256,768]{1,0:T(8,128)(2,1)S(1)}, u32[]{:S(2)}, u32[]{:S(2)}) %collective-permute-start.5) | collective-permute-done | bytes 393248 | tf_op jit(solution)/shard_map/ppermute | solution.py:22
  69.8 11.0 %convolution_convert_fusion.refs_1_.proj = bf16[1024,768]{1,0:T(8,128)(2,1)S(1)} fusion(bf16[1024,4096]{1,0:T(8,128)(2,1)} %all-gather.2.cloned.1.call-done.refs_0_.refs_1_.refs_2_.refs_3_.refs_4_.refs_5_.refs_6_.refs_7_, bf16[768,4096]{1,0:T(8,128)(2,1)} %bitcast.61), kind=kOutput, calls=%fused_computation.7 | convolution fusion | flops 6443237376 | bytes 16252928 | tf_op jit(solution)/shard_map/dot_general | solution.py:291
  80.9 2.5 %collective-permute-start.10 = (bf16[256,768]{1,0:T(8,128)(2,1)S(1)}, bf16[256,768]{1,0:T(8,128)(2,1)S(1)}, u32[]{:S(2)}, u32[]{:S(2)}) collective-permute-start(bf16[256,768]{1,0:T(8,128)(2,1)S(1)} %copy-done.21), channel_id=1, source_target_pairs={{0,16},{1,49},{16,32},{17,1},{32,48},{33,17},{48,0},{49,33},{2,18}... | collective-permute-start | bytes 1179656 | tf_op jit(solution)/shard_map/ppermute | solution.py:299
  83.8 1.8 %collective-permute-start.16 = (bf16[256,768]{1,0:T(8,128)(2,1)S(1)}, bf16[256,768]{1,0:T(8,128)(2,1)S(1)}, u32[]{:S(2)}, u32[]{:S(2)}) collective-permute-start(bf16[256,768]{1,0:T(8,128)(2,1)S(1)} %broadcast_select_fusion.4), channel_id=1, source_target_pairs={{0,16},{1,49},{16,32},{17,1},{32,48},{33,17},{48,0},{49,33},{2,18}... | collective-permute-start | bytes 1179656 | tf_op jit(solution)/shard_map/ppermute | solution.py:299
  85.8 2.3 %collective-permute-done.10.refs_15_ = bf16[256,768]{1,0:T(8,128)(2,1)S(1)} collective-permute-done((bf16[256,768]{1,0:T(8,128)(2,1)S(1)}, bf16[256,768]{1,0:T(8,128)(2,1)S(1)}, u32[]{:S(2)}, u32[]{:S(2)}) %collective-permute-start.10) | collective-permute-done | bytes 393248 | tf_op jit(solution)/shard_map/ppermute | solution.py:299
  88.1 6.3 %shard_map.64.refs_16_ = f32[1024,768]{1,0:T(8,128)S(1)} custom-call(s32[8]{0:T(128)S(1)} %copy-done.13, bf16[1024,4096]{1,0:T(8,128)(2,1)} %all-gather.2.cloned.1.call-done.refs_0_.refs_1_.refs_2_.refs_3_.refs_4_.refs_5_.refs_6_.refs_7_, bf16[1024,4096]{1,0:T(8,128)(2,1)} %all-gather.2.cloned.1.call-done.refs_0_.refs_1_.refs_2_.refs_3_.refs_4_.refs_5_.refs_6_.refs_7_, ...), custom_call_target="tpu_custom_call" | custom-call | flops 3221225472 | bytes 8000000 | tf_op jit(solution)/shard_map/pallas_call | solution.py:119
  94.7 3.8 %collective-permute-start.18 = (bf16[176,256]{1,0:T(8,128)(2,1)S(1)}, bf16[176,256]{1,0:T(8,128)(2,1)S(1)}, u32[]{:S(2)}, u32[]{:S(2)}) collective-permute-start(bf16[176,256]{1,0:T(8,128)(2,1)S(1)} %pad_maximum_fusion.1), channel_id=1, source_target_pairs={{0,8},{8,16},{16,24},{24,32},{32,40},{40,48},{48,56},{56,64},{64,7... | collective-permute-start | bytes 270344 | tf_op jit(solution)/shard_map/ppermute | solution.py:287
  98.6 8.6 %shard_map.66.into = bf16[1024,512]{1,0:T(8,128)(2,1)} custom-call(s32[8]{0:T(128)S(1)} %copy-done.15, bf16[1024,768]{1,0:T(8,128)(2,1)S(1)} %convolution_convert_fusion.refs_1_.proj, bf16[176,256]{1,0:T(8,128)(2,1)S(1)} %broadcast_in_dim.92.refs_2_, f32[9,256]{1,0:T(8,128)S(1)} %copy-done.8, bf16[16,256,128]{2,1,0:T(8,128)(2,1)S(1)} %copy-done.17, ...), custom_call_target="tpu_custom_call" | custom-call | flops 6144000000 | bytes 4000000 | tf_op jit(solution)/shard_map/pallas_call | solution.py:209
  107.2 6.3 %shard_map.67.proj = bf16[1024,768]{1,0:T(8,128)(2,1)S(1)} custom-call(s32[8]{0:T(128)S(1)} %copy-done.12, bf16[1024,4096]{1,0:T(8,128)(2,1)} %all-gather.2.cloned.1.call-done.refs_0_.refs_1_.refs_2_.refs_3_.refs_4_.refs_5_.refs_6_.refs_7_, bf16[1024,4096]{1,0:T(8,128)(2,1)} %all-gather.2.cloned.1.call-done.refs_0_.refs_1_.refs_2_.refs_3_.refs_4_.refs_5_.refs_6_.refs_7_, ...), custom_call_target="tpu_custom_call" | custom-call | flops 3221225472 | bytes 8000000 | tf_op jit(solution)/shard_map/pallas_call | solution.py:119
  113.8 1.6 collective-permute-start.17
  115.4 8.5 %shard_map.69.into = bf16[1024,512]{1,0:T(8,128)(2,1)} custom-call(s32[8]{0:T(128)S(1)} %copy-done.15, bf16[1024,768]{1,0:T(8,128)(2,1)S(1)} %shard_map.67.proj, bf16[176,256]{1,0:T(8,128)(2,1)S(1)} %collective-permute-done.18.halo, f32[9,256]{1,0:T(8,128)S(1)} %slice_convert_fusion.short, ...), custom_call_target="tpu_custom_call", output_to_operand_aliasing={{}: (7, {})} | custom-call | flops 6144000000 | bytes 4000000 | tf_op jit(solution)/shard_map/pallas_call | solution.py:209
  124.0 3.4 %shard_map.70 = bf16[1024,512]{1,0:T(8,128)(2,1)} custom-call(s32[2]{0:T(128)S(1)} %copy-done.14, bf16[1024,768]{1,0:T(8,128)(2,1)S(1)} %convolution_convert_fusion.refs_1_.proj, bf16[176,256]{1,0:T(8,128)(2,1)S(1)} %collective-permute-done.17.halo, f32[9,256]{1,0:T(8,128)S(1)} %copy-done.8, ...), custom_call_target="tpu_custom_call", output_to_operand_aliasing={{}: (7, {})} | custom-call | flops 1536000000 | bytes 4000000 | tf_op jit(solution)/shard_map/pallas_call | solution.py:209
  127.3 12.9 %all-to-all-start = ((bf16[8,128,512]{2,1,0:T(8,128)(2,1)}), bf16[8,128,512]{2,1,0:T(8,128)(2,1)S(1)}, u32[]{:S(2)}, u32[]{:S(2)}) async-start(bf16[8,128,512]{2,1,0:T(8,128)(2,1)} %bitcast.39), calls=%async_computation | async-start | bytes 2097152 | tf_op jit(solution)/shard_map/all_to_all | solution.py:313
  140.2 15.1 %all-to-all-done = bf16[8,128,512]{2,1,0:T(8,128)(2,1)S(1)} async-done(((bf16[8,128,512]{2,1,0:T(8,128)(2,1)}), bf16[8,128,512]{2,1,0:T(8,128)(2,1)S(1)}, u32[]{:S(2)}, u32[]{:S(2)}) %all-to-all-start) | async-done | bytes 1048608 | tf_op jit(solution)/shard_map/all_to_all | solution.py:313
  155.6 1.5 fusion.6
  (161 shorter events, 28.1 us)
Async XLA Ops:
  6.5 63.3 %all-gather.2.cloned.1.call-start = ((), (), s32[]{:S(2)}) async-start(), calls=%async_computation.1 | async-start | bytes 9437184 | tf_op jit(solution)/shard_map/all_gather | solution.py:271
  9.7 25.6 %collective-permute-start = (bf16[256,768]{1,0:T(8,128)(2,1)S(1)}, bf16[256,768]{1,0:T(8,128)(2,1)S(1)}, u32[]{:S(2)}, u32[]{:S(2)}) collective-permute-start(bf16[256,768]{1,0:T(8,128)(2,1)S(1)} %copy.28), channel_id=1, source_target_pairs={{0,136},{8,128},{64,200},{72,192},{128,8},{136,0},{192,72},{200,64... | collective-permute-start | bytes 1179656 | tf_op jit(solution)/shard_map/ppermute | solution.py:55
  16.7 22.1 %collective-permute-start.11 = (bf16[17,256]{1,0:T(8,128)(2,1)S(1)}, bf16[17,256]{1,0:T(8,128)(2,1)S(1)}, u32[]{:S(2)}, u32[]{:S(2)}) collective-permute-start(bf16[17,256]{1,0:T(8,128)(2,1)S(1)} %pad_maximum_fusion.2), channel_id=1, source_target_pairs={{0,8},{8,0},{1,9},{9,1},{2,10},{10,2},{3,11},{11,3},{4,12},{12,4},... | collective-permute-start | bytes 26120 | tf_op jit(solution)/shard_map/ppermute | solution.py:17
  35.6 10.3 %collective-permute-start.7 = (bf16[256,768]{1,0:T(8,128)(2,1)S(1)}, bf16[256,768]{1,0:T(8,128)(2,1)S(1)}, u32[]{:S(2)}, u32[]{:S(2)}) collective-permute-start(bf16[256,768]{1,0:T(8,128)(2,1)S(1)} %get-tuple-element.49), channel_id=1, source_target_pairs={{0,200},{8,192},{64,0},{72,8},{128,64},{136,72},{192,128},{200,136... | collective-permute-start | bytes 1179656 | tf_op jit(solution)/shard_map/ppermute | solution.py:65
  38.8 10.4 %collective-permute-start.4 = (bf16[256,768]{1,0:T(8,128)(2,1)S(1)}, bf16[256,768]{1,0:T(8,128)(2,1)S(1)}, u32[]{:S(2)}, u32[]{:S(2)}) collective-permute-start(bf16[256,768]{1,0:T(8,128)(2,1)S(1)} %get-tuple-element.50), channel_id=1, source_target_pairs={{0,64},{8,72},{64,128},{72,136},{128,192},{136,200},{192,8},{200,0... | collective-permute-start | bytes 1179656 | tf_op jit(solution)/shard_map/ppermute | solution.py:65
  39.4 13.5 %collective-permute-start.1 = (bf16[256,768]{1,0:T(8,128)(2,1)S(1)}, bf16[256,768]{1,0:T(8,128)(2,1)S(1)}, u32[]{:S(2)}, u32[]{:S(2)}) collective-permute-start(bf16[256,768]{1,0:T(8,128)(2,1)S(1)} %collective-permute-done.refs_8_), channel_id=1, source_target_pairs={{0,16},{16,32},{32,48},{48,0},{1,17},{17,33},{33,49},{49,1},{2,18}... | collective-permute-start | bytes 1179656 | tf_op jit(solution)/shard_map/ppermute | solution.py:22
  40.6 12.3 %collective-permute-start.2 = (bf16[256,768]{1,0:T(8,128)(2,1)S(1)}, bf16[256,768]{1,0:T(8,128)(2,1)S(1)}, u32[]{:S(2)}, u32[]{:S(2)}) collective-permute-start(bf16[256,768]{1,0:T(8,128)(2,1)S(1)} %collective-permute-done.refs_8_), channel_id=1, source_target_pairs={{0,48},{16,0},{32,16},{48,32},{1,49},{17,1},{33,17},{49,33},{2,50}... | collective-permute-start | bytes 1179656 | tf_op jit(solution)/shard_map/ppermute | solution.py:22
  49.2 11.2 %collective-permute-start.13 = (bf16[256,768]{1,0:T(8,128)(2,1)S(1)}, bf16[256,768]{1,0:T(8,128)(2,1)}, u32[]{:S(2)}, u32[]{:S(2)}) collective-permute-start(bf16[256,768]{1,0:T(8,128)(2,1)S(1)} %select_select_fusion), channel_id=1, source_target_pairs={{64,128},{128,64},{0,200},{192,8},{72,136},{136,72},{8,192},{200,0... | collective-permute-start | bytes 1179656 | tf_op jit(solution)/shard_map/ppermute | solution.py:79
  49.6 9.6 %collective-permute-start.8 = (bf16[256,768]{1,0:T(8,128)(2,1)S(1)}, bf16[256,768]{1,0:T(8,128)(2,1)S(1)}, u32[]{:S(2)}, u32[]{:S(2)}) collective-permute-start(bf16[256,768]{1,0:T(8,128)(2,1)S(1)} %collective-permute-done.7.refs_8_), channel_id=1, source_target_pairs={{0,16},{16,32},{32,48},{48,0},{1,17},{17,33},{33,49},{49,1},{2,18}... | collective-permute-start | bytes 1179656 | tf_op jit(solution)/shard_map/ppermute | solution.py:22
  50.8 9.8 %collective-permute-start.9 = (bf16[256,768]{1,0:T(8,128)(2,1)S(1)}, bf16[256,768]{1,0:T(8,128)(2,1)S(1)}, u32[]{:S(2)}, u32[]{:S(2)}) collective-permute-start(bf16[256,768]{1,0:T(8,128)(2,1)S(1)} %collective-permute-done.7.refs_8_), channel_id=1, source_target_pairs={{0,48},{16,0},{32,16},{48,32},{1,49},{17,1},{33,17},{49,33},{2,50}... | collective-permute-start | bytes 1179656 | tf_op jit(solution)/shard_map/ppermute | solution.py:22
  52.9 14.6 %collective-permute-start.5 = (bf16[256,768]{1,0:T(8,128)(2,1)S(1)}, bf16[256,768]{1,0:T(8,128)(2,1)S(1)}, u32[]{:S(2)}, u32[]{:S(2)}) collective-permute-start(bf16[256,768]{1,0:T(8,128)(2,1)S(1)} %collective-permute-done.4.refs_12_), channel_id=1, source_target_pairs={{0,16},{16,32},{32,48},{48,0},{1,17},{17,33},{33,49},{49,1},{2,18}... | collective-permute-start | bytes 1179656 | tf_op jit(solution)/shard_map/ppermute | solution.py:22
  53.0 14.5 %collective-permute-start.6 = (bf16[256,768]{1,0:T(8,128)(2,1)S(1)}, bf16[256,768]{1,0:T(8,128)(2,1)S(1)}, u32[]{:S(2)}, u32[]{:S(2)}) collective-permute-start(bf16[256,768]{1,0:T(8,128)(2,1)S(1)} %collective-permute-done.4.refs_12_), channel_id=1, source_target_pairs={{0,48},{16,0},{32,16},{48,32},{1,49},{17,1},{33,17},{49,33},{2,50}... | collective-permute-start | bytes 1179656 | tf_op jit(solution)/shard_map/ppermute | solution.py:22
  59.2 26.6 %collective-permute-start.3 = (bf16[256,768]{1,0:T(8,128)(2,1)}, bf16[256,768]{1,0:T(8,128)(2,1)}, u32[]{:S(2)}, u32[]{:S(2)}) collective-permute-start(bf16[256,768]{1,0:T(8,128)(2,1)} %broadcast_select_fusion.7), channel_id=1, source_target_pairs={{0,16},{1,49},{16,32},{17,1},{32,48},{33,17},{48,0},{49,33},{2,18}... | collective-permute-start | bytes 1179656 | tf_op jit(solution)/shard_map/ppermute | solution.py:299
  60.5 23.2 %collective-permute-start.14 = (bf16[256,768]{1,0:T(8,128)(2,1)}, bf16[256,768]{1,0:T(8,128)(2,1)S(1)}, u32[]{:S(2)}, u32[]{:S(2)}) collective-permute-start(bf16[256,768]{1,0:T(8,128)(2,1)} %collective-permute-done.13.refs_12_), channel_id=1, source_target_pairs={{0,16},{16,32},{32,48},{48,0},{1,17},{17,33},{33,49},{49,1},{2,18}... | collective-permute-start | bytes 1179656 | tf_op jit(solution)/shard_map/ppermute | solution.py:22
  60.7 23.0 %collective-permute-start.15 = (bf16[256,768]{1,0:T(8,128)(2,1)}, bf16[256,768]{1,0:T(8,128)(2,1)S(1)}, u32[]{:S(2)}, u32[]{:S(2)}) collective-permute-start(bf16[256,768]{1,0:T(8,128)(2,1)} %collective-permute-done.13.refs_12_), channel_id=1, source_target_pairs={{0,48},{16,0},{32,16},{48,32},{1,49},{17,1},{33,17},{49,33},{2,50}... | collective-permute-start | bytes 1179656 | tf_op jit(solution)/shard_map/ppermute | solution.py:22
  80.9 7.2 %collective-permute-start.10 = (bf16[256,768]{1,0:T(8,128)(2,1)S(1)}, bf16[256,768]{1,0:T(8,128)(2,1)S(1)}, u32[]{:S(2)}, u32[]{:S(2)}) collective-permute-start(bf16[256,768]{1,0:T(8,128)(2,1)S(1)} %copy-done.21), channel_id=1, source_target_pairs={{0,16},{1,49},{16,32},{17,1},{32,48},{33,17},{48,0},{49,33},{2,18}... | collective-permute-start | bytes 1179656 | tf_op jit(solution)/shard_map/ppermute | solution.py:299
  83.8 14.7 %copy-start.4 = (s32[1024,1]{1,0:T(8,128)S(1)}, s32[1024,1]{1,0:T(8,128)}, u32[]{:S(2)}) copy-start(s32[1024,1]{1,0:T(8,128)} %copy.35.refs_5_.start_col) | copy-start | bytes 12292
  83.8 14.7 %copy-start.7 = (s32[1024]{0:T(1024)S(1)}, s32[1024]{0:T(1024)}, u32[]{:S(2)}) copy-start(s32[1024]{0:T(1024)} %copy-done.6) | copy-start | bytes 12292
  83.8 14.7 %copy-start.8 = (f32[9,256]{1,0:T(8,128)S(1)}, f32[9,256]{1,0:T(8,128)}, u32[]{:S(2)}) copy-start(f32[9,256]{1,0:T(8,128)} %convert_element_type.88.refs_3_.short) | copy-start | bytes 27652
  83.8 23.3 %collective-permute-start.16 = (bf16[256,768]{1,0:T(8,128)(2,1)S(1)}, bf16[256,768]{1,0:T(8,128)(2,1)S(1)}, u32[]{:S(2)}, u32[]{:S(2)}) collective-permute-start(bf16[256,768]{1,0:T(8,128)(2,1)S(1)} %broadcast_select_fusion.4), channel_id=1, source_target_pairs={{0,16},{1,49},{16,32},{17,1},{32,48},{33,17},{48,0},{49,33},{2,18}... | collective-permute-start | bytes 1179656 | tf_op jit(solution)/shard_map/ppermute | solution.py:299
  85.7 21.5 %collective-permute-start.12 = (bf16[256,768]{1,0:T(8,128)(2,1)S(1)}, bf16[256,768]{1,0:T(8,128)(2,1)S(1)}, u32[]{:S(2)}, u32[]{:S(2)}) collective-permute-start(bf16[256,768]{1,0:T(8,128)(2,1)S(1)} %copy-done.20), channel_id=1, source_target_pairs={{0,16},{1,49},{16,32},{17,1},{32,48},{33,17},{48,0},{49,33},{2,18}... | collective-permute-start | bytes 1179656 | tf_op jit(solution)/shard_map/ppermute | solution.py:299
  94.7 20.7 %collective-permute-start.18 = (bf16[176,256]{1,0:T(8,128)(2,1)S(1)}, bf16[176,256]{1,0:T(8,128)(2,1)S(1)}, u32[]{:S(2)}, u32[]{:S(2)}) collective-permute-start(bf16[176,256]{1,0:T(8,128)(2,1)S(1)} %pad_maximum_fusion.1), channel_id=1, source_target_pairs={{0,8},{8,16},{16,24},{24,32},{32,40},{40,48},{48,56},{56,64},{64,7... | collective-permute-start | bytes 270344 | tf_op jit(solution)/shard_map/ppermute | solution.py:287
  113.8 10.1 %collective-permute-start.17 = (bf16[176,256]{1,0:T(8,128)(2,1)S(1)}, bf16[176,256]{1,0:T(8,128)(2,1)S(1)}, u32[]{:S(2)}, u32[]{:S(2)}) collective-permute-start(bf16[176,256]{1,0:T(8,128)(2,1)S(1)} %pad_maximum_fusion), channel_id=1, source_target_pairs={{0,8},{8,16},{16,24},{24,32},{32,40},{40,48},{48,56},{56,64},{64,7... | collective-permute-start | bytes 270344 | tf_op jit(solution)/shard_map/ppermute | solution.py:287
  127.3 28.0 %all-to-all-start = ((bf16[8,128,512]{2,1,0:T(8,128)(2,1)}), bf16[8,128,512]{2,1,0:T(8,128)(2,1)S(1)}, u32[]{:S(2)}, u32[]{:S(2)}) async-start(bf16[8,128,512]{2,1,0:T(8,128)(2,1)} %bitcast.39), calls=%async_computation | async-start | bytes 2097152 | tf_op jit(solution)/shard_map/all_to_all | solution.py:313
  (38 other events, 299.6 us)
Sparse Core Ops, SparseCore 0:
  9.7 56.5 all-gather.1

commit v5 on v4

--- a/solution.py
+++ b/solution.py
@@ -92,39 +92,61 @@
     return [first + x, first + (x + size - 1) % size, first + (x + 1) % size, first + (x + 2) % size]
 
 
-def add_product_kernel(count, places, *refs):
-    del places
-    lefts, rights, rest = refs[:count], refs[count : 2 * count], refs[2 * count :]
-    left = jnp.concatenate([ref[...] for ref in lefts], axis=1)
-    right = jnp.concatenate([ref[...] for ref in rights], axis=0)
-    total = jnp.dot(left, right, preferred_element_type=jnp.float32)
-    if len(rest) == 2:
-        total = total + rest[0][...]
-    rest[-1][...] = total.astype(rest[-1].dtype)
+def add_product_kernel(count, places, left, *refs):
+    rights, rest = refs[:count], refs[count:]
+    deep = rights[0].shape[0]
+    step = 256
+    for first in range(0, left.shape[0], step):
+        rows = slice(first, first + step)
+        total = rest[0][rows, :] if len(rest) == 2 else None
+        for n, right in enumerate(rights):
+            columns = pl.ds(pl.multiple_of(places[n] * deep, deep), deep)
+            term = jnp.dot(left[rows, columns], right[...], preferred_element_type=jnp.float32)
+            total = term if total is None else total + term
+        rest[-1][rows, :] = total.astype(rest[-1].dtype)
 
 
 def add_product(left, pieces, places, total, dtype):
     length = left.shape[0]
     deep, wide = pieces[0].shape
-    rows = 512
     count = len(pieces)
-    spec = pltpu.PrefetchScalarGridSpec(
-        num_scalar_prefetch=1,
-        grid=(length // rows,),
-        in_specs=[pl.BlockSpec((rows, deep), lambda r, at, n=n: (r, at[n])) for n in range(count)]
-        + [pl.BlockSpec((deep, wide), lambda r, at: (0, 0)) for _ in range(count)]
-        + ([] if total is None else [pl.BlockSpec((rows, wide), lambda r, at: (r, 0))]),
-        out_specs=pl.BlockSpec((rows, wide), lambda r, at: (r, 0)),
-    )
+    vmem = pl.BlockSpec(memory_space=pltpu.VMEM)
+    given = [left, *pieces] + ([] if total is None else [total])
     return pl.pallas_call(
         functools.partial(add_product_kernel, count),
         out_shape=jax.ShapeDtypeStruct((length, wide), dtype),
-        grid_spec=spec,
-        compiler_params=pltpu.CompilerParams(vmem_limit_bytes=40 << 20),
+        in_specs=[pl.BlockSpec(memory_space=pltpu.SMEM)] + [vmem] * len(given),
+        out_specs=vmem,
+        compiler_params=pltpu.CompilerParams(vmem_limit_bytes=24 << 20),
         cost_estimate=pl.CostEstimate(
             flops=2 * length * deep * wide * count, bytes_accessed=8_000_000, transcendentals=0
         ),
-    )(jnp.stack(places).astype(jnp.int32), *[left] * count, *pieces, *([] if total is None else [total]))
+    )(jnp.stack(places).astype(jnp.int32), *given)
+
+
+def add_returned_kernel(half, tokens, returned, out):
+    rows = tokens.shape[0]
+    sources = returned.shape[0] // rows
+    channels = returned.shape[1] // 2
+    for side in range(2):
+        for n in range(sources):
+            first = ((half[0] if side == 0 else 1 - half[0]) * sources + n) * channels
+            columns = pl.ds(pl.multiple_of(first, channels), channels)
+            gated = returned[n * rows : (n + 1) * rows, side * channels : (side + 1) * channels]
+            total = tokens[:, columns].astype(jnp.float32) + gated.astype(jnp.float32)
+            out[:, columns] = total.astype(out.dtype)
+
+
+def add_returned(tokens, returned, half):
+    vmem = pl.BlockSpec(memory_space=pltpu.VMEM)
+    return pl.pallas_call(
+        add_returned_kernel,
+        out_shape=jax.ShapeDtypeStruct(tokens.shape, jnp.bfloat16),
+        in_specs=[pl.BlockSpec(memory_space=pltpu.SMEM), vmem, vmem],
+        out_specs=vmem,
+        compiler_params=pltpu.CompilerParams(vmem_limit_bytes=16 << 20),
+        cost_estimate=pl.CostEstimate(flops=1_000_000, bytes_accessed=3_000_000, transcendentals=0),
+    )(half[None].astype(jnp.int32), tokens, returned)
 
 
 def mix_conv_kernel(
@@ -293,7 +315,7 @@
     ).astype(jnp.bfloat16)
     rows_of = [spread_rows(mine) for _, mine in columns]
     onwards = [onward for _, _, onward in rows_of]
-    onwards[1], onwards[2], own_projected = lax.optimization_barrier((onwards[1], onwards[2], own_projected))
+    onwards[3], own_projected = lax.optimization_barrier((onwards[3], own_projected))
     pieces, places = [], []
     for (by, mine), (below, above, _), onward in zip(columns, rows_of, onwards):
         pieces += [mine, below, above, lax.ppermute(onward, ("x", "core"), fan("x"))]
@@ -310,13 +332,8 @@
     own_halo = halo_of(other_projected, other_short)
     gated = mix_conv(other_projected, other_halo, other_short, other_band, starts, length, gated, 1)
     gated = mix_conv(own_projected, own_halo, own_short, own_band, starts, 2 * SPAN, gated, 0)
-    returned = lax.all_to_all(gated, ("y", "core"), split_axis=0, concat_axis=1, tiled=True)
-    returned = returned.reshape(rows, -1, 2, channels)
-    own, other = returned[:, :, 0].reshape(rows, -1), returned[:, :, 1].reshape(rows, -1)
-    left = jnp.where(z_hi == 0, own, other)
-    right = jnp.where(z_hi == 0, other, own)
-    gated = jnp.concatenate([left, right], axis=1)
-    return (float_tokens + gated.astype(jnp.float32)).astype(jnp.bfloat16)
+    returned = lax.all_to_all(gated, ("y", "core"), split_axis=0, concat_axis=0, tiled=True)
+    return add_returned(tokens, returned, z_hi)
 
 
 def solution(mesh):

time: 166 us -> 164 us (0.988)
  the two profiles are of different devices: /device:TPU:1 before, /device:TPU:6 now
where the time goes in v5:
time: 164 us
  starting transfers between devices  33.8 us (21%)
  waiting for transfers between devices  32 us (20%)
  Pallas kernels  24.2 us (15%)
  blocking collectives  20.3 us (12%)
  local copies, waits for them, and re-layouts  19.4 us (12%)
  between operations  14.3 us (9%)
  matrix products  11.1 us (7%)
  other arithmetic  9.38 us (6%)
    all_to_all x1, blocking collectives, per_device(): lax.all_to_all(gated, ('y', 'core'), split_axis=0, concat_axis=0, tiled=T...  20.3 us
    ppermute x8, waiting for transfers between devices, shift(): lax.ppermute(value, axis, [(i, (i + by) % size) for i in range(size)])  16.2 us
    pallas_call x3, Pallas kernels, mix_conv(): pl.pallas_call(body, out_shape=jax.ShapeDtypeStruct((length, 2 * channels...  13.3 us
    dot_general x1, matrix products, per_device(): lax.dot_general(gathered, weight_t, (((1,), (1,)), ((), ())), preferred_e...  11.1 us
    pallas_call x2, Pallas kernels, add_product(): pl.pallas_call(functools.partial(add_product_kernel, count), out_shape=ja...  9.19 us
    optimization_barrier x1, local copies, waits for them, and re-layouts, per_device(): in_weight, normed = lax.optimization_barrier((in_weight, normed))  8.82 us
    ppermute x8, starting transfers between devices, shift(): lax.ppermute(value, axis, [(i, (i + by) % size) for i in range(size)])  8.18 us
    ppermute x2, starting transfers between devices, halo_of(): lax.ppermute(tail_of(projected, short, starts), ('z_lo', 'x', 'z_hi'), ne...  7.96 us
  transfers between devices with their start and end apart: 20, of which 8 were waited for; matrix products, arithmetic and copies ran while one was open for 21% of the time, Pallas kernels for 12%

profile of v5, /device:TPU:6, one launch (start us, length us, event | category | flops | bytes accessed | tf_op | source)
XLA Modules:
  0.0 164.4 jit_solution(5965004026275155867)
XLA Ops:
  9.7 6.4 %collective-permute-start = (bf16[256,768]{1,0:T(8,128)(2,1)S(1)}, bf16[256,768]{1,0:T(8,128)(2,1)S(1)}, u32[]{:S(2)}, u32[]{:S(2)}) collective-permute-start(bf16[256,768]{1,0:T(8,128)(2,1)S(1)} %copy.24), channel_id=1, source_target_pairs={{0,136},{8,128},{64,200},{72,192},{128,8},{136,0},{192,72},{200,64... | collective-permute-start | bytes 1179656 | tf_op jit(solution)/shard_map/ppermute | solution.py:55
  21.0 8.8 %copy.25 = bf16[4096,3,256]{0,2,1:T(8,128)(2,1)} copy(bf16[4096,3,256]{2,0,1:T(8,128)(2,1)} %param.8) | data formatting | bytes 12582912 | tf_op jit(solution)/shard_map/optimization_barrier | solution.py:292
  36.9 2.1 %collective-permute-start.8 = (bf16[256,768]{1,0:T(8,128)(2,1)}, bf16[256,768]{1,0:T(8,128)(2,1)S(1)}, u32[]{:S(2)}, u32[]{:S(2)}) collective-permute-start(bf16[256,768]{1,0:T(8,128)(2,1)} %get-tuple-element.43), channel_id=1, source_target_pairs={{0,200},{8,192},{64,0},{72,8},{128,64},{136,72},{192,128},{200,136... | collective-permute-start | bytes 1179656 | tf_op jit(solution)/shard_map/ppermute | solution.py:65
  40.0 1.6 collective-permute-start.2
  42.5 5.4 %collective-permute-done.4.refs_4_ = bf16[256,768]{1,0:T(8,128)(2,1)S(1)} collective-permute-done((bf16[256,768]{1,0:T(8,128)(2,1)}, bf16[256,768]{1,0:T(8,128)(2,1)S(1)}, u32[]{:S(2)}, u32[]{:S(2)}) %collective-permute-start.4) | collective-permute-done | bytes 393248 | tf_op jit(solution)/shard_map/ppermute | solution.py:65
  49.0 3.0 %collective-permute-start.9 = (bf16[256,768]{1,0:T(8,128)(2,1)S(1)}, bf16[256,768]{1,0:T(8,128)(2,1)S(1)}, u32[]{:S(2)}, u32[]{:S(2)}) collective-permute-start(bf16[256,768]{1,0:T(8,128)(2,1)S(1)} %select_select_fusion), channel_id=1, source_target_pairs={{64,128},{128,64},{0,200},{192,8},{72,136},{136,72},{8,192},{200,0... | collective-permute-start | bytes 1179656 | tf_op jit(solution)/shard_map/ppermute | solution.py:79
  54.3 1.8 %collective-permute-start.13 = (bf16[256,768]{1,0:T(8,128)(2,1)S(1)}, bf16[256,768]{1,0:T(8,128)(2,1)S(1)}, u32[]{:S(2)}, u32[]{:S(2)}) collective-permute-start(bf16[256,768]{1,0:T(8,128)(2,1)S(1)} %collective-permute-done.8.refs_0_), channel_id=1, source_target_pairs={{0,16},{16,32},{32,48},{48,0},{1,17},{17,33},{33,49},{49,1},{2,18}... | collective-permute-start | bytes 1179656 | tf_op jit(solution)/shard_map/ppermute | solution.py:22
  57.2 3.1 %collective-permute-done.9.refs_4_ = bf16[256,768]{1,0:T(8,128)(2,1)S(1)} collective-permute-done((bf16[256,768]{1,0:T(8,128)(2,1)S(1)}, bf16[256,768]{1,0:T(8,128)(2,1)S(1)}, u32[]{:S(2)}, u32[]{:S(2)}) %collective-permute-start.9) | collective-permute-done | bytes 393248 | tf_op jit(solution)/shard_map/ppermute | solution.py:79
  60.8 3.2 %collective-permute-done.5.refs_5_ = bf16[256,768]{1,0:T(8,128)(2,1)S(1)} collective-permute-done((bf16[256,768]{1,0:T(8,128)(2,1)S(1)}, bf16[256,768]{1,0:T(8,128)(2,1)S(1)}, u32[]{:S(2)}, u32[]{:S(2)}) %collective-permute-start.5) | collective-permute-done | bytes 393248 | tf_op jit(solution)/shard_map/ppermute | solution.py:22
  64.1 1.7 %collective-permute-start.10 = (bf16[256,768]{1,0:T(8,128)(2,1)S(1)}, bf16[256,768]{1,0:T(8,128)(2,1)S(1)}, u32[]{:S(2)}, u32[]{:S(2)}) collective-permute-start(bf16[256,768]{1,0:T(8,128)(2,1)S(1)} %collective-permute-done.9.refs_4_), channel_id=1, source_target_pairs={{0,16},{16,32},{32,48},{48,0},{1,17},{17,33},{33,49},{49,1},{2,18}... | collective-permute-start | bytes 1179656 | tf_op jit(solution)/shard_map/ppermute | solution.py:22
  66.9 5.6 %collective-permute-done.13.refs_1_ = bf16[256,768]{1,0:T(8,128)(2,1)S(1)} collective-permute-done((bf16[256,768]{1,0:T(8,128)(2,1)S(1)}, bf16[256,768]{1,0:T(8,128)(2,1)S(1)}, u32[]{:S(2)}, u32[]{:S(2)}) %collective-permute-start.13) | collective-permute-done | bytes 393248 | tf_op jit(solution)/shard_map/ppermute | solution.py:22
  72.5 1.7 %collective-permute-start.7 = (bf16[256,768]{1,0:T(8,128)(2,1)}, bf16[256,768]{1,0:T(8,128)(2,1)}, u32[]{:S(2)}, u32[]{:S(2)}) collective-permute-start(bf16[256,768]{1,0:T(8,128)(2,1)} %broadcast_select_fusion.4), channel_id=1, source_target_pairs={{0,16},{1,49},{16,32},{17,1},{32,48},{33,17},{48,0},{49,33},{2,18}... | collective-permute-start | bytes 1179656 | tf_op jit(solution)/shard_map/ppermute | solution.py:321
  75.3 7.2 %collective-permute-done.10.refs_5_ = bf16[256,768]{1,0:T(8,128)(2,1)S(1)} collective-permute-done((bf16[256,768]{1,0:T(8,128)(2,1)S(1)}, bf16[256,768]{1,0:T(8,128)(2,1)S(1)}, u32[]{:S(2)}, u32[]{:S(2)}) %collective-permute-start.10) | collective-permute-done | bytes 393248 | tf_op jit(solution)/shard_map/ppermute | solution.py:22
  85.0 11.1 %convolution_convert_fusion.refs_1_.proj = bf16[1024,768]{1,0:T(8,128)(2,1)S(1)} fusion(bf16[1024,4096]{1,0:T(8,128)(2,1)} %all-gather.2.cloned.1.call-done.left, bf16[768,4096]{1,0:T(8,128)(2,1)} %bitcast.54), kind=kOutput, calls=%fused_computation.5 | convolution fusion | flops 6443237376 | bytes 16252928 | tf_op jit(solution)/shard_map/dot_general | solution.py:313
  96.4 4.8 %shard_map.64.refs_8_ = f32[1024,768]{1,0:T(8,128)S(1)} custom-call(s32[8]{0:T(128)S(1)} %copy-done.19, bf16[1024,4096]{1,0:T(8,128)(2,1)S(1)} %copy-done, bf16[256,768]{1,0:T(8,128)(2,1)S(1)} %collective-permute-done.refs_0_, bf16[256,768]{1,0:T(8,128)(2,1)S(1)} %collective-permute-done.1.refs_1_, bf16[256,768]{1,0:T(8,128)(2,1)} %collective-permute-done.2.refs_2_, ...), custom_call_target="tpu_custom_call" | custom-call | flops 3221225472 | bytes 8000000 | tf_op jit(solution)/shard_map/pallas_call | solution.py:115
  101.4 6.0 %collective-permute-start.18 = (bf16[176,256]{1,0:T(8,128)(2,1)S(1)}, bf16[176,256]{1,0:T(8,128)(2,1)S(1)}, u32[]{:S(2)}, u32[]{:S(2)}) collective-permute-start(bf16[176,256]{1,0:T(8,128)(2,1)S(1)} %pad_maximum_fusion.1), channel_id=1, source_target_pairs={{0,8},{8,16},{16,24},{24,32},{32,40},{40,48},{48,56},{56,64},{64,7... | collective-permute-start | bytes 270344 | tf_op jit(solution)/shard_map/ppermute | solution.py:309
  108.6 5.4 %shard_map.66.into = bf16[1024,512]{1,0:T(8,128)(2,1)S(1)} custom-call(s32[8]{0:T(128)S(1)} %copy-done.21, bf16[1024,768]{1,0:T(8,128)(2,1)S(1)} %convolution_convert_fusion.refs_1_.proj, bf16[176,256]{1,0:T(8,128)(2,1)S(1)} %broadcast_in_dim.96.refs_2_, f32[9,256]{1,0:T(8,128)S(1)} %copy-done.15, bf16[16,256,128]{2,1,0:T(8,128)(2,1)S(1)} %copy-done.23, ...), custom_call_target="tpu_custom_call" | custom-call | flops 6144000000 | bytes 4000000 | tf_op jit(solution)/shard_map/pallas_call | solution.py:231
  114.0 3.2 %collective-permute-done.16.refs_7_ = bf16[256,768]{1,0:T(8,128)(2,1)S(1)} collective-permute-done((bf16[256,768]{1,0:T(8,128)(2,1)S(1)}, bf16[256,768]{1,0:T(8,128)(2,1)S(1)}, u32[]{:S(2)}, u32[]{:S(2)}) %collective-permute-start.16) | collective-permute-done | bytes 393248 | tf_op jit(solution)/shard_map/ppermute | solution.py:321
  117.3 4.4 %shard_map.67.proj = bf16[1024,768]{1,0:T(8,128)(2,1)S(1)} custom-call(s32[8]{0:T(128)S(1)} %copy-done.18, bf16[1024,4096]{1,0:T(8,128)(2,1)S(1)} %copy-done, bf16[256,768]{1,0:T(8,128)(2,1)S(1)} %collective-permute-done.8.refs_0_, bf16[256,768]{1,0:T(8,128)(2,1)S(1)} %collective-permute-done.13.refs_1_, ...), custom_call_target="tpu_custom_call" | custom-call | flops 3221225472 | bytes 8000000 | tf_op jit(solution)/shard_map/pallas_call | solution.py:115
  122.0 1.9 %collective-permute-start.17 = (bf16[176,256]{1,0:T(8,128)(2,1)S(1)}, bf16[176,256]{1,0:T(8,128)(2,1)S(1)}, u32[]{:S(2)}, u32[]{:S(2)}) collective-permute-start(bf16[176,256]{1,0:T(8,128)(2,1)S(1)} %pad_maximum_fusion), channel_id=1, source_target_pairs={{0,8},{8,16},{16,24},{24,32},{32,40},{40,48},{48,56},{56,64},{64,7... | collective-permute-start | bytes 270344 | tf_op jit(solution)/shard_map/ppermute | solution.py:309
  123.9 5.2 %shard_map.69.into = bf16[1024,512]{1,0:T(8,128)(2,1)S(1)} custom-call(s32[8]{0:T(128)S(1)} %copy-done.21, bf16[1024,768]{1,0:T(8,128)(2,1)S(1)} %shard_map.67.proj, bf16[176,256]{1,0:T(8,128)(2,1)S(1)} %collective-permute-done.18.halo, f32[9,256]{1,0:T(8,128)S(1)} %slice_convert_fusion.short, ...), custom_call_target="tpu_custom_call", output_to_operand_aliasing={{}: (7, {})} | custom-call | flops 6144000000 | bytes 4000000 | tf_op jit(solution)/shard_map/pallas_call | solution.py:231
  129.1 4.1 %collective-permute-done.17.halo = bf16[176,256]{1,0:T(8,128)(2,1)S(1)} collective-permute-done((bf16[176,256]{1,0:T(8,128)(2,1)S(1)}, bf16[176,256]{1,0:T(8,128)(2,1)S(1)}, u32[]{:S(2)}, u32[]{:S(2)}) %collective-permute-start.17) | collective-permute-done | bytes 90144 | tf_op jit(solution)/shard_map/ppermute | solution.py:309
  133.2 2.7 %shard_map.70 = bf16[1024,512]{1,0:T(8,128)(2,1)S(1)} custom-call(s32[2]{0:T(128)S(1)} %copy-done.20, bf16[1024,768]{1,0:T(8,128)(2,1)S(1)} %convolution_convert_fusion.refs_1_.proj, bf16[176,256]{1,0:T(8,128)(2,1)S(1)} %collective-permute-done.17.halo, f32[9,256]{1,0:T(8,128)S(1)} %copy-done.15, ...), custom_call_target="tpu_custom_call", output_to_operand_aliasing={{}: (7, {})} | custom-call | flops 1536000000 | bytes 4000000 | tf_op jit(solution)/shard_map/pallas_call | solution.py:231
  136.0 20.3 %all_to_all.11 = bf16[8,128,512]{2,1,0:T(8,128)(2,1)S(1)} all-to-all(bf16[8,128,512]{2,1,0:T(8,128)(2,1)S(1)} %bitcast.48), channel_id=1, replica_groups=mesh['z_lo'=4,'x'=4,'z_hi'=2,'y'=4,'core'=2] {'y','core'}, dimensions={0} | all-to-all | bytes 2097152 | tf_op jit(solution)/shard_map/all_to_all | solution.py:335
  (165 shorter events, 29.4 us)
Async XLA Ops:
  6.5 78.5 %all-gather.2.cloned.1.call-start = ((), (), s32[]{:S(2)}) async-start(), calls=%async_computation.1 | async-start | bytes 9437184 | tf_op jit(solution)/shard_map/all_gather | solution.py:293
  9.7 24.5 %collective-permute-start = (bf16[256,768]{1,0:T(8,128)(2,1)S(1)}, bf16[256,768]{1,0:T(8,128)(2,1)S(1)}, u32[]{:S(2)}, u32[]{:S(2)}) collective-permute-start(bf16[256,768]{1,0:T(8,128)(2,1)S(1)} %copy.24), channel_id=1, source_target_pairs={{0,136},{8,128},{64,200},{72,192},{128,8},{136,0},{192,72},{200,64... | collective-permute-start | bytes 1179656 | tf_op jit(solution)/shard_map/ppermute | solution.py:55
  16.2 18.0 %collective-permute-start.12 = (bf16[17,256]{1,0:T(8,128)(2,1)S(1)}, bf16[17,256]{1,0:T(8,128)(2,1)S(1)}, u32[]{:S(2)}, u32[]{:S(2)}) collective-permute-start(bf16[17,256]{1,0:T(8,128)(2,1)S(1)} %pad_maximum_fusion.2), channel_id=1, source_target_pairs={{0,8},{8,0},{1,9},{9,1},{2,10},{10,2},{3,11},{11,3},{4,12},{12,4},... | collective-permute-start | bytes 26120 | tf_op jit(solution)/shard_map/ppermute | solution.py:17
  35.4 12.5 %collective-permute-start.4 = (bf16[256,768]{1,0:T(8,128)(2,1)}, bf16[256,768]{1,0:T(8,128)(2,1)S(1)}, u32[]{:S(2)}, u32[]{:S(2)}) collective-permute-start(bf16[256,768]{1,0:T(8,128)(2,1)} %get-tuple-element.44), channel_id=1, source_target_pairs={{0,64},{8,72},{64,128},{72,136},{128,192},{136,200},{192,8},{200,0... | collective-permute-start | bytes 1179656 | tf_op jit(solution)/shard_map/ppermute | solution.py:65
  36.9 11.0 %collective-permute-start.8 = (bf16[256,768]{1,0:T(8,128)(2,1)}, bf16[256,768]{1,0:T(8,128)(2,1)S(1)}, u32[]{:S(2)}, u32[]{:S(2)}) collective-permute-start(bf16[256,768]{1,0:T(8,128)(2,1)} %get-tuple-element.43), channel_id=1, source_target_pairs={{0,200},{8,192},{64,0},{72,8},{128,64},{136,72},{192,128},{200,136... | collective-permute-start | bytes 1179656 | tf_op jit(solution)/shard_map/ppermute | solution.py:65
  39.5 14.7 %collective-permute-start.1 = (bf16[256,768]{1,0:T(8,128)(2,1)S(1)}, bf16[256,768]{1,0:T(8,128)(2,1)S(1)}, u32[]{:S(2)}, u32[]{:S(2)}) collective-permute-start(bf16[256,768]{1,0:T(8,128)(2,1)S(1)} %collective-permute-done.refs_0_), channel_id=1, source_target_pairs={{0,16},{16,32},{32,48},{48,0},{1,17},{17,33},{33,49},{49,1},{2,18}... | collective-permute-start | bytes 1179656 | tf_op jit(solution)/shard_map/ppermute | solution.py:22
  40.0 16.1 %collective-permute-start.2 = (bf16[256,768]{1,0:T(8,128)(2,1)S(1)}, bf16[256,768]{1,0:T(8,128)(2,1)}, u32[]{:S(2)}, u32[]{:S(2)}) collective-permute-start(bf16[256,768]{1,0:T(8,128)(2,1)S(1)} %collective-permute-done.refs_0_), channel_id=1, source_target_pairs={{0,48},{16,0},{32,16},{48,32},{1,49},{17,1},{33,17},{49,33},{2,50}... | collective-permute-start | bytes 1179656 | tf_op jit(solution)/shard_map/ppermute | solution.py:22
  49.0 11.3 %collective-permute-start.9 = (bf16[256,768]{1,0:T(8,128)(2,1)S(1)}, bf16[256,768]{1,0:T(8,128)(2,1)S(1)}, u32[]{:S(2)}, u32[]{:S(2)}) collective-permute-start(bf16[256,768]{1,0:T(8,128)(2,1)S(1)} %select_select_fusion), channel_id=1, source_target_pairs={{64,128},{128,64},{0,200},{192,8},{72,136},{136,72},{8,192},{200,0... | collective-permute-start | bytes 1179656 | tf_op jit(solution)/shard_map/ppermute | solution.py:79
  52.0 12.1 %collective-permute-start.5 = (bf16[256,768]{1,0:T(8,128)(2,1)S(1)}, bf16[256,768]{1,0:T(8,128)(2,1)S(1)}, u32[]{:S(2)}, u32[]{:S(2)}) collective-permute-start(bf16[256,768]{1,0:T(8,128)(2,1)S(1)} %collective-permute-done.4.refs_4_), channel_id=1, source_target_pairs={{0,16},{16,32},{32,48},{48,0},{1,17},{17,33},{33,49},{49,1},{2,18}... | collective-permute-start | bytes 1179656 | tf_op jit(solution)/shard_map/ppermute | solution.py:22
  52.5 13.3 %collective-permute-start.6 = (bf16[256,768]{1,0:T(8,128)(2,1)S(1)}, bf16[256,768]{1,0:T(8,128)(2,1)S(1)}, u32[]{:S(2)}, u32[]{:S(2)}) collective-permute-start(bf16[256,768]{1,0:T(8,128)(2,1)S(1)} %collective-permute-done.4.refs_4_), channel_id=1, source_target_pairs={{0,48},{16,0},{32,16},{48,32},{1,49},{17,1},{33,17},{49,33},{2,50}... | collective-permute-start | bytes 1179656 | tf_op jit(solution)/shard_map/ppermute | solution.py:22
  54.3 28.4 %copy-start.24 = (bf16[16,256,128]{2,1,0:T(8,128)(2,1)}, bf16[16,256,128]{2,1,0:T(8,128)(2,1)S(1)}, u32[]{:S(2)}) copy-start(bf16[16,256,128]{2,1,0:T(8,128)(2,1)S(1)} %shard_map.68.band) | copy-start | bytes 3145732
  54.3 18.2 %collective-permute-start.13 = (bf16[256,768]{1,0:T(8,128)(2,1)S(1)}, bf16[256,768]{1,0:T(8,128)(2,1)S(1)}, u32[]{:S(2)}, u32[]{:S(2)}) collective-permute-start(bf16[256,768]{1,0:T(8,128)(2,1)S(1)} %collective-permute-done.8.refs_0_), channel_id=1, source_target_pairs={{0,16},{16,32},{32,48},{48,0},{1,17},{17,33},{33,49},{49,1},{2,18}... | collective-permute-start | bytes 1179656 | tf_op jit(solution)/shard_map/ppermute | solution.py:22
  56.1 18.1 %collective-permute-start.14 = (bf16[256,768]{1,0:T(8,128)(2,1)S(1)}, bf16[256,768]{1,0:T(8,128)(2,1)S(1)}, u32[]{:S(2)}, u32[]{:S(2)}) collective-permute-start(bf16[256,768]{1,0:T(8,128)(2,1)S(1)} %collective-permute-done.8.refs_0_), channel_id=1, source_target_pairs={{0,48},{16,0},{32,16},{48,32},{1,49},{17,1},{33,17},{49,33},{2,50}... | collective-permute-start | bytes 1179656 | tf_op jit(solution)/shard_map/ppermute | solution.py:22
  60.3 22.4 %copy-start.11 = (bf16[256,768]{1,0:T(8,128)(2,1)}, bf16[256,768]{1,0:T(8,128)(2,1)S(1)}, u32[]{:S(2)}) copy-start(bf16[256,768]{1,0:T(8,128)(2,1)S(1)} %collective-permute-done.9.refs_4_) | copy-start | bytes 1179652
  60.3 36.0 %collective-permute-start.3 = (bf16[256,768]{1,0:T(8,128)(2,1)}, bf16[256,768]{1,0:T(8,128)(2,1)}, u32[]{:S(2)}, u32[]{:S(2)}) collective-permute-start(bf16[256,768]{1,0:T(8,128)(2,1)} %broadcast_select_fusion.5), channel_id=1, source_target_pairs={{0,16},{1,49},{16,32},{17,1},{32,48},{33,17},{48,0},{49,33},{2,18}... | collective-permute-start | bytes 1179656 | tf_op jit(solution)/shard_map/ppermute | solution.py:321
  64.1 18.6 %copy-start.6 = (bf16[256,768]{1,0:T(8,128)(2,1)}, bf16[256,768]{1,0:T(8,128)(2,1)S(1)}, u32[]{:S(2)}) copy-start(bf16[256,768]{1,0:T(8,128)(2,1)S(1)} %collective-permute-done.5.refs_5_) | copy-start | bytes 1179652
  64.1 18.4 %collective-permute-start.10 = (bf16[256,768]{1,0:T(8,128)(2,1)S(1)}, bf16[256,768]{1,0:T(8,128)(2,1)S(1)}, u32[]{:S(2)}, u32[]{:S(2)}) collective-permute-start(bf16[256,768]{1,0:T(8,128)(2,1)S(1)} %collective-permute-done.9.refs_4_), channel_id=1, source_target_pairs={{0,16},{16,32},{32,48},{48,0},{1,17},{17,33},{33,49},{49,1},{2,18}... | collective-permute-start | bytes 1179656 | tf_op jit(solution)/shard_map/ppermute | solution.py:22
  65.8 16.9 %copy-start.8 = (bf16[256,768]{1,0:T(8,128)(2,1)}, bf16[256,768]{1,0:T(8,128)(2,1)S(1)}, u32[]{:S(2)}) copy-start(bf16[256,768]{1,0:T(8,128)(2,1)S(1)} %collective-permute-done.6.refs_6_) | copy-start | bytes 1179652
  65.8 16.8 %collective-permute-start.11 = (bf16[256,768]{1,0:T(8,128)(2,1)S(1)}, bf16[256,768]{1,0:T(8,128)(2,1)S(1)}, u32[]{:S(2)}, u32[]{:S(2)}) collective-permute-start(bf16[256,768]{1,0:T(8,128)(2,1)S(1)} %collective-permute-done.9.refs_4_), channel_id=1, source_target_pairs={{0,48},{16,0},{32,16},{48,32},{1,49},{17,1},{33,17},{49,33},{2,50}... | collective-permute-start | bytes 1179656 | tf_op jit(solution)/shard_map/ppermute | solution.py:22
  72.5 23.8 %collective-permute-start.7 = (bf16[256,768]{1,0:T(8,128)(2,1)}, bf16[256,768]{1,0:T(8,128)(2,1)}, u32[]{:S(2)}, u32[]{:S(2)}) collective-permute-start(bf16[256,768]{1,0:T(8,128)(2,1)} %broadcast_select_fusion.4), channel_id=1, source_target_pairs={{0,16},{1,49},{16,32},{17,1},{32,48},{33,17},{48,0},{49,33},{2,18}... | collective-permute-start | bytes 1179656 | tf_op jit(solution)/shard_map/ppermute | solution.py:321
  75.0 39.0 %collective-permute-start.15 = (bf16[256,768]{1,0:T(8,128)(2,1)}, bf16[256,768]{1,0:T(8,128)(2,1)}, u32[]{:S(2)}, u32[]{:S(2)}) collective-permute-start(bf16[256,768]{1,0:T(8,128)(2,1)} %broadcast_select_fusion.2), channel_id=1, source_target_pairs={{0,16},{1,49},{16,32},{17,1},{32,48},{33,17},{48,0},{49,33},{2,18}... | collective-permute-start | bytes 1179656 | tf_op jit(solution)/shard_map/ppermute | solution.py:321
  101.4 22.5 %collective-permute-start.18 = (bf16[176,256]{1,0:T(8,128)(2,1)S(1)}, bf16[176,256]{1,0:T(8,128)(2,1)S(1)}, u32[]{:S(2)}, u32[]{:S(2)}) collective-permute-start(bf16[176,256]{1,0:T(8,128)(2,1)S(1)} %pad_maximum_fusion.1), channel_id=1, source_target_pairs={{0,8},{8,16},{16,24},{24,32},{32,40},{40,48},{48,56},{56,64},{64,7... | collective-permute-start | bytes 270344 | tf_op jit(solution)/shard_map/ppermute | solution.py:309
  107.5 9.8 %collective-permute-start.16 = (bf16[256,768]{1,0:T(8,128)(2,1)S(1)}, bf16[256,768]{1,0:T(8,128)(2,1)S(1)}, u32[]{:S(2)}, u32[]{:S(2)}) collective-permute-start(bf16[256,768]{1,0:T(8,128)(2,1)S(1)} %copy-done.26), channel_id=1, source_target_pairs={{0,16},{1,49},{16,32},{17,1},{32,48},{33,17},{48,0},{49,33},{2,18}... | collective-permute-start | bytes 1179656 | tf_op jit(solution)/shard_map/ppermute | solution.py:321
  122.0 11.2 %collective-permute-start.17 = (bf16[176,256]{1,0:T(8,128)(2,1)S(1)}, bf16[176,256]{1,0:T(8,128)(2,1)S(1)}, u32[]{:S(2)}, u32[]{:S(2)}) collective-permute-start(bf16[176,256]{1,0:T(8,128)(2,1)S(1)} %pad_maximum_fusion), channel_id=1, source_target_pairs={{0,8},{8,16},{16,24},{24,32},{32,40},{40,48},{48,56},{56,64},{64,7... | collective-permute-start | bytes 270344 | tf_op jit(solution)/shard_map/ppermute | solution.py:309
  (42 other events, 337.2 us)
Sparse Core Ops, SparseCore 0:
  9.7 55.1 all-gather.1

commit v6 on v5

--- a/solution.py
+++ b/solution.py
@@ -315,7 +315,7 @@
     ).astype(jnp.bfloat16)
     rows_of = [spread_rows(mine) for _, mine in columns]
     onwards = [onward for _, _, onward in rows_of]
-    onwards[3], own_projected = lax.optimization_barrier((onwards[3], own_projected))
+    onwards[2], own_projected = lax.optimization_barrier((onwards[2], own_projected))
     pieces, places = [], []
     for (by, mine), (below, above, _), onward in zip(columns, rows_of, onwards):
         pieces += [mine, below, above, lax.ppermute(onward, ("x", "core"), fan("x"))]

time: 164 us -> 164 us (level)
  the two profiles are of different devices: /device:TPU:6 before, /device:TPU:1 now
where the time goes in v6:
time: 164 us; the launch traced here: 163 us
  starting transfers between devices  35.7 us (22%)
  waiting for transfers between devices  26 us (16%)
  Pallas kernels  24.8 us (15%)
  blocking collectives  22.1 us (13%)
  local copies, waits for them, and re-layouts  18.7 us (11%)
  between operations  14.3 us (9%)
  matrix products  11.1 us (7%)
  other arithmetic  10.5 us (6%)
    all_to_all x1, blocking collectives, per_device(): lax.all_to_all(gated, ('y', 'core'), split_axis=0, concat_axis=0, tiled=T...  22.1 us
    ppermute x8, waiting for transfers between devices, shift(): lax.ppermute(value, axis, [(i, (i + by) % size) for i in range(size)])  19 us
    pallas_call x3, Pallas kernels, mix_conv(): pl.pallas_call(body, out_shape=jax.ShapeDtypeStruct((length, 2 * channels...  13.9 us
    dot_general x1, matrix products, per_device(): lax.dot_general(gathered, weight_t, (((1,), (1,)), ((), ())), preferred_e...  11.1 us
    ppermute x8, starting transfers between devices, shift(): lax.ppermute(value, axis, [(i, (i + by) % size) for i in range(size)])  9.57 us
    pallas_call x2, Pallas kernels, add_product(): pl.pallas_call(functools.partial(add_product_kernel, count), out_shape=ja...  9.19 us
    optimization_barrier x1, local copies, waits for them, and re-layouts, per_device(): in_weight, normed = lax.optimization_barrier((in_weight, normed))  8.9 us
    ppermute x2, starting transfers between devices, halo_of(): lax.ppermute(tail_of(projected, short, starts), ('z_lo', 'x', 'z_hi'), ne...  7.99 us
  transfers between devices with their start and end apart: 20, of which 7 were waited for; matrix products, arithmetic and copies ran while one was open for 22% of the time, Pallas kernels for 13%

profile of v6, /device:TPU:1, one launch (start us, length us, event | category | flops | bytes accessed | tf_op | source)
XLA Modules:
  0.0 163.3 jit_solution(16377174812224301403)
XLA Ops:
  9.7 6.9 %collective-permute-start = (bf16[256,768]{1,0:T(8,128)(2,1)S(1)}, bf16[256,768]{1,0:T(8,128)(2,1)S(1)}, u32[]{:S(2)}, u32[]{:S(2)}) collective-permute-start(bf16[256,768]{1,0:T(8,128)(2,1)S(1)} %copy.24), channel_id=1, source_target_pairs={{0,136},{8,128},{64,200},{72,192},{128,8},{136,0},{192,72},{200,64... | collective-permute-start | bytes 1179656 | tf_op jit(solution)/shard_map/ppermute | solution.py:55
  21.6 8.9 %copy.25 = bf16[4096,3,256]{0,2,1:T(8,128)(2,1)} copy(bf16[4096,3,256]{2,0,1:T(8,128)(2,1)} %param.8) | data formatting | bytes 12582912 | tf_op jit(solution)/shard_map/optimization_barrier | solution.py:292
  36.0 3.2 %collective-permute-start.8 = (bf16[256,768]{1,0:T(8,128)(2,1)}, bf16[256,768]{1,0:T(8,128)(2,1)S(1)}, u32[]{:S(2)}, u32[]{:S(2)}) collective-permute-start(bf16[256,768]{1,0:T(8,128)(2,1)} %get-tuple-element.43), channel_id=1, source_target_pairs={{0,200},{8,192},{64,0},{72,8},{128,64},{136,72},{192,128},{200,136... | collective-permute-start | bytes 1179656 | tf_op jit(solution)/shard_map/ppermute | solution.py:65
  41.0 1.5 collective-permute-start.2
  43.4 3.5 %collective-permute-done.8.refs_0_ = bf16[256,768]{1,0:T(8,128)(2,1)S(1)} collective-permute-done((bf16[256,768]{1,0:T(8,128)(2,1)}, bf16[256,768]{1,0:T(8,128)(2,1)S(1)}, u32[]{:S(2)}, u32[]{:S(2)}) %collective-permute-start.8) | collective-permute-done | bytes 393248 | tf_op jit(solution)/shard_map/ppermute | solution.py:65
  46.9 3.1 %collective-permute-done.4.refs_4_ = bf16[256,768]{1,0:T(8,128)(2,1)S(1)} collective-permute-done((bf16[256,768]{1,0:T(8,128)(2,1)}, bf16[256,768]{1,0:T(8,128)(2,1)S(1)}, u32[]{:S(2)}, u32[]{:S(2)}) %collective-permute-start.4) | collective-permute-done | bytes 393248 | tf_op jit(solution)/shard_map/ppermute | solution.py:65
  52.7 1.5 collective-permute-start.6
  55.9 1.9 %broadcast_select_fusion.5 = bf16[256,768]{1,0:T(8,128)(2,1)} fusion(bf16[256,768]{1,0:T(8,128)(2,1)S(1)} %collective-permute-done.1.refs_1_, bf16[256,768]{1,0:T(8,128)(2,1)} %collective-permute-done.2.refs_2_, pred[]{:T(512)S(6)} %eq.35), kind=kLoop, calls=%fused_computation.12 | loop fusion | flops 196608 | bytes 1179649 | tf_op jit(solution)/shard_map/jit(_where)/select_n | solution.py:85
  57.8 3.5 %collective-permute-done.5.refs_5_ = bf16[256,768]{1,0:T(8,128)(2,1)S(1)} collective-permute-done((bf16[256,768]{1,0:T(8,128)(2,1)S(1)}, bf16[256,768]{1,0:T(8,128)(2,1)S(1)}, u32[]{:S(2)}, u32[]{:S(2)}) %collective-permute-start.5) | collective-permute-done | bytes 393248 | tf_op jit(solution)/shard_map/ppermute | solution.py:22
  62.8 2.3 %collective-permute-start.15 = (bf16[256,768]{1,0:T(8,128)(2,1)S(1)}, bf16[256,768]{1,0:T(8,128)(2,1)S(1)}, u32[]{:S(2)}, u32[]{:S(2)}) collective-permute-start(bf16[256,768]{1,0:T(8,128)(2,1)S(1)} %collective-permute-done.13.refs_4_), channel_id=1, source_target_pairs={{0,48},{16,0},{32,16},{48,32},{1,49},{17,1},{33,17},{49,33},{2,50}... | collective-permute-start | bytes 1179656 | tf_op jit(solution)/shard_map/ppermute | solution.py:22
  65.9 3.5 %collective-permute-done.10.refs_2_ = bf16[256,768]{1,0:T(8,128)(2,1)S(1)} collective-permute-done((bf16[256,768]{1,0:T(8,128)(2,1)S(1)}, bf16[256,768]{1,0:T(8,128)(2,1)S(1)}, u32[]{:S(2)}, u32[]{:S(2)}) %collective-permute-start.10) | collective-permute-done | bytes 393248 | tf_op jit(solution)/shard_map/ppermute | solution.py:22
  69.3 2.7 %collective-permute-start.7 = (bf16[256,768]{1,0:T(8,128)(2,1)}, bf16[256,768]{1,0:T(8,128)(2,1)}, u32[]{:S(2)}, u32[]{:S(2)}) collective-permute-start(bf16[256,768]{1,0:T(8,128)(2,1)} %broadcast_select_fusion.4), channel_id=1, source_target_pairs={{0,16},{1,49},{16,32},{17,1},{32,48},{33,17},{48,0},{49,33},{2,18}... | collective-permute-start | bytes 1179656 | tf_op jit(solution)/shard_map/ppermute | solution.py:321
  72.8 5.3 %collective-permute-done.14.refs_5_ = bf16[256,768]{1,0:T(8,128)(2,1)S(1)} collective-permute-done((bf16[256,768]{1,0:T(8,128)(2,1)S(1)}, bf16[256,768]{1,0:T(8,128)(2,1)S(1)}, u32[]{:S(2)}, u32[]{:S(2)}) %collective-permute-start.14) | collective-permute-done | bytes 393248 | tf_op jit(solution)/shard_map/ppermute | solution.py:22
  78.2 6.7 %collective-permute-done.15.refs_6_ = bf16[256,768]{1,0:T(8,128)(2,1)S(1)} collective-permute-done((bf16[256,768]{1,0:T(8,128)(2,1)S(1)}, bf16[256,768]{1,0:T(8,128)(2,1)S(1)}, u32[]{:S(2)}, u32[]{:S(2)}) %collective-permute-start.15) | collective-permute-done | bytes 393248 | tf_op jit(solution)/shard_map/ppermute | solution.py:22
  86.5 2.4 %collective-permute-start.16 = (bf16[256,768]{1,0:T(8,128)(2,1)}, bf16[256,768]{1,0:T(8,128)(2,1)}, u32[]{:S(2)}, u32[]{:S(2)}) collective-permute-start(bf16[256,768]{1,0:T(8,128)(2,1)} %broadcast_select_fusion.2), channel_id=1, source_target_pairs={{0,16},{1,49},{16,32},{17,1},{32,48},{33,17},{48,0},{49,33},{2,18}... | collective-permute-start | bytes 1179656 | tf_op jit(solution)/shard_map/ppermute | solution.py:321
  88.9 11.1 %convolution_convert_fusion.refs_1_.proj = bf16[1024,768]{1,0:T(8,128)(2,1)S(1)} fusion(bf16[1024,4096]{1,0:T(8,128)(2,1)} %all-gather.2.cloned.1.call-done.left, bf16[768,4096]{1,0:T(8,128)(2,1)} %bitcast.54), kind=kOutput, calls=%fused_computation.5 | convolution fusion | flops 6443237376 | bytes 16252928 | tf_op jit(solution)/shard_map/dot_general | solution.py:313
  100.3 4.8 %shard_map.64.refs_8_ = f32[1024,768]{1,0:T(8,128)S(1)} custom-call(s32[8]{0:T(128)S(1)} %copy-done.19, bf16[1024,4096]{1,0:T(8,128)(2,1)S(1)} %copy-done, bf16[256,768]{1,0:T(8,128)(2,1)S(1)} %collective-permute-done.refs_0_, bf16[256,768]{1,0:T(8,128)(2,1)S(1)} %collective-permute-done.1.refs_1_, bf16[256,768]{1,0:T(8,128)(2,1)} %collective-permute-done.2.refs_2_, ...), custom_call_target="tpu_custom_call" | custom-call | flops 3221225472 | bytes 8000000 | tf_op jit(solution)/shard_map/pallas_call | solution.py:115
  105.4 3.0 %collective-permute-start.18 = (bf16[176,256]{1,0:T(8,128)(2,1)S(1)}, bf16[176,256]{1,0:T(8,128)(2,1)S(1)}, u32[]{:S(2)}, u32[]{:S(2)}) collective-permute-start(bf16[176,256]{1,0:T(8,128)(2,1)S(1)} %pad_maximum_fusion.1), channel_id=1, source_target_pairs={{0,8},{8,16},{16,24},{24,32},{32,40},{40,48},{48,56},{56,64},{64,7... | collective-permute-start | bytes 270344 | tf_op jit(solution)/shard_map/ppermute | solution.py:309
  108.9 6.0 %shard_map.66.into = bf16[1024,512]{1,0:T(8,128)(2,1)S(1)} custom-call(s32[8]{0:T(128)S(1)} %copy-done.21, bf16[1024,768]{1,0:T(8,128)(2,1)S(1)} %convolution_convert_fusion.refs_1_.proj, bf16[176,256]{1,0:T(8,128)(2,1)S(1)} %broadcast_in_dim.96.refs_2_, f32[9,256]{1,0:T(8,128)S(1)} %copy-done.15, bf16[16,256,128]{2,1,0:T(8,128)(2,1)S(1)} %copy-done.23, ...), custom_call_target="tpu_custom_call" | custom-call | flops 6144000000 | bytes 4000000 | tf_op jit(solution)/shard_map/pallas_call | solution.py:231
  115.4 4.4 %shard_map.67.proj = bf16[1024,768]{1,0:T(8,128)(2,1)S(1)} custom-call(s32[8]{0:T(128)S(1)} %copy-done.18, bf16[1024,4096]{1,0:T(8,128)(2,1)S(1)} %copy-done, bf16[256,768]{1,0:T(8,128)(2,1)S(1)} %collective-permute-done.8.refs_0_, bf16[256,768]{1,0:T(8,128)(2,1)S(1)} %collective-permute-done.9.refs_1_, ...), custom_call_target="tpu_custom_call" | custom-call | flops 3221225472 | bytes 8000000 | tf_op jit(solution)/shard_map/pallas_call | solution.py:115
  120.1 5.0 %collective-permute-start.17 = (bf16[176,256]{1,0:T(8,128)(2,1)S(1)}, bf16[176,256]{1,0:T(8,128)(2,1)S(1)}, u32[]{:S(2)}, u32[]{:S(2)}) collective-permute-start(bf16[176,256]{1,0:T(8,128)(2,1)S(1)} %pad_maximum_fusion), channel_id=1, source_target_pairs={{0,8},{8,16},{16,24},{24,32},{32,40},{40,48},{48,56},{56,64},{64,7... | collective-permute-start | bytes 270344 | tf_op jit(solution)/shard_map/ppermute | solution.py:309
  125.1 5.8 %shard_map.69.into = bf16[1024,512]{1,0:T(8,128)(2,1)S(1)} custom-call(s32[8]{0:T(128)S(1)} %copy-done.21, bf16[1024,768]{1,0:T(8,128)(2,1)S(1)} %shard_map.67.proj, bf16[176,256]{1,0:T(8,128)(2,1)S(1)} %collective-permute-done.18.halo, f32[9,256]{1,0:T(8,128)S(1)} %slice_convert_fusion.short, ...), custom_call_target="tpu_custom_call", output_to_operand_aliasing={{}: (7, {})} | custom-call | flops 6144000000 | bytes 4000000 | tf_op jit(solution)/shard_map/pallas_call | solution.py:231
  131.0 2.1 %shard_map.70 = bf16[1024,512]{1,0:T(8,128)(2,1)S(1)} custom-call(s32[2]{0:T(128)S(1)} %copy-done.20, bf16[1024,768]{1,0:T(8,128)(2,1)S(1)} %convolution_convert_fusion.refs_1_.proj, bf16[176,256]{1,0:T(8,128)(2,1)S(1)} %collective-permute-done.17.halo, f32[9,256]{1,0:T(8,128)S(1)} %copy-done.15, ...), custom_call_target="tpu_custom_call", output_to_operand_aliasing={{}: (7, {})} | custom-call | flops 1536000000 | bytes 4000000 | tf_op jit(solution)/shard_map/pallas_call | solution.py:231
  133.1 22.1 %all_to_all.11 = bf16[8,128,512]{2,1,0:T(8,128)(2,1)S(1)} all-to-all(bf16[8,128,512]{2,1,0:T(8,128)(2,1)S(1)} %bitcast.48), channel_id=1, replica_groups=mesh['z_lo'=4,'x'=4,'z_hi'=2,'y'=4,'core'=2] {'y','core'}, dimensions={0} | all-to-all | bytes 2097152 | tf_op jit(solution)/shard_map/all_to_all | solution.py:335
  (165 shorter events, 27.9 us)
Async XLA Ops:
  6.5 82.4 %all-gather.2.cloned.1.call-start = ((), (), s32[]{:S(2)}) async-start(), calls=%async_computation.1 | async-start | bytes 9437184 | tf_op jit(solution)/shard_map/all_gather | solution.py:293
  9.7 25.1 %collective-permute-start = (bf16[256,768]{1,0:T(8,128)(2,1)S(1)}, bf16[256,768]{1,0:T(8,128)(2,1)S(1)}, u32[]{:S(2)}, u32[]{:S(2)}) collective-permute-start(bf16[256,768]{1,0:T(8,128)(2,1)S(1)} %copy.24), channel_id=1, source_target_pairs={{0,136},{8,128},{64,200},{72,192},{128,8},{136,0},{192,72},{200,64... | collective-permute-start | bytes 1179656 | tf_op jit(solution)/shard_map/ppermute | solution.py:55
  16.7 18.1 %collective-permute-start.11 = (bf16[17,256]{1,0:T(8,128)(2,1)S(1)}, bf16[17,256]{1,0:T(8,128)(2,1)S(1)}, u32[]{:S(2)}, u32[]{:S(2)}) collective-permute-start(bf16[17,256]{1,0:T(8,128)(2,1)S(1)} %pad_maximum_fusion.2), channel_id=1, source_target_pairs={{0,8},{8,0},{1,9},{9,1},{2,10},{10,2},{3,11},{11,3},{4,12},{12,4},... | collective-permute-start | bytes 26120 | tf_op jit(solution)/shard_map/ppermute | solution.py:17
  36.0 10.9 %collective-permute-start.8 = (bf16[256,768]{1,0:T(8,128)(2,1)}, bf16[256,768]{1,0:T(8,128)(2,1)S(1)}, u32[]{:S(2)}, u32[]{:S(2)}) collective-permute-start(bf16[256,768]{1,0:T(8,128)(2,1)} %get-tuple-element.43), channel_id=1, source_target_pairs={{0,200},{8,192},{64,0},{72,8},{128,64},{136,72},{192,128},{200,136... | collective-permute-start | bytes 1179656 | tf_op jit(solution)/shard_map/ppermute | solution.py:65
  39.2 10.9 %collective-permute-start.4 = (bf16[256,768]{1,0:T(8,128)(2,1)}, bf16[256,768]{1,0:T(8,128)(2,1)S(1)}, u32[]{:S(2)}, u32[]{:S(2)}) collective-permute-start(bf16[256,768]{1,0:T(8,128)(2,1)} %get-tuple-element.44), channel_id=1, source_target_pairs={{0,64},{8,72},{64,128},{72,136},{128,192},{136,200},{192,8},{200,0... | collective-permute-start | bytes 1179656 | tf_op jit(solution)/shard_map/ppermute | solution.py:65
  39.8 14.6 %collective-permute-start.1 = (bf16[256,768]{1,0:T(8,128)(2,1)S(1)}, bf16[256,768]{1,0:T(8,128)(2,1)S(1)}, u32[]{:S(2)}, u32[]{:S(2)}) collective-permute-start(bf16[256,768]{1,0:T(8,128)(2,1)S(1)} %collective-permute-done.refs_0_), channel_id=1, source_target_pairs={{0,16},{16,32},{32,48},{48,0},{1,17},{17,33},{33,49},{49,1},{2,18}... | collective-permute-start | bytes 1179656 | tf_op jit(solution)/shard_map/ppermute | solution.py:22
  41.0 14.6 %collective-permute-start.2 = (bf16[256,768]{1,0:T(8,128)(2,1)S(1)}, bf16[256,768]{1,0:T(8,128)(2,1)}, u32[]{:S(2)}, u32[]{:S(2)}) collective-permute-start(bf16[256,768]{1,0:T(8,128)(2,1)S(1)} %collective-permute-done.refs_0_), channel_id=1, source_target_pairs={{0,48},{16,0},{32,16},{48,32},{1,49},{17,1},{33,17},{49,33},{2,50}... | collective-permute-start | bytes 1179656 | tf_op jit(solution)/shard_map/ppermute | solution.py:22
  51.1 11.3 %collective-permute-start.13 = (bf16[256,768]{1,0:T(8,128)(2,1)S(1)}, bf16[256,768]{1,0:T(8,128)(2,1)S(1)}, u32[]{:S(2)}, u32[]{:S(2)}) collective-permute-start(bf16[256,768]{1,0:T(8,128)(2,1)S(1)} %select_select_fusion), channel_id=1, source_target_pairs={{64,128},{128,64},{0,200},{192,8},{72,136},{136,72},{8,192},{200,0... | collective-permute-start | bytes 1179656 | tf_op jit(solution)/shard_map/ppermute | solution.py:79
  51.5 9.8 %collective-permute-start.5 = (bf16[256,768]{1,0:T(8,128)(2,1)S(1)}, bf16[256,768]{1,0:T(8,128)(2,1)S(1)}, u32[]{:S(2)}, u32[]{:S(2)}) collective-permute-start(bf16[256,768]{1,0:T(8,128)(2,1)S(1)} %collective-permute-done.4.refs_4_), channel_id=1, source_target_pairs={{0,16},{16,32},{32,48},{48,0},{1,17},{17,33},{33,49},{49,1},{2,18}... | collective-permute-start | bytes 1179656 | tf_op jit(solution)/shard_map/ppermute | solution.py:22
  52.7 10.1 %collective-permute-start.6 = (bf16[256,768]{1,0:T(8,128)(2,1)S(1)}, bf16[256,768]{1,0:T(8,128)(2,1)S(1)}, u32[]{:S(2)}, u32[]{:S(2)}) collective-permute-start(bf16[256,768]{1,0:T(8,128)(2,1)S(1)} %collective-permute-done.4.refs_4_), channel_id=1, source_target_pairs={{0,48},{16,0},{32,16},{48,32},{1,49},{17,1},{33,17},{49,33},{2,50}... | collective-permute-start | bytes 1179656 | tf_op jit(solution)/shard_map/ppermute | solution.py:22
  54.4 31.3 %copy-start.24 = (bf16[16,256,128]{2,1,0:T(8,128)(2,1)}, bf16[16,256,128]{2,1,0:T(8,128)(2,1)S(1)}, u32[]{:S(2)}) copy-start(bf16[16,256,128]{2,1,0:T(8,128)(2,1)S(1)} %shard_map.68.band) | copy-start | bytes 3145732
  54.4 14.9 %collective-permute-start.10 = (bf16[256,768]{1,0:T(8,128)(2,1)S(1)}, bf16[256,768]{1,0:T(8,128)(2,1)S(1)}, u32[]{:S(2)}, u32[]{:S(2)}) collective-permute-start(bf16[256,768]{1,0:T(8,128)(2,1)S(1)} %collective-permute-done.8.refs_0_), channel_id=1, source_target_pairs={{0,48},{16,0},{32,16},{48,32},{1,49},{17,1},{33,17},{49,33},{2,50}... | collective-permute-start | bytes 1179656 | tf_op jit(solution)/shard_map/ppermute | solution.py:22
  55.6 16.4 %collective-permute-start.9 = (bf16[256,768]{1,0:T(8,128)(2,1)S(1)}, bf16[256,768]{1,0:T(8,128)(2,1)S(1)}, u32[]{:S(2)}, u32[]{:S(2)}) collective-permute-start(bf16[256,768]{1,0:T(8,128)(2,1)S(1)} %collective-permute-done.8.refs_0_), channel_id=1, source_target_pairs={{0,16},{16,32},{32,48},{48,0},{1,17},{17,33},{33,49},{49,1},{2,18}... | collective-permute-start | bytes 1179656 | tf_op jit(solution)/shard_map/ppermute | solution.py:22
  61.3 24.4 %copy-start.6 = (bf16[256,768]{1,0:T(8,128)(2,1)}, bf16[256,768]{1,0:T(8,128)(2,1)S(1)}, u32[]{:S(2)}) copy-start(bf16[256,768]{1,0:T(8,128)(2,1)S(1)} %collective-permute-done.5.refs_5_) | copy-start | bytes 1179652
  61.3 38.9 %collective-permute-start.3 = (bf16[256,768]{1,0:T(8,128)(2,1)}, bf16[256,768]{1,0:T(8,128)(2,1)}, u32[]{:S(2)}, u32[]{:S(2)}) collective-permute-start(bf16[256,768]{1,0:T(8,128)(2,1)} %broadcast_select_fusion.5), channel_id=1, source_target_pairs={{0,16},{1,49},{16,32},{17,1},{32,48},{33,17},{48,0},{49,33},{2,18}... | collective-permute-start | bytes 1179656 | tf_op jit(solution)/shard_map/ppermute | solution.py:321
  62.4 23.3 %copy-start.11 = (bf16[256,768]{1,0:T(8,128)(2,1)}, bf16[256,768]{1,0:T(8,128)(2,1)S(1)}, u32[]{:S(2)}) copy-start(bf16[256,768]{1,0:T(8,128)(2,1)S(1)} %collective-permute-done.13.refs_4_) | copy-start | bytes 1179652
  62.4 15.7 %collective-permute-start.14 = (bf16[256,768]{1,0:T(8,128)(2,1)S(1)}, bf16[256,768]{1,0:T(8,128)(2,1)S(1)}, u32[]{:S(2)}, u32[]{:S(2)}) collective-permute-start(bf16[256,768]{1,0:T(8,128)(2,1)S(1)} %collective-permute-done.13.refs_4_), channel_id=1, source_target_pairs={{0,16},{16,32},{32,48},{48,0},{1,17},{17,33},{33,49},{49,1},{2,18}... | collective-permute-start | bytes 1179656 | tf_op jit(solution)/shard_map/ppermute | solution.py:22
  62.8 22.9 %copy-start.8 = (bf16[256,768]{1,0:T(8,128)(2,1)}, bf16[256,768]{1,0:T(8,128)(2,1)S(1)}, u32[]{:S(2)}) copy-start(bf16[256,768]{1,0:T(8,128)(2,1)S(1)} %collective-permute-done.6.refs_6_) | copy-start | bytes 1179652
  62.8 22.1 %collective-permute-start.15 = (bf16[256,768]{1,0:T(8,128)(2,1)S(1)}, bf16[256,768]{1,0:T(8,128)(2,1)S(1)}, u32[]{:S(2)}, u32[]{:S(2)}) collective-permute-start(bf16[256,768]{1,0:T(8,128)(2,1)S(1)} %collective-permute-done.13.refs_4_), channel_id=1, source_target_pairs={{0,48},{16,0},{32,16},{48,32},{1,49},{17,1},{33,17},{49,33},{2,50}... | collective-permute-start | bytes 1179656 | tf_op jit(solution)/shard_map/ppermute | solution.py:22
  69.3 30.9 %collective-permute-start.7 = (bf16[256,768]{1,0:T(8,128)(2,1)}, bf16[256,768]{1,0:T(8,128)(2,1)}, u32[]{:S(2)}, u32[]{:S(2)}) collective-permute-start(bf16[256,768]{1,0:T(8,128)(2,1)} %broadcast_select_fusion.4), channel_id=1, source_target_pairs={{0,16},{1,49},{16,32},{17,1},{32,48},{33,17},{48,0},{49,33},{2,18}... | collective-permute-start | bytes 1179656 | tf_op jit(solution)/shard_map/ppermute | solution.py:321
  86.5 28.5 %collective-permute-start.16 = (bf16[256,768]{1,0:T(8,128)(2,1)}, bf16[256,768]{1,0:T(8,128)(2,1)}, u32[]{:S(2)}, u32[]{:S(2)}) collective-permute-start(bf16[256,768]{1,0:T(8,128)(2,1)} %broadcast_select_fusion.2), channel_id=1, source_target_pairs={{0,16},{1,49},{16,32},{17,1},{32,48},{33,17},{48,0},{49,33},{2,18}... | collective-permute-start | bytes 1179656 | tf_op jit(solution)/shard_map/ppermute | solution.py:321
  105.4 19.7 %collective-permute-start.18 = (bf16[176,256]{1,0:T(8,128)(2,1)S(1)}, bf16[176,256]{1,0:T(8,128)(2,1)S(1)}, u32[]{:S(2)}, u32[]{:S(2)}) collective-permute-start(bf16[176,256]{1,0:T(8,128)(2,1)S(1)} %pad_maximum_fusion.1), channel_id=1, source_target_pairs={{0,8},{8,16},{16,24},{24,32},{32,40},{40,48},{48,56},{56,64},{64,7... | collective-permute-start | bytes 270344 | tf_op jit(solution)/shard_map/ppermute | solution.py:309
  108.3 7.0 %collective-permute-start.12 = (bf16[256,768]{1,0:T(8,128)(2,1)S(1)}, bf16[256,768]{1,0:T(8,128)(2,1)S(1)}, u32[]{:S(2)}, u32[]{:S(2)}) collective-permute-start(bf16[256,768]{1,0:T(8,128)(2,1)S(1)} %copy-done.26), channel_id=1, source_target_pairs={{0,16},{1,49},{16,32},{17,1},{32,48},{33,17},{48,0},{49,33},{2,18}... | collective-permute-start | bytes 1179656 | tf_op jit(solution)/shard_map/ppermute | solution.py:321
  120.1 10.9 %collective-permute-start.17 = (bf16[176,256]{1,0:T(8,128)(2,1)S(1)}, bf16[176,256]{1,0:T(8,128)(2,1)S(1)}, u32[]{:S(2)}, u32[]{:S(2)}) collective-permute-start(bf16[176,256]{1,0:T(8,128)(2,1)S(1)} %pad_maximum_fusion), channel_id=1, source_target_pairs={{0,8},{8,16},{16,24},{24,32},{32,40},{40,48},{48,56},{56,64},{64,7... | collective-permute-start | bytes 270344 | tf_op jit(solution)/shard_map/ppermute | solution.py:309
  (42 other events, 291.0 us)
Sparse Core Ops, SparseCore 0:
  9.7 56.5 all-gather.1

commit v7 on v6

--- a/solution.py
+++ b/solution.py
@@ -313,15 +313,19 @@
     own_projected = lax.dot_general(
         gathered, weight_t, (((1,), (1,)), ((), ())), preferred_element_type=jnp.float32
     ).astype(jnp.bfloat16)
+    (_, mine) = columns[3]
+    mine, own_projected = lax.optimization_barrier((mine, own_projected))
+    columns = (*columns[:3], (columns[3][0], mine))
     rows_of = [spread_rows(mine) for _, mine in columns]
-    onwards = [onward for _, _, onward in rows_of]
-    onwards[2], own_projected = lax.optimization_barrier((onwards[2], own_projected))
     pieces, places = [], []
-    for (by, mine), (below, above, _), onward in zip(columns, rows_of, onwards):
+    half = 8
+    for n, ((by, mine), (below, above, onward)) in enumerate(zip(columns, rows_of)):
+        if n == 2:
+            first_sum = add_product(gathered, pieces, places, None, jnp.float32)
+        if n == 3:
+            onward, first_sum = lax.optimization_barrier((onward, first_sum))
         pieces += [mine, below, above, lax.ppermute(onward, ("x", "core"), fan("x"))]
         places += places_of(by)
-    half = len(pieces) // 2
-    first_sum = add_product(gathered, pieces[:half], places[:half], None, jnp.float32)
     first_sum, own_projected = lax.optimization_barrier((first_sum, own_projected))
     other_halo = halo_of(own_projected, own_short)
     own_band, other_band = banded(long_filter), banded(other_long)

time: 164 us -> 153 us (0.933)
  the two profiles are of different devices: /device:TPU:1 before, /device:TPU:2 now
where the time goes in v7:
time: 153 us; the launch traced here: 152 us
  starting transfers between devices  37.8 us (25%)
  Pallas kernels  22.6 us (15%)
  local copies, waits for them, and re-layouts  21.3 us (14%)
  blocking collectives  19.5 us (13%)
  waiting for transfers between devices  16.5 us (11%)
  between operations  14.1 us (9%)
  matrix products  11.1 us (7%)
  other arithmetic  9.6 us (6%)
    all_to_all x1, blocking collectives, per_device(): lax.all_to_all(gated, ('y', 'core'), split_axis=0, concat_axis=0, tiled=T...  19.5 us
    pallas_call x3, Pallas kernels, mix_conv(): pl.pallas_call(body, out_shape=jax.ShapeDtypeStruct((length, 2 * channels...  11.9 us
    dot_general x1, matrix products, per_device(): lax.dot_general(gathered, weight_t, (((1,), (1,)), ((), ())), preferred_e...  11.1 us
    ppermute x2, starting transfers between devices, halo_of(): lax.ppermute(tail_of(projected, short, starts), ('z_lo', 'x', 'z_hi'), ne...  10.5 us
    pallas_call x2, Pallas kernels, add_product(): pl.pallas_call(functools.partial(add_product_kernel, count), out_shape=ja...  8.95 us
    optimization_barrier x1, local copies, waits for them, and re-layouts, per_device(): in_weight, normed = lax.optimization_barrier((in_weight, normed))  8.81 us
    ppermute x8, waiting for transfers between devices, shift(): lax.ppermute(value, axis, [(i, (i + by) % size) for i in range(size)])  8.78 us
    ppermute x8, starting transfers between devices, shift(): lax.ppermute(value, axis, [(i, (i + by) % size) for i in range(size)])  8.35 us
  transfers between devices with their start and end apart: 20, of which 6 were waited for; matrix products, arithmetic and copies ran while one was open for 23% of the time, Pallas kernels for 12%

profile of v7, /device:TPU:2, one launch (start us, length us, event | category | flops | bytes accessed | tf_op | source)
XLA Modules:
  0.0 152.5 jit_solution(3880719014914955423)
XLA Ops:
  10.4 6.4 %collective-permute-start = (bf16[256,768]{1,0:T(8,128)(2,1)S(1)}, bf16[256,768]{1,0:T(8,128)(2,1)S(1)}, u32[]{:S(2)}, u32[]{:S(2)}) collective-permute-start(bf16[256,768]{1,0:T(8,128)(2,1)S(1)} %copy.24), channel_id=1, source_target_pairs={{0,136},{8,128},{64,200},{72,192},{128,8},{136,0},{192,72},{200,64... | collective-permute-start | bytes 1179656 | tf_op jit(solution)/shard_map/ppermute | solution.py:55
  17.8 8.8 %copy.25 = bf16[4096,3,256]{0,2,1:T(8,128)(2,1)} copy(bf16[4096,3,256]{2,0,1:T(8,128)(2,1)} %param.8) | data formatting | bytes 12582912 | tf_op jit(solution)/shard_map/optimization_barrier | solution.py:292
  30.6 1.9 %constant_dynamic-slice_fusion = (bf16[256,3,256]{0,2,1:T(8,128)(2,1)}, bf16[256,3,256]{0,2,1:T(8,128)(2,1)S(1)}) fusion(bf16[4096,3,256]{0,2,1:T(8,128)(2,1)} %copy.25, s32[]{:T(128)S(6)} %select_n.159, s32[]{:T(128)S(6)} %select_n.157), kind=kLoop, calls=%fused_computation.25 | loop fusion | bytes 1572872 | tf_op jit(solution)/shard_map/dynamic_slice | solution.py:283
  38.3 2.1 %collective-permute-start.2 = (bf16[256,768]{1,0:T(8,128)(2,1)}, bf16[256,768]{1,0:T(8,128)(2,1)S(1)}, u32[]{:S(2)}, u32[]{:S(2)}) collective-permute-start(bf16[256,768]{1,0:T(8,128)(2,1)} %get-tuple-element.47), channel_id=1, source_target_pairs={{0,200},{8,192},{64,0},{72,8},{128,64},{136,72},{192,128},{200,136... | collective-permute-start | bytes 1179656 | tf_op jit(solution)/shard_map/ppermute | solution.py:65
  44.2 1.9 %copy.30 = bf16[256,768]{1,0:T(8,128)(2,1)} copy(bf16[256,768]{0,1:T(8,128)(2,1)} %bitcast.56) | data formatting | bytes 786432 | tf_op jit(solution)/shard_map/optimization_barrier | solution.py:297
  46.2 3.0 %collective-permute-done.1.refs_4_ = bf16[256,768]{1,0:T(8,128)(2,1)S(1)} collective-permute-done((bf16[256,768]{1,0:T(8,128)(2,1)}, bf16[256,768]{1,0:T(8,128)(2,1)S(1)}, u32[]{:S(2)}, u32[]{:S(2)}) %collective-permute-start.1) | collective-permute-done | bytes 393248 | tf_op jit(solution)/shard_map/ppermute | solution.py:65
  51.2 1.8 %select_select_fusion = bf16[256,768]{1,0:T(8,128)(2,1)} fusion(bf16[256,768]{1,0:T(8,128)(2,1)} %copy.30, bf16[256,768]{1,0:T(8,128)(2,1)S(1)} %collective-permute-done.1.refs_4_, bf16[256,768]{1,0:T(8,128)(2,1)S(1)} %collective-permute-done.2.refs_0_, pred[]{:T(512)S(6)} %eq.37, pred[]{:T(512)S(6)} %or.3), kind=kLoop, calls=%fused_computation.6 | loop fusion | flops 393216 | bytes 1572866 | tf_op jit(solution)/shard_map/jit(_where)/select_n | solution.py:78
  53.0 1.7 %collective-permute-start.3 = (bf16[256,768]{1,0:T(8,128)(2,1)}, bf16[256,768]{1,0:T(8,128)(2,1)}, u32[]{:S(2)}, u32[]{:S(2)}) collective-permute-start(bf16[256,768]{1,0:T(8,128)(2,1)} %select_select_fusion), channel_id=1, source_target_pairs={{64,128},{128,64},{0,200},{192,8},{72,136},{136,72},{8,192},{200,0... | collective-permute-start | bytes 1179656 | tf_op jit(solution)/shard_map/ppermute | solution.py:79
  58.3 2.8 %collective-permute-done.9.refs_5_ = bf16[256,768]{1,0:T(8,128)(2,1)S(1)} collective-permute-done((bf16[256,768]{1,0:T(8,128)(2,1)S(1)}, bf16[256,768]{1,0:T(8,128)(2,1)S(1)}, u32[]{:S(2)}, u32[]{:S(2)}) %collective-permute-start.9) | collective-permute-done | bytes 393248 | tf_op jit(solution)/shard_map/ppermute | solution.py:22
  65.6 11.1 %convolution_convert_fusion.refs_1_.proj = bf16[1024,768]{1,0:T(8,128)(2,1)S(1)} fusion(bf16[1024,4096]{1,0:T(8,128)(2,1)} %all-gather.2.cloned.1.call-done.left, bf16[768,4096]{1,0:T(8,128)(2,1)} %bitcast.54), kind=kOutput, calls=%fused_computation.5 | convolution fusion | flops 6443237376 | bytes 16252928 | tf_op jit(solution)/shard_map/dot_general | solution.py:313
  76.7 1.7 %collective-permute-start.4 = (bf16[256,768]{1,0:T(8,128)(2,1)}, bf16[256,768]{1,0:T(8,128)(2,1)S(1)}, u32[]{:S(2)}, u32[]{:S(2)}) collective-permute-start(bf16[256,768]{1,0:T(8,128)(2,1)} %collective-permute-done.3.refs_4_), channel_id=1, source_target_pairs={{0,16},{16,32},{32,48},{48,0},{1,17},{17,33},{33,49},{49,1},{2,18}... | collective-permute-start | bytes 1179656 | tf_op jit(solution)/shard_map/ppermute | solution.py:22
  78.9 1.7 %collective-permute-start.15 = (bf16[256,768]{1,0:T(8,128)(2,1)S(1)}, bf16[256,768]{1,0:T(8,128)(2,1)S(1)}, u32[]{:S(2)}, u32[]{:S(2)}) collective-permute-start(bf16[256,768]{1,0:T(8,128)(2,1)S(1)} %broadcast_select_fusion.2), channel_id=1, source_target_pairs={{0,16},{1,49},{16,32},{17,1},{32,48},{33,17},{48,0},{49,33},{2,18}... | collective-permute-start | bytes 1179656 | tf_op jit(solution)/shard_map/ppermute | solution.py:327
  80.7 4.5 %shard_map.64.refs_8_ = f32[1024,768]{1,0:T(8,128)S(1)} custom-call(s32[8]{0:T(128)S(1)} %copy-done.15, bf16[1024,4096]{1,0:T(8,128)(2,1)S(1)} %copy-done, bf16[256,768]{1,0:T(8,128)(2,1)S(1)} %collective-permute-done.refs_0_, bf16[256,768]{1,0:T(8,128)(2,1)S(1)} %collective-permute-done.6.refs_1_, bf16[256,768]{1,0:T(8,128)(2,1)S(1)} %copy-done.3, ...), custom_call_target="tpu_custom_call" | custom-call | flops 3221225472 | bytes 8000000 | tf_op jit(solution)/shard_map/pallas_call | solution.py:115
  85.3 3.0 %collective-permute-done.4.refs_5_ = bf16[256,768]{1,0:T(8,128)(2,1)S(1)} collective-permute-done((bf16[256,768]{1,0:T(8,128)(2,1)}, bf16[256,768]{1,0:T(8,128)(2,1)S(1)}, u32[]{:S(2)}, u32[]{:S(2)}) %collective-permute-start.4) | collective-permute-done | bytes 393248 | tf_op jit(solution)/shard_map/ppermute | solution.py:22
  88.3 2.4 %collective-permute-done.5.refs_6_ = bf16[256,768]{1,0:T(8,128)(2,1)S(1)} collective-permute-done((bf16[256,768]{1,0:T(8,128)(2,1)}, bf16[256,768]{1,0:T(8,128)(2,1)S(1)}, u32[]{:S(2)}, u32[]{:S(2)}) %collective-permute-start.5) | collective-permute-done | bytes 393248 | tf_op jit(solution)/shard_map/ppermute | solution.py:22
  90.7 1.7 %collective-permute-start.16 = (bf16[256,768]{1,0:T(8,128)(2,1)S(1)}, bf16[256,768]{1,0:T(8,128)(2,1)S(1)}, u32[]{:S(2)}, u32[]{:S(2)}) collective-permute-start(bf16[256,768]{1,0:T(8,128)(2,1)S(1)} %broadcast_select_fusion.5), channel_id=1, source_target_pairs={{0,16},{1,49},{16,32},{17,1},{32,48},{33,17},{48,0},{49,33},{2,18}... | collective-permute-start | bytes 1179656 | tf_op jit(solution)/shard_map/ppermute | solution.py:327
  92.6 4.6 %shard_map.66.into = bf16[1024,512]{1,0:T(8,128)(2,1)S(1)} custom-call(s32[8]{0:T(128)S(1)} %copy-done.17, bf16[1024,768]{1,0:T(8,128)(2,1)S(1)} %convolution_convert_fusion.refs_1_.proj, bf16[176,256]{1,0:T(8,128)(2,1)S(1)} %broadcast_in_dim.96.refs_2_, f32[9,256]{1,0:T(8,128)S(1)} %copy-done.11, bf16[16,256,128]{2,1,0:T(8,128)(2,1)S(1)} %copy-done.19, ...), custom_call_target="tpu_custom_call" | custom-call | flops 6144000000 | bytes 4000000 | tf_op jit(solution)/shard_map/pallas_call | solution.py:231
  97.5 8.6 %collective-permute-start.18 = (bf16[176,256]{1,0:T(8,128)(2,1)S(1)}, bf16[176,256]{1,0:T(8,128)(2,1)S(1)}, u32[]{:S(2)}, u32[]{:S(2)}) collective-permute-start(bf16[176,256]{1,0:T(8,128)(2,1)S(1)} %pad_maximum_fusion.1), channel_id=1, source_target_pairs={{0,8},{8,16},{16,24},{24,32},{32,40},{40,48},{48,56},{56,64},{64,7... | collective-permute-start | bytes 270344 | tf_op jit(solution)/shard_map/ppermute | solution.py:309
  106.2 4.4 %shard_map.67.proj = bf16[1024,768]{1,0:T(8,128)(2,1)S(1)} custom-call(s32[8]{0:T(128)S(1)} %copy-done.14, bf16[1024,4096]{1,0:T(8,128)(2,1)S(1)} %copy-done, bf16[256,768]{1,0:T(8,128)(2,1)S(1)} %collective-permute-done.2.refs_0_, bf16[256,768]{1,0:T(8,128)(2,1)S(1)} %collective-permute-done.13.refs_1_, ...), custom_call_target="tpu_custom_call" | custom-call | flops 3221225472 | bytes 8000000 | tf_op jit(solution)/shard_map/pallas_call | solution.py:115
  110.9 1.9 %collective-permute-start.17 = (bf16[176,256]{1,0:T(8,128)(2,1)S(1)}, bf16[176,256]{1,0:T(8,128)(2,1)S(1)}, u32[]{:S(2)}, u32[]{:S(2)}) collective-permute-start(bf16[176,256]{1,0:T(8,128)(2,1)S(1)} %pad_maximum_fusion), channel_id=1, source_target_pairs={{0,8},{8,16},{16,24},{24,32},{32,40},{40,48},{48,56},{56,64},{64,7... | collective-permute-start | bytes 270344 | tf_op jit(solution)/shard_map/ppermute | solution.py:309
  112.8 4.6 %shard_map.69.into = bf16[1024,512]{1,0:T(8,128)(2,1)S(1)} custom-call(s32[8]{0:T(128)S(1)} %copy-done.17, bf16[1024,768]{1,0:T(8,128)(2,1)S(1)} %shard_map.67.proj, bf16[176,256]{1,0:T(8,128)(2,1)S(1)} %collective-permute-done.18.halo, f32[9,256]{1,0:T(8,128)S(1)} %slice_convert_fusion.short, ...), custom_call_target="tpu_custom_call", output_to_operand_aliasing={{}: (7, {})} | custom-call | flops 6144000000 | bytes 4000000 | tf_op jit(solution)/shard_map/pallas_call | solution.py:231
  117.5 4.6 %collective-permute-done.17.halo = bf16[176,256]{1,0:T(8,128)(2,1)S(1)} collective-permute-done((bf16[176,256]{1,0:T(8,128)(2,1)S(1)}, bf16[176,256]{1,0:T(8,128)(2,1)S(1)}, u32[]{:S(2)}, u32[]{:S(2)}) %collective-permute-start.17) | collective-permute-done | bytes 90144 | tf_op jit(solution)/shard_map/ppermute | solution.py:309
  122.1 2.7 %shard_map.70 = bf16[1024,512]{1,0:T(8,128)(2,1)S(1)} custom-call(s32[2]{0:T(128)S(1)} %copy-done.16, bf16[1024,768]{1,0:T(8,128)(2,1)S(1)} %convolution_convert_fusion.refs_1_.proj, bf16[176,256]{1,0:T(8,128)(2,1)S(1)} %collective-permute-done.17.halo, f32[9,256]{1,0:T(8,128)S(1)} %copy-done.11, ...), custom_call_target="tpu_custom_call", output_to_operand_aliasing={{}: (7, {})} | custom-call | flops 1536000000 | bytes 4000000 | tf_op jit(solution)/shard_map/pallas_call | solution.py:231
  124.8 19.5 %all_to_all.11 = bf16[8,128,512]{2,1,0:T(8,128)(2,1)S(1)} all-to-all(bf16[8,128,512]{2,1,0:T(8,128)(2,1)S(1)} %bitcast.48), channel_id=1, replica_groups=mesh['z_lo'=4,'x'=4,'z_hi'=2,'y'=4,'core'=2] {'y','core'}, dimensions={0} | all-to-all | bytes 2097152 | tf_op jit(solution)/shard_map/all_to_all | solution.py:339
  (153 shorter events, 30.6 us)
Async XLA Ops:
  6.5 59.0 %all-gather.2.cloned.1.call-start = ((), (), s32[]{:S(2)}) async-start(), calls=%async_computation.1 | async-start | bytes 9437184 | tf_op jit(solution)/shard_map/all_gather | solution.py:293
  10.4 25.2 %collective-permute-start = (bf16[256,768]{1,0:T(8,128)(2,1)S(1)}, bf16[256,768]{1,0:T(8,128)(2,1)S(1)}, u32[]{:S(2)}, u32[]{:S(2)}) collective-permute-start(bf16[256,768]{1,0:T(8,128)(2,1)S(1)} %copy.24), channel_id=1, source_target_pairs={{0,136},{8,128},{64,200},{72,192},{128,8},{136,0},{192,72},{200,64... | collective-permute-start | bytes 1179656 | tf_op jit(solution)/shard_map/ppermute | solution.py:55
  16.8 18.8 %collective-permute-start.12 = (bf16[17,256]{1,0:T(8,128)(2,1)S(1)}, bf16[17,256]{1,0:T(8,128)(2,1)S(1)}, u32[]{:S(2)}, u32[]{:S(2)}) collective-permute-start(bf16[17,256]{1,0:T(8,128)(2,1)S(1)} %pad_maximum_fusion.2), channel_id=1, source_target_pairs={{0,8},{8,0},{1,9},{9,1},{2,10},{10,2},{3,11},{11,3},{4,12},{12,4},... | collective-permute-start | bytes 26120 | tf_op jit(solution)/shard_map/ppermute | solution.py:17
  36.7 12.4 %collective-permute-start.1 = (bf16[256,768]{1,0:T(8,128)(2,1)}, bf16[256,768]{1,0:T(8,128)(2,1)S(1)}, u32[]{:S(2)}, u32[]{:S(2)}) collective-permute-start(bf16[256,768]{1,0:T(8,128)(2,1)} %get-tuple-element.48), channel_id=1, source_target_pairs={{0,64},{8,72},{64,128},{72,136},{128,192},{136,200},{192,8},{200,0... | collective-permute-start | bytes 1179656 | tf_op jit(solution)/shard_map/ppermute | solution.py:65
  38.3 12.9 %collective-permute-start.2 = (bf16[256,768]{1,0:T(8,128)(2,1)}, bf16[256,768]{1,0:T(8,128)(2,1)S(1)}, u32[]{:S(2)}, u32[]{:S(2)}) collective-permute-start(bf16[256,768]{1,0:T(8,128)(2,1)} %get-tuple-element.47), channel_id=1, source_target_pairs={{0,200},{8,192},{64,0},{72,8},{128,64},{136,72},{192,128},{200,136... | collective-permute-start | bytes 1179656 | tf_op jit(solution)/shard_map/ppermute | solution.py:65
  41.0 13.7 %collective-permute-start.6 = (bf16[256,768]{1,0:T(8,128)(2,1)S(1)}, bf16[256,768]{1,0:T(8,128)(2,1)S(1)}, u32[]{:S(2)}, u32[]{:S(2)}) collective-permute-start(bf16[256,768]{1,0:T(8,128)(2,1)S(1)} %collective-permute-done.refs_0_), channel_id=1, source_target_pairs={{0,16},{16,32},{32,48},{48,0},{1,17},{17,33},{33,49},{49,1},{2,18}... | collective-permute-start | bytes 1179656 | tf_op jit(solution)/shard_map/ppermute | solution.py:22
  42.5 12.3 %collective-permute-start.7 = (bf16[256,768]{1,0:T(8,128)(2,1)S(1)}, bf16[256,768]{1,0:T(8,128)(2,1)S(1)}, u32[]{:S(2)}, u32[]{:S(2)}) collective-permute-start(bf16[256,768]{1,0:T(8,128)(2,1)S(1)} %collective-permute-done.refs_0_), channel_id=1, source_target_pairs={{0,48},{16,0},{32,16},{48,32},{1,49},{17,1},{33,17},{49,33},{2,50}... | collective-permute-start | bytes 1179656 | tf_op jit(solution)/shard_map/ppermute | solution.py:22
  49.1 12.1 %collective-permute-start.9 = (bf16[256,768]{1,0:T(8,128)(2,1)S(1)}, bf16[256,768]{1,0:T(8,128)(2,1)S(1)}, u32[]{:S(2)}, u32[]{:S(2)}) collective-permute-start(bf16[256,768]{1,0:T(8,128)(2,1)S(1)} %collective-permute-done.1.refs_4_), channel_id=1, source_target_pairs={{0,16},{16,32},{32,48},{48,0},{1,17},{17,33},{33,49},{49,1},{2,18}... | collective-permute-start | bytes 1179656 | tf_op jit(solution)/shard_map/ppermute | solution.py:22
  50.6 12.1 %collective-permute-start.10 = (bf16[256,768]{1,0:T(8,128)(2,1)S(1)}, bf16[256,768]{1,0:T(8,128)(2,1)S(1)}, u32[]{:S(2)}, u32[]{:S(2)}) collective-permute-start(bf16[256,768]{1,0:T(8,128)(2,1)S(1)} %collective-permute-done.1.refs_4_), channel_id=1, source_target_pairs={{0,48},{16,0},{32,16},{48,32},{1,49},{17,1},{33,17},{49,33},{2,50}... | collective-permute-start | bytes 1179656 | tf_op jit(solution)/shard_map/ppermute | solution.py:22
  53.0 23.7 %collective-permute-start.3 = (bf16[256,768]{1,0:T(8,128)(2,1)}, bf16[256,768]{1,0:T(8,128)(2,1)}, u32[]{:S(2)}, u32[]{:S(2)}) collective-permute-start(bf16[256,768]{1,0:T(8,128)(2,1)} %select_select_fusion), channel_id=1, source_target_pairs={{64,128},{128,64},{0,200},{192,8},{72,136},{136,72},{8,192},{200,0... | collective-permute-start | bytes 1179656 | tf_op jit(solution)/shard_map/ppermute | solution.py:79
  55.7 25.0 %collective-permute-start.8 = (bf16[256,768]{1,0:T(8,128)(2,1)}, bf16[256,768]{1,0:T(8,128)(2,1)}, u32[]{:S(2)}, u32[]{:S(2)}) collective-permute-start(bf16[256,768]{1,0:T(8,128)(2,1)} %broadcast_select_fusion.4), channel_id=1, source_target_pairs={{0,16},{1,49},{16,32},{17,1},{32,48},{33,17},{48,0},{49,33},{2,18}... | collective-permute-start | bytes 1179656 | tf_op jit(solution)/shard_map/ppermute | solution.py:327
  57.1 21.3 %collective-permute-start.13 = (bf16[256,768]{1,0:T(8,128)(2,1)S(1)}, bf16[256,768]{1,0:T(8,128)(2,1)S(1)}, u32[]{:S(2)}, u32[]{:S(2)}) collective-permute-start(bf16[256,768]{1,0:T(8,128)(2,1)S(1)} %collective-permute-done.2.refs_0_), channel_id=1, source_target_pairs={{0,16},{16,32},{32,48},{48,0},{1,17},{17,33},{33,49},{49,1},{2,18}... | collective-permute-start | bytes 1179656 | tf_op jit(solution)/shard_map/ppermute | solution.py:22
  61.2 17.7 %collective-permute-start.14 = (bf16[256,768]{1,0:T(8,128)(2,1)S(1)}, bf16[256,768]{1,0:T(8,128)(2,1)S(1)}, u32[]{:S(2)}, u32[]{:S(2)}) collective-permute-start(bf16[256,768]{1,0:T(8,128)(2,1)S(1)} %collective-permute-done.2.refs_0_), channel_id=1, source_target_pairs={{0,48},{16,0},{32,16},{48,32},{1,49},{17,1},{33,17},{49,33},{2,50}... | collective-permute-start | bytes 1179656 | tf_op jit(solution)/shard_map/ppermute | solution.py:22
  64.3 16.3 %collective-permute-start.11 = (bf16[256,768]{1,0:T(8,128)(2,1)}, bf16[256,768]{1,0:T(8,128)(2,1)}, u32[]{:S(2)}, u32[]{:S(2)}) collective-permute-start(bf16[256,768]{1,0:T(8,128)(2,1)} %broadcast_select_fusion.3), channel_id=1, source_target_pairs={{0,16},{1,49},{16,32},{17,1},{32,48},{33,17},{48,0},{49,33},{2,18}... | collective-permute-start | bytes 1179656 | tf_op jit(solution)/shard_map/ppermute | solution.py:327
  65.6 15.1 %copy-start.5 = (bf16[256,768]{1,0:T(8,128)(2,1)S(1)}, bf16[256,768]{1,0:T(8,128)(2,1)}, u32[]{:S(2)}) copy-start(bf16[256,768]{1,0:T(8,128)(2,1)} %copy-done.4) | copy-start | bytes 1179652
  65.6 15.1 %copy-start.7 = (bf16[256,768]{1,0:T(8,128)(2,1)S(1)}, bf16[256,768]{1,0:T(8,128)(2,1)}, u32[]{:S(2)}) copy-start(bf16[256,768]{1,0:T(8,128)(2,1)} %copy-done.6) | copy-start | bytes 1179652
  65.6 15.2 %copy-start.15 = (s32[8]{0:T(128)S(1)}, s32[8]{0:T(128)}, u32[]{:S(2)}) copy-start(s32[8]{0:T(128)} %stack.62.places) | copy-start | bytes 100
  76.7 11.6 %collective-permute-start.4 = (bf16[256,768]{1,0:T(8,128)(2,1)}, bf16[256,768]{1,0:T(8,128)(2,1)S(1)}, u32[]{:S(2)}, u32[]{:S(2)}) collective-permute-start(bf16[256,768]{1,0:T(8,128)(2,1)} %collective-permute-done.3.refs_4_), channel_id=1, source_target_pairs={{0,16},{16,32},{32,48},{48,0},{1,17},{17,33},{33,49},{49,1},{2,18}... | collective-permute-start | bytes 1179656 | tf_op jit(solution)/shard_map/ppermute | solution.py:22
  78.5 12.2 %collective-permute-start.5 = (bf16[256,768]{1,0:T(8,128)(2,1)}, bf16[256,768]{1,0:T(8,128)(2,1)S(1)}, u32[]{:S(2)}, u32[]{:S(2)}) collective-permute-start(bf16[256,768]{1,0:T(8,128)(2,1)} %collective-permute-done.3.refs_4_), channel_id=1, source_target_pairs={{0,48},{16,0},{32,16},{48,32},{1,49},{17,1},{33,17},{49,33},{2,50}... | collective-permute-start | bytes 1179656 | tf_op jit(solution)/shard_map/ppermute | solution.py:22
  78.9 27.2 %collective-permute-start.15 = (bf16[256,768]{1,0:T(8,128)(2,1)S(1)}, bf16[256,768]{1,0:T(8,128)(2,1)S(1)}, u32[]{:S(2)}, u32[]{:S(2)}) collective-permute-start(bf16[256,768]{1,0:T(8,128)(2,1)S(1)} %broadcast_select_fusion.2), channel_id=1, source_target_pairs={{0,16},{1,49},{16,32},{17,1},{32,48},{33,17},{48,0},{49,33},{2,18}... | collective-permute-start | bytes 1179656 | tf_op jit(solution)/shard_map/ppermute | solution.py:327
  90.7 15.4 %collective-permute-start.16 = (bf16[256,768]{1,0:T(8,128)(2,1)S(1)}, bf16[256,768]{1,0:T(8,128)(2,1)S(1)}, u32[]{:S(2)}, u32[]{:S(2)}) collective-permute-start(bf16[256,768]{1,0:T(8,128)(2,1)S(1)} %broadcast_select_fusion.5), channel_id=1, source_target_pairs={{0,16},{1,49},{16,32},{17,1},{32,48},{33,17},{48,0},{49,33},{2,18}... | collective-permute-start | bytes 1179656 | tf_op jit(solution)/shard_map/ppermute | solution.py:327
  97.5 15.3 %copy-start.21 = (bf16[16,256,128]{2,1,0:T(8,128)(2,1)S(1)}, bf16[16,256,128]{2,1,0:T(8,128)(2,1)}, u32[]{:S(2)}) copy-start(bf16[16,256,128]{2,1,0:T(8,128)(2,1)} %copy-done.20) | copy-start | bytes 3145732
  97.5 15.3 %collective-permute-start.18 = (bf16[176,256]{1,0:T(8,128)(2,1)S(1)}, bf16[176,256]{1,0:T(8,128)(2,1)S(1)}, u32[]{:S(2)}, u32[]{:S(2)}) collective-permute-start(bf16[176,256]{1,0:T(8,128)(2,1)S(1)} %pad_maximum_fusion.1), channel_id=1, source_target_pairs={{0,8},{8,16},{16,24},{24,32},{32,40},{40,48},{48,56},{56,64},{64,7... | collective-permute-start | bytes 270344 | tf_op jit(solution)/shard_map/ppermute | solution.py:309
  110.9 11.2 %collective-permute-start.17 = (bf16[176,256]{1,0:T(8,128)(2,1)S(1)}, bf16[176,256]{1,0:T(8,128)(2,1)S(1)}, u32[]{:S(2)}, u32[]{:S(2)}) collective-permute-start(bf16[176,256]{1,0:T(8,128)(2,1)S(1)} %pad_maximum_fusion), channel_id=1, source_target_pairs={{0,8},{8,16},{16,24},{24,32},{32,40},{40,48},{48,56},{56,64},{64,7... | collective-permute-start | bytes 270344 | tf_op jit(solution)/shard_map/ppermute | solution.py:309
  (36 other events, 300.5 us)
Sparse Core Ops, SparseCore 0:
  10.3 55.2 all-gather.1

commit v8 on v7

--- a/solution.py
+++ b/solution.py
@@ -77,7 +77,7 @@
         pairs += [(2 * 0 + h, 2 * 3 + 1 - h), (2 * 3 + h, 2 * 0 + 1 - h)]
     onward = jnp.where(jnp.logical_or(top, bottom), ends[1], jnp.where(z_lo == 1, up, down))
     opposite = lax.ppermute(onward, ("z_lo", "z_hi"), pairs)
-    return (0, piece), (1, up), (-1, down), (2, opposite)
+    return piece, up, down, opposite
 
 
 def spread_rows(mine):
@@ -310,23 +310,21 @@
 
     own_short = short_filter.reshape(3 * taps, channels).astype(jnp.float32)
     other_short = other_short.astype(jnp.float32)
+    late, gathered = lax.optimization_barrier((columns[2:], gathered))
+    columns = (*columns[:2], *late)
     own_projected = lax.dot_general(
         gathered, weight_t, (((1,), (1,)), ((), ())), preferred_element_type=jnp.float32
     ).astype(jnp.bfloat16)
-    (_, mine) = columns[3]
-    mine, own_projected = lax.optimization_barrier((mine, own_projected))
-    columns = (*columns[:3], (columns[3][0], mine))
-    rows_of = [spread_rows(mine) for _, mine in columns]
+    rows_of = [spread_rows(mine) for mine in columns]
     pieces, places = [], []
     half = 8
-    for n, ((by, mine), (below, above, onward)) in enumerate(zip(columns, rows_of)):
+    for n, (by, mine, (below, above, onward)) in enumerate(zip((0, 1, -1, 2), columns, rows_of)):
         if n == 2:
             first_sum = add_product(gathered, pieces, places, None, jnp.float32)
         if n == 3:
-            onward, first_sum = lax.optimization_barrier((onward, first_sum))
+            onward, own_projected = lax.optimization_barrier((onward, own_projected))
         pieces += [mine, below, above, lax.ppermute(onward, ("x", "core"), fan("x"))]
         places += places_of(by)
-    first_sum, own_projected = lax.optimization_barrier((first_sum, own_projected))
     other_halo = halo_of(own_projected, own_short)
     own_band, other_band = banded(long_filter), banded(other_long)
     nothing = jnp.zeros((SPAN + 3 * RIM, channels), jnp.bfloat16)

time: 153 us -> 156 us (1.020)
  the two profiles are of different devices: /device:TPU:2 before, /device:TPU:1 now
where the time goes in v8:
time: 156 us; the launch traced here: 154 us
  starting transfers between devices  42.8 us (27%)
  blocking collectives  23.1 us (15%)
  Pallas kernels  22.5 us (14%)
  local copies, waits for them, and re-layouts  21.2 us (14%)
  between operations  14.2 us (9%)
  matrix products  11.1 us (7%)
  waiting for transfers between devices  10.3 us (7%)
  other arithmetic  8.64 us (6%)
    all_to_all x1, blocking collectives, per_device(): lax.all_to_all(gated, ('y', 'core'), split_axis=0, concat_axis=0, tiled=T...  23.1 us
    ppermute x2, starting transfers between devices, halo_of(): lax.ppermute(tail_of(projected, short, starts), ('z_lo', 'x', 'z_hi'), ne...  13.9 us
    pallas_call x3, Pallas kernels, mix_conv(): pl.pallas_call(body, out_shape=jax.ShapeDtypeStruct((length, 2 * channels...  11.8 us
    dot_general x1, matrix products, per_device(): lax.dot_general(gathered, weight_t, (((1,), (1,)), ((), ())), preferred_e...  11.1 us
    ppermute x8, starting transfers between devices, shift(): lax.ppermute(value, axis, [(i, (i + by) % size) for i in range(size)])  10.8 us
    pallas_call x2, Pallas kernels, add_product(): pl.pallas_call(functools.partial(add_product_kernel, count), out_shape=ja...  8.95 us
    optimization_barrier x1, local copies, waits for them, and re-layouts, per_device(): in_weight, normed = lax.optimization_barrier((in_weight, normed))  8.81 us
    ppermute x4, starting transfers between devices, per_device(): lax.ppermute(onward, ('x', 'core'), fan('x'))  6.94 us
  transfers between devices with their start and end apart: 20, of which 3 were waited for; matrix products, arithmetic and copies ran while one was open for 22% of the time, Pallas kernels for 12%

profile of v8, /device:TPU:1, one launch (start us, length us, event | category | flops | bytes accessed | tf_op | source)
XLA Modules:
  0.0 153.9 jit_solution(3766254242625586418)
XLA Ops:
  10.4 6.9 %collective-permute-start = (bf16[256,768]{1,0:T(8,128)(2,1)S(1)}, bf16[256,768]{1,0:T(8,128)(2,1)S(1)}, u32[]{:S(2)}, u32[]{:S(2)}) collective-permute-start(bf16[256,768]{1,0:T(8,128)(2,1)S(1)} %copy.24), channel_id=1, source_target_pairs={{0,136},{8,128},{64,200},{72,192},{128,8},{136,0},{192,72},{200,64... | collective-permute-start | bytes 1179656 | tf_op jit(solution)/shard_map/ppermute | solution.py:55
  18.4 8.8 %copy.25 = bf16[4096,3,256]{0,2,1:T(8,128)(2,1)} copy(bf16[4096,3,256]{2,0,1:T(8,128)(2,1)} %param.8) | data formatting | bytes 12582912 | tf_op jit(solution)/shard_map/optimization_barrier | solution.py:292
  31.1 1.9 %constant_dynamic-slice_fusion = (bf16[256,3,256]{0,2,1:T(8,128)(2,1)}, bf16[256,3,256]{0,2,1:T(8,128)(2,1)S(1)}) fusion(bf16[4096,3,256]{0,2,1:T(8,128)(2,1)} %copy.25, s32[]{:T(128)S(6)} %select_n.159, s32[]{:T(128)S(6)} %select_n.157), kind=kLoop, calls=%fused_computation.25 | loop fusion | bytes 1572872 | tf_op jit(solution)/shard_map/dynamic_slice | solution.py:283
  37.2 3.1 %collective-permute-start.1 = (bf16[256,768]{1,0:T(8,128)(2,1)}, bf16[256,768]{1,0:T(8,128)(2,1)S(1)}, u32[]{:S(2)}, u32[]{:S(2)}) collective-permute-start(bf16[256,768]{1,0:T(8,128)(2,1)} %get-tuple-element.46), channel_id=1, source_target_pairs={{0,200},{8,192},{64,0},{72,8},{128,64},{136,72},{192,128},{200,136... | collective-permute-start | bytes 1179656 | tf_op jit(solution)/shard_map/ppermute | solution.py:65
  42.2 1.5 collective-permute-start.12
  44.8 1.9 %copy.30 = bf16[256,768]{1,0:T(8,128)(2,1)} copy(bf16[256,768]{0,1:T(8,128)(2,1)} %bitcast.56) | data formatting | bytes 786432 | tf_op jit(solution)/shard_map/optimization_barrier | solution.py:297
  46.7 4.2 %collective-permute-done.2.refs_4_ = bf16[256,768]{1,0:T(8,128)(2,1)S(1)} collective-permute-done((bf16[256,768]{1,0:T(8,128)(2,1)}, bf16[256,768]{1,0:T(8,128)(2,1)S(1)}, u32[]{:S(2)}, u32[]{:S(2)}) %collective-permute-start.2) | collective-permute-done | bytes 393248 | tf_op jit(solution)/shard_map/ppermute | solution.py:65
  52.2 1.5 collective-permute-start.15
  56.9 3.7 %collective-permute-done.14.refs_5_ = bf16[256,768]{1,0:T(8,128)(2,1)S(1)} collective-permute-done((bf16[256,768]{1,0:T(8,128)(2,1)S(1)}, bf16[256,768]{1,0:T(8,128)(2,1)S(1)}, u32[]{:S(2)}, u32[]{:S(2)}) %collective-permute-start.14) | collective-permute-done | bytes 393248 | tf_op jit(solution)/shard_map/ppermute | solution.py:22
  62.1 2.4 %collective-permute-start.16 = (bf16[256,768]{1,0:T(8,128)(2,1)}, bf16[256,768]{1,0:T(8,128)(2,1)}, u32[]{:S(2)}, u32[]{:S(2)}) collective-permute-start(bf16[256,768]{1,0:T(8,128)(2,1)} %broadcast_select_fusion.2), channel_id=1, source_target_pairs={{0,16},{1,49},{16,32},{17,1},{32,48},{33,17},{48,0},{49,33},{2,18}... | collective-permute-start | bytes 1179656 | tf_op jit(solution)/shard_map/ppermute | solution.py:326
  64.5 2.3 %all-gather.2.cloned.1.call-done.left = bf16[1024,4096]{1,0:T(8,128)(2,1)} async-done(((bf16[128,4096]{1,0:T(8,128)(2,1)}), bf16[1024,4096]{1,0:T(8,128)(2,1)}) %all-gather.2.cloned.1.call-update) | async-done | bytes 8388624 | tf_op jit(solution)/shard_map/all_gather | solution.py:293
  68.0 1.5 collective-permute-start.5
  69.5 11.1 %convolution_convert_fusion.refs_1_.proj = bf16[1024,768]{1,0:T(8,128)(2,1)S(1)} fusion(bf16[1024,4096]{1,0:T(8,128)(2,1)} %all-gather.2.cloned.1.call-done.left, bf16[768,4096]{1,0:T(8,128)(2,1)} %bitcast.54), kind=kOutput, calls=%fused_computation.5 | convolution fusion | flops 6443237376 | bytes 16252928 | tf_op jit(solution)/shard_map/dot_general | solution.py:315
  80.7 2.8 %collective-permute-start.8 = (bf16[256,768]{1,0:T(8,128)(2,1)S(1)}, bf16[256,768]{1,0:T(8,128)(2,1)S(1)}, u32[]{:S(2)}, u32[]{:S(2)}) collective-permute-start(bf16[256,768]{1,0:T(8,128)(2,1)S(1)} %collective-permute-done.1.refs_0_), channel_id=1, source_target_pairs={{0,48},{16,0},{32,16},{48,32},{1,49},{17,1},{33,17},{49,33},{2,50}... | collective-permute-start | bytes 1179656 | tf_op jit(solution)/shard_map/ppermute | solution.py:22
  83.5 4.5 %shard_map.64.refs_8_ = f32[1024,768]{1,0:T(8,128)S(1)} custom-call(s32[8]{0:T(128)S(1)} %copy-done.11, bf16[1024,4096]{1,0:T(8,128)(2,1)S(1)} %copy-done, bf16[256,768]{1,0:T(8,128)(2,1)S(1)} %collective-permute-done.refs_0_, bf16[256,768]{1,0:T(8,128)(2,1)S(1)} %collective-permute-done.11.refs_1_, bf16[256,768]{1,0:T(8,128)(2,1)S(1)} %collective-permute-done.12.refs_2_, ...), custom_call_target="tpu_custom_call" | custom-call | flops 3221225472 | bytes 8000000 | tf_op jit(solution)/shard_map/pallas_call | solution.py:115
  88.2 3.2 %collective-permute-start.9 = (bf16[256,768]{1,0:T(8,128)(2,1)S(1)}, bf16[256,768]{1,0:T(8,128)(2,1)S(1)}, u32[]{:S(2)}, u32[]{:S(2)}) collective-permute-start(bf16[256,768]{1,0:T(8,128)(2,1)S(1)} %broadcast_select_fusion.4), channel_id=1, source_target_pairs={{0,16},{1,49},{16,32},{17,1},{32,48},{33,17},{48,0},{49,33},{2,18}... | collective-permute-start | bytes 1179656 | tf_op jit(solution)/shard_map/ppermute | solution.py:326
  91.7 4.6 %shard_map.66.into = bf16[1024,512]{1,0:T(8,128)(2,1)S(1)} custom-call(s32[8]{0:T(128)S(1)} %copy-done.13, bf16[1024,768]{1,0:T(8,128)(2,1)S(1)} %convolution_convert_fusion.refs_1_.proj, bf16[176,256]{1,0:T(8,128)(2,1)S(1)} %broadcast_in_dim.96.refs_2_, f32[9,256]{1,0:T(8,128)S(1)} %copy-done.7, bf16[16,256,128]{2,1,0:T(8,128)(2,1)S(1)} %copy-done.15, ...), custom_call_target="tpu_custom_call" | custom-call | flops 6144000000 | bytes 4000000 | tf_op jit(solution)/shard_map/pallas_call | solution.py:231
  96.6 11.8 %collective-permute-start.18 = (bf16[176,256]{1,0:T(8,128)(2,1)S(1)}, bf16[176,256]{1,0:T(8,128)(2,1)S(1)}, u32[]{:S(2)}, u32[]{:S(2)}) collective-permute-start(bf16[176,256]{1,0:T(8,128)(2,1)S(1)} %pad_maximum_fusion.1), channel_id=1, source_target_pairs={{0,8},{8,16},{16,24},{24,32},{32,40},{40,48},{48,56},{56,64},{64,7... | collective-permute-start | bytes 270344 | tf_op jit(solution)/shard_map/ppermute | solution.py:309
  108.5 4.4 %shard_map.67.proj = bf16[1024,768]{1,0:T(8,128)(2,1)S(1)} custom-call(s32[8]{0:T(128)S(1)} %copy-done.10, bf16[1024,4096]{1,0:T(8,128)(2,1)S(1)} %copy-done, bf16[256,768]{1,0:T(8,128)(2,1)S(1)} %collective-permute-done.1.refs_0_, bf16[256,768]{1,0:T(8,128)(2,1)S(1)} %collective-permute-done.7.refs_1_, bf16[256,768]{1,0:T(8,128)(2,1)S(1)} %collective-permute-done.8.refs_2_, ...), custom_call_target="tpu_custom_call" | custom-call | flops 3221225472 | bytes 8000000 | tf_op jit(solution)/shard_map/pallas_call | solution.py:115
  113.2 2.1 %collective-permute-start.17 = (bf16[176,256]{1,0:T(8,128)(2,1)S(1)}, bf16[176,256]{1,0:T(8,128)(2,1)S(1)}, u32[]{:S(2)}, u32[]{:S(2)}) collective-permute-start(bf16[176,256]{1,0:T(8,128)(2,1)S(1)} %pad_maximum_fusion), channel_id=1, source_target_pairs={{0,8},{8,16},{16,24},{24,32},{32,40},{40,48},{48,56},{56,64},{64,7... | collective-permute-start | bytes 270344 | tf_op jit(solution)/shard_map/ppermute | solution.py:309
  115.3 4.6 %shard_map.69.into = bf16[1024,512]{1,0:T(8,128)(2,1)S(1)} custom-call(s32[8]{0:T(128)S(1)} %copy-done.13, bf16[1024,768]{1,0:T(8,128)(2,1)S(1)} %shard_map.67.proj, bf16[176,256]{1,0:T(8,128)(2,1)S(1)} %collective-permute-done.18.halo, f32[9,256]{1,0:T(8,128)S(1)} %slice_convert_fusion.short, ...), custom_call_target="tpu_custom_call", output_to_operand_aliasing={{}: (7, {})} | custom-call | flops 6144000000 | bytes 4000000 | tf_op jit(solution)/shard_map/pallas_call | solution.py:231
  119.9 2.7 %shard_map.70 = bf16[1024,512]{1,0:T(8,128)(2,1)S(1)} custom-call(s32[2]{0:T(128)S(1)} %copy-done.12, bf16[1024,768]{1,0:T(8,128)(2,1)S(1)} %convolution_convert_fusion.refs_1_.proj, bf16[176,256]{1,0:T(8,128)(2,1)S(1)} %collective-permute-done.17.halo, f32[9,256]{1,0:T(8,128)S(1)} %copy-done.7, ...), custom_call_target="tpu_custom_call", output_to_operand_aliasing={{}: (7, {})} | custom-call | flops 1536000000 | bytes 4000000 | tf_op jit(solution)/shard_map/pallas_call | solution.py:231
  122.6 23.1 %all_to_all.11 = bf16[8,128,512]{2,1,0:T(8,128)(2,1)S(1)} all-to-all(bf16[8,128,512]{2,1,0:T(8,128)(2,1)S(1)} %bitcast.48), channel_id=1, replica_groups=mesh['z_lo'=4,'x'=4,'z_hi'=2,'y'=4,'core'=2] {'y','core'}, dimensions={0} | all-to-all | bytes 2097152 | tf_op jit(solution)/shard_map/all_to_all | solution.py:337
  145.7 1.3 shard_map.71
  (145 shorter events, 23.8 us)
Async XLA Ops:
  6.5 60.3 %all-gather.2.cloned.1.call-start = ((), (), s32[]{:S(2)}) async-start(), calls=%async_computation.1 | async-start | bytes 9437184 | tf_op jit(solution)/shard_map/all_gather | solution.py:293
  10.4 25.8 %collective-permute-start = (bf16[256,768]{1,0:T(8,128)(2,1)S(1)}, bf16[256,768]{1,0:T(8,128)(2,1)S(1)}, u32[]{:S(2)}, u32[]{:S(2)}) collective-permute-start(bf16[256,768]{1,0:T(8,128)(2,1)S(1)} %copy.24), channel_id=1, source_target_pairs={{0,136},{8,128},{64,200},{72,192},{128,8},{136,0},{192,72},{200,64... | collective-permute-start | bytes 1179656 | tf_op jit(solution)/shard_map/ppermute | solution.py:55
  17.3 18.7 %collective-permute-start.6 = (bf16[17,256]{1,0:T(8,128)(2,1)S(1)}, bf16[17,256]{1,0:T(8,128)(2,1)S(1)}, u32[]{:S(2)}, u32[]{:S(2)}) collective-permute-start(bf16[17,256]{1,0:T(8,128)(2,1)S(1)} %pad_maximum_fusion.2), channel_id=1, source_target_pairs={{0,8},{8,0},{1,9},{9,1},{2,10},{10,2},{3,11},{11,3},{4,12},{12,4},... | collective-permute-start | bytes 26120 | tf_op jit(solution)/shard_map/ppermute | solution.py:17
  37.2 16.4 %collective-permute-start.1 = (bf16[256,768]{1,0:T(8,128)(2,1)}, bf16[256,768]{1,0:T(8,128)(2,1)S(1)}, u32[]{:S(2)}, u32[]{:S(2)}) collective-permute-start(bf16[256,768]{1,0:T(8,128)(2,1)} %get-tuple-element.46), channel_id=1, source_target_pairs={{0,200},{8,192},{64,0},{72,8},{128,64},{136,72},{192,128},{200,136... | collective-permute-start | bytes 1179656 | tf_op jit(solution)/shard_map/ppermute | solution.py:65
  40.4 10.6 %collective-permute-start.2 = (bf16[256,768]{1,0:T(8,128)(2,1)}, bf16[256,768]{1,0:T(8,128)(2,1)S(1)}, u32[]{:S(2)}, u32[]{:S(2)}) collective-permute-start(bf16[256,768]{1,0:T(8,128)(2,1)} %get-tuple-element.45), channel_id=1, source_target_pairs={{0,64},{8,72},{64,128},{72,136},{128,192},{136,200},{192,8},{200,0... | collective-permute-start | bytes 1179656 | tf_op jit(solution)/shard_map/ppermute | solution.py:65
  40.9 13.9 %collective-permute-start.11 = (bf16[256,768]{1,0:T(8,128)(2,1)S(1)}, bf16[256,768]{1,0:T(8,128)(2,1)S(1)}, u32[]{:S(2)}, u32[]{:S(2)}) collective-permute-start(bf16[256,768]{1,0:T(8,128)(2,1)S(1)} %collective-permute-done.refs_0_), channel_id=1, source_target_pairs={{0,16},{16,32},{32,48},{48,0},{1,17},{17,33},{33,49},{49,1},{2,18}... | collective-permute-start | bytes 1179656 | tf_op jit(solution)/shard_map/ppermute | solution.py:22
  42.2 12.7 %collective-permute-start.12 = (bf16[256,768]{1,0:T(8,128)(2,1)S(1)}, bf16[256,768]{1,0:T(8,128)(2,1)S(1)}, u32[]{:S(2)}, u32[]{:S(2)}) collective-permute-start(bf16[256,768]{1,0:T(8,128)(2,1)S(1)} %collective-permute-done.refs_0_), channel_id=1, source_target_pairs={{0,48},{16,0},{32,16},{48,32},{1,49},{17,1},{33,17},{49,33},{2,50}... | collective-permute-start | bytes 1179656 | tf_op jit(solution)/shard_map/ppermute | solution.py:22
  51.0 9.6 %collective-permute-start.14 = (bf16[256,768]{1,0:T(8,128)(2,1)S(1)}, bf16[256,768]{1,0:T(8,128)(2,1)S(1)}, u32[]{:S(2)}, u32[]{:S(2)}) collective-permute-start(bf16[256,768]{1,0:T(8,128)(2,1)S(1)} %collective-permute-done.2.refs_4_), channel_id=1, source_target_pairs={{0,16},{16,32},{32,48},{48,0},{1,17},{17,33},{33,49},{49,1},{2,18}... | collective-permute-start | bytes 1179656 | tf_op jit(solution)/shard_map/ppermute | solution.py:22
  52.2 8.4 %collective-permute-start.15 = (bf16[256,768]{1,0:T(8,128)(2,1)S(1)}, bf16[256,768]{1,0:T(8,128)(2,1)S(1)}, u32[]{:S(2)}, u32[]{:S(2)}) collective-permute-start(bf16[256,768]{1,0:T(8,128)(2,1)S(1)} %collective-permute-done.2.refs_4_), channel_id=1, source_target_pairs={{0,48},{16,0},{32,16},{48,32},{1,49},{17,1},{33,17},{49,33},{2,50}... | collective-permute-start | bytes 1179656 | tf_op jit(solution)/shard_map/ppermute | solution.py:22
  54.7 9.8 %collective-permute-start.3 = (bf16[256,768]{1,0:T(8,128)(2,1)S(1)}, bf16[256,768]{1,0:T(8,128)(2,1)}, u32[]{:S(2)}, u32[]{:S(2)}) collective-permute-start(bf16[256,768]{1,0:T(8,128)(2,1)S(1)} %select_select_fusion), channel_id=1, source_target_pairs={{64,128},{128,64},{0,200},{192,8},{72,136},{136,72},{8,192},{200,0... | collective-permute-start | bytes 1179656 | tf_op jit(solution)/shard_map/ppermute | solution.py:79
  55.6 25.0 %collective-permute-start.13 = (bf16[256,768]{1,0:T(8,128)(2,1)}, bf16[256,768]{1,0:T(8,128)(2,1)}, u32[]{:S(2)}, u32[]{:S(2)}) collective-permute-start(bf16[256,768]{1,0:T(8,128)(2,1)} %broadcast_select_fusion.3), channel_id=1, source_target_pairs={{0,16},{1,49},{16,32},{17,1},{32,48},{33,17},{48,0},{49,33},{2,18}... | collective-permute-start | bytes 1179656 | tf_op jit(solution)/shard_map/ppermute | solution.py:326
  62.1 21.3 %collective-permute-start.16 = (bf16[256,768]{1,0:T(8,128)(2,1)}, bf16[256,768]{1,0:T(8,128)(2,1)}, u32[]{:S(2)}, u32[]{:S(2)}) collective-permute-start(bf16[256,768]{1,0:T(8,128)(2,1)} %broadcast_select_fusion.2), channel_id=1, source_target_pairs={{0,16},{1,49},{16,32},{17,1},{32,48},{33,17},{48,0},{49,33},{2,18}... | collective-permute-start | bytes 1179656 | tf_op jit(solution)/shard_map/ppermute | solution.py:326
  66.9 16.6 %copy-start.3 = (bf16[256,768]{1,0:T(8,128)(2,1)S(1)}, bf16[256,768]{1,0:T(8,128)(2,1)}, u32[]{:S(2)}) copy-start(bf16[256,768]{1,0:T(8,128)(2,1)} %copy-done.2) | copy-start | bytes 1179652
  66.9 16.6 %copy-start.11 = (s32[8]{0:T(128)S(1)}, s32[8]{0:T(128)}, u32[]{:S(2)}) copy-start(s32[8]{0:T(128)} %stack.71.places) | copy-start | bytes 100
  66.9 21.2 %collective-permute-start.4 = (bf16[256,768]{1,0:T(8,128)(2,1)}, bf16[256,768]{1,0:T(8,128)(2,1)S(1)}, u32[]{:S(2)}, u32[]{:S(2)}) collective-permute-start(bf16[256,768]{1,0:T(8,128)(2,1)} %collective-permute-done.3.refs_4_), channel_id=1, source_target_pairs={{0,16},{16,32},{32,48},{48,0},{1,17},{17,33},{33,49},{49,1},{2,18}... | collective-permute-start | bytes 1179656 | tf_op jit(solution)/shard_map/ppermute | solution.py:22
  68.0 20.0 %collective-permute-start.5 = (bf16[256,768]{1,0:T(8,128)(2,1)}, bf16[256,768]{1,0:T(8,128)(2,1)S(1)}, u32[]{:S(2)}, u32[]{:S(2)}) collective-permute-start(bf16[256,768]{1,0:T(8,128)(2,1)} %collective-permute-done.3.refs_4_), channel_id=1, source_target_pairs={{0,48},{16,0},{32,16},{48,32},{1,49},{17,1},{33,17},{49,33},{2,50}... | collective-permute-start | bytes 1179656 | tf_op jit(solution)/shard_map/ppermute | solution.py:22
  69.5 18.6 %collective-permute-start.7 = (bf16[256,768]{1,0:T(8,128)(2,1)S(1)}, bf16[256,768]{1,0:T(8,128)(2,1)S(1)}, u32[]{:S(2)}, u32[]{:S(2)}) collective-permute-start(bf16[256,768]{1,0:T(8,128)(2,1)S(1)} %collective-permute-done.1.refs_0_), channel_id=1, source_target_pairs={{0,16},{16,32},{32,48},{48,0},{1,17},{17,33},{33,49},{49,1},{2,18}... | collective-permute-start | bytes 1179656 | tf_op jit(solution)/shard_map/ppermute | solution.py:22
  80.7 7.5 %collective-permute-start.8 = (bf16[256,768]{1,0:T(8,128)(2,1)S(1)}, bf16[256,768]{1,0:T(8,128)(2,1)S(1)}, u32[]{:S(2)}, u32[]{:S(2)}) collective-permute-start(bf16[256,768]{1,0:T(8,128)(2,1)S(1)} %collective-permute-done.1.refs_0_), channel_id=1, source_target_pairs={{0,48},{16,0},{32,16},{48,32},{1,49},{17,1},{33,17},{49,33},{2,50}... | collective-permute-start | bytes 1179656 | tf_op jit(solution)/shard_map/ppermute | solution.py:22
  88.2 20.2 %collective-permute-start.9 = (bf16[256,768]{1,0:T(8,128)(2,1)S(1)}, bf16[256,768]{1,0:T(8,128)(2,1)S(1)}, u32[]{:S(2)}, u32[]{:S(2)}) collective-permute-start(bf16[256,768]{1,0:T(8,128)(2,1)S(1)} %broadcast_select_fusion.4), channel_id=1, source_target_pairs={{0,16},{1,49},{16,32},{17,1},{32,48},{33,17},{48,0},{49,33},{2,18}... | collective-permute-start | bytes 1179656 | tf_op jit(solution)/shard_map/ppermute | solution.py:326
  91.4 17.0 %collective-permute-start.10 = (bf16[256,768]{1,0:T(8,128)(2,1)S(1)}, bf16[256,768]{1,0:T(8,128)(2,1)S(1)}, u32[]{:S(2)}, u32[]{:S(2)}) collective-permute-start(bf16[256,768]{1,0:T(8,128)(2,1)S(1)} %broadcast_select_fusion.5), channel_id=1, source_target_pairs={{0,16},{1,49},{16,32},{17,1},{32,48},{33,17},{48,0},{49,33},{2,18}... | collective-permute-start | bytes 1179656 | tf_op jit(solution)/shard_map/ppermute | solution.py:326
  91.6 16.8 %copy-start.10 = (s32[8]{0:T(128)S(1)}, s32[8]{0:T(128)}, u32[]{:S(2)}) copy-start(s32[8]{0:T(128)} %stack.62.places) | copy-start | bytes 100
  96.6 18.7 %copy-start.17 = (bf16[16,256,128]{2,1,0:T(8,128)(2,1)S(1)}, bf16[16,256,128]{2,1,0:T(8,128)(2,1)}, u32[]{:S(2)}) copy-start(bf16[16,256,128]{2,1,0:T(8,128)(2,1)} %copy-done.16) | copy-start | bytes 3145732
  96.6 18.7 %collective-permute-start.18 = (bf16[176,256]{1,0:T(8,128)(2,1)S(1)}, bf16[176,256]{1,0:T(8,128)(2,1)S(1)}, u32[]{:S(2)}, u32[]{:S(2)}) collective-permute-start(bf16[176,256]{1,0:T(8,128)(2,1)S(1)} %pad_maximum_fusion.1), channel_id=1, source_target_pairs={{0,8},{8,16},{16,24},{24,32},{32,40},{40,48},{48,56},{56,64},{64,7... | collective-permute-start | bytes 270344 | tf_op jit(solution)/shard_map/ppermute | solution.py:309
  113.2 6.7 %collective-permute-start.17 = (bf16[176,256]{1,0:T(8,128)(2,1)S(1)}, bf16[176,256]{1,0:T(8,128)(2,1)S(1)}, u32[]{:S(2)}, u32[]{:S(2)}) collective-permute-start(bf16[176,256]{1,0:T(8,128)(2,1)S(1)} %pad_maximum_fusion), channel_id=1, source_target_pairs={{0,8},{8,16},{16,24},{24,32},{32,40},{40,48},{48,56},{56,64},{64,7... | collective-permute-start | bytes 270344 | tf_op jit(solution)/shard_map/ppermute | solution.py:309
  (32 other events, 229.9 us)
Sparse Core Ops, SparseCore 0:
  10.3 56.5 all-gather.1

commit v9 on v7

--- a/solution.py
+++ b/solution.py
@@ -318,16 +318,16 @@
     columns = (*columns[:3], (columns[3][0], mine))
     rows_of = [spread_rows(mine) for _, mine in columns]
     pieces, places = [], []
+    other_halo = halo_of(own_projected, own_short)
     half = 8
     for n, ((by, mine), (below, above, onward)) in enumerate(zip(columns, rows_of)):
         if n == 2:
+            pieces[0], other_halo = lax.optimization_barrier((pieces[0], other_halo))
             first_sum = add_product(gathered, pieces, places, None, jnp.float32)
         if n == 3:
             onward, first_sum = lax.optimization_barrier((onward, first_sum))
         pieces += [mine, below, above, lax.ppermute(onward, ("x", "core"), fan("x"))]
         places += places_of(by)
-    first_sum, own_projected = lax.optimization_barrier((first_sum, own_projected))
-    other_halo = halo_of(own_projected, own_short)
     own_band, other_band = banded(long_filter), banded(other_long)
     nothing = jnp.zeros((SPAN + 3 * RIM, channels), jnp.bfloat16)
     gated = mix_conv(own_projected, nothing, own_short, own_band, starts, length, None, 0)

time: 153 us -> 156 us (1.020)
  the two profiles are of different devices: /device:TPU:2 before, /device:TPU:1 now
where the time goes in v9:
time: 156 us; the launch traced here: 155 us
  starting transfers between devices  41.6 us (27%)
  blocking collectives  24.3 us (16%)
  Pallas kernels  23.5 us (15%)
  local copies, waits for them, and re-layouts  20.5 us (13%)
  between operations  14.1 us (9%)
  matrix products  11.1 us (7%)
  waiting for transfers between devices  10.8 us (7%)
  other arithmetic  8.79 us (6%)
    all_to_all x1, blocking collectives, per_device(): lax.all_to_all(gated, ('y', 'core'), split_axis=0, concat_axis=0, tiled=T...  24.3 us
    ppermute x2, starting transfers between devices, halo_of(): lax.ppermute(tail_of(projected, short, starts), ('z_lo', 'x', 'z_hi'), ne...  14.1 us
    pallas_call x3, Pallas kernels, mix_conv(): pl.pallas_call(body, out_shape=jax.ShapeDtypeStruct((length, 2 * channels...  12.7 us
    dot_general x1, matrix products, per_device(): lax.dot_general(gathered, weight_t, (((1,), (1,)), ((), ())), preferred_e...  11.1 us
    ppermute x8, starting transfers between devices, shift(): lax.ppermute(value, axis, [(i, (i + by) % size) for i in range(size)])  9.74 us
    pallas_call x2, Pallas kernels, add_product(): pl.pallas_call(functools.partial(add_product_kernel, count), out_shape=ja...  9.06 us
    optimization_barrier x1, local copies, waits for them, and re-layouts, per_device(): in_weight, normed = lax.optimization_barrier((in_weight, normed))  8.73 us
    ppermute x1, starting transfers between devices, across(): return lax.ppermute(value, ('z_lo', 'z_hi'), pairs)  6.94 us
  transfers between devices with their start and end apart: 20, of which 5 were waited for; matrix products, arithmetic and copies ran while one was open for 22% of the time, Pallas kernels for 10%

profile of v9, /device:TPU:1, one launch (start us, length us, event | category | flops | bytes accessed | tf_op | source)
XLA Modules:
  0.0 154.7 jit_solution(8630675039967457668)
XLA Ops:
  8.2 1.3 fusion.2
  9.7 6.9 %collective-permute-start = (bf16[256,768]{1,0:T(8,128)(2,1)S(1)}, bf16[256,768]{1,0:T(8,128)(2,1)S(1)}, u32[]{:S(2)}, u32[]{:S(2)}) collective-permute-start(bf16[256,768]{1,0:T(8,128)(2,1)S(1)} %copy.24), channel_id=1, source_target_pairs={{0,136},{8,128},{64,200},{72,192},{128,8},{136,0},{192,72},{200,64... | collective-permute-start | bytes 1179656 | tf_op jit(solution)/shard_map/ppermute | solution.py:55
  17.7 8.7 %copy.25 = bf16[4096,3,256]{0,2,1:T(8,128)(2,1)} copy(bf16[4096,3,256]{2,0,1:T(8,128)(2,1)} %param.8) | data formatting | bytes 12582912 | tf_op jit(solution)/shard_map/optimization_barrier | solution.py:292
  30.4 1.9 %constant_dynamic-slice_fusion = (bf16[256,3,256]{0,2,1:T(8,128)(2,1)}, bf16[256,3,256]{0,2,1:T(8,128)(2,1)S(1)}) fusion(bf16[4096,3,256]{0,2,1:T(8,128)(2,1)} %copy.25, s32[]{:T(128)S(6)} %select_n.158, s32[]{:T(128)S(6)} %select_n.156), kind=kLoop, calls=%fused_computation.25 | loop fusion | bytes 1572872 | tf_op jit(solution)/shard_map/dynamic_slice | solution.py:283
  36.7 1.5 collective-permute-start.12
  40.8 2.2 %collective-permute-start.2 = (bf16[256,768]{1,0:T(8,128)(2,1)}, bf16[256,768]{1,0:T(8,128)(2,1)S(1)}, u32[]{:S(2)}, u32[]{:S(2)}) collective-permute-start(bf16[256,768]{1,0:T(8,128)(2,1)} %get-tuple-element.47), channel_id=1, source_target_pairs={{0,200},{8,192},{64,0},{72,8},{128,64},{136,72},{192,128},{200,136... | collective-permute-start | bytes 1179656 | tf_op jit(solution)/shard_map/ppermute | solution.py:65
  45.4 4.9 %collective-permute-done.1.refs_4_ = bf16[256,768]{1,0:T(8,128)(2,1)S(1)} collective-permute-done((bf16[256,768]{1,0:T(8,128)(2,1)}, bf16[256,768]{1,0:T(8,128)(2,1)S(1)}, u32[]{:S(2)}, u32[]{:S(2)}) %collective-permute-start.1) | collective-permute-done | bytes 393248 | tf_op jit(solution)/shard_map/ppermute | solution.py:65
  50.3 2.7 %collective-permute-start.15 = (bf16[256,768]{1,0:T(8,128)(2,1)S(1)}, bf16[256,768]{1,0:T(8,128)(2,1)S(1)}, u32[]{:S(2)}, u32[]{:S(2)}) collective-permute-start(bf16[256,768]{1,0:T(8,128)(2,1)S(1)} %collective-permute-done.1.refs_4_), channel_id=1, source_target_pairs={{0,48},{16,0},{32,16},{48,32},{1,49},{17,1},{33,17},{49,33},{2,50}... | collective-permute-start | bytes 1179656 | tf_op jit(solution)/shard_map/ppermute | solution.py:22
  55.9 1.4 collective-permute-start.5
  57.3 2.6 %collective-permute-done.14.refs_5_ = bf16[256,768]{1,0:T(8,128)(2,1)S(1)} collective-permute-done((bf16[256,768]{1,0:T(8,128)(2,1)S(1)}, bf16[256,768]{1,0:T(8,128)(2,1)S(1)}, u32[]{:S(2)}, u32[]{:S(2)}) %collective-permute-start.14) | collective-permute-done | bytes 393248 | tf_op jit(solution)/shard_map/ppermute | solution.py:22
  61.6 2.3 %collective-permute-start.16 = (bf16[256,768]{1,0:T(8,128)(2,1)}, bf16[256,768]{1,0:T(8,128)(2,1)}, u32[]{:S(2)}, u32[]{:S(2)}) collective-permute-start(bf16[256,768]{1,0:T(8,128)(2,1)} %broadcast_select_fusion), channel_id=1, source_target_pairs={{0,16},{1,49},{16,32},{17,1},{32,48},{33,17},{48,0},{49,33},{2,18}... | collective-permute-start | bytes 1179656 | tf_op jit(solution)/shard_map/ppermute | solution.py:329
  63.9 2.3 %all-gather.2.cloned.1.call-done.left = bf16[1024,4096]{1,0:T(8,128)(2,1)} async-done(((bf16[128,4096]{1,0:T(8,128)(2,1)}), bf16[1024,4096]{1,0:T(8,128)(2,1)}) %all-gather.2.cloned.1.call-update) | async-done | bytes 8388624 | tf_op jit(solution)/shard_map/all_gather | solution.py:293
  66.3 11.1 %convolution_convert_fusion.refs_1_.proj = bf16[1024,768]{1,0:T(8,128)(2,1)S(1)} fusion(bf16[1024,4096]{1,0:T(8,128)(2,1)} %all-gather.2.cloned.1.call-done.left, bf16[768,4096]{1,0:T(8,128)(2,1)} %bitcast.54), kind=kOutput, calls=%fused_computation.5 | convolution fusion | flops 6443237376 | bytes 16252928 | tf_op jit(solution)/shard_map/dot_general | solution.py:313
  79.0 1.5 %collective-permute-start.9 = (bf16[256,768]{1,0:T(8,128)(2,1)}, bf16[256,768]{1,0:T(8,128)(2,1)S(1)}, u32[]{:S(2)}, u32[]{:S(2)}) collective-permute-start(bf16[256,768]{1,0:T(8,128)(2,1)} %collective-permute-done.3.refs_4_), channel_id=1, source_target_pairs={{0,48},{16,0},{32,16},{48,32},{1,49},{17,1},{33,17},{49,33},{2,50}... | collective-permute-start | bytes 1179656 | tf_op jit(solution)/shard_map/ppermute | solution.py:22
  80.6 7.3 %collective-permute-start.10 = (bf16[176,256]{1,0:T(8,128)(2,1)S(1)}, bf16[176,256]{1,0:T(8,128)(2,1)S(1)}, u32[]{:S(2)}, u32[]{:S(2)}) collective-permute-start(bf16[176,256]{1,0:T(8,128)(2,1)S(1)} %pad_maximum_fusion), channel_id=1, source_target_pairs={{0,8},{8,16},{16,24},{24,32},{32,40},{40,48},{48,56},{56,64},{64,7... | collective-permute-start | bytes 270344 | tf_op jit(solution)/shard_map/ppermute | solution.py:309
  89.5 2.5 %collective-permute-start.7 = (bf16[256,768]{1,0:T(8,128)(2,1)S(1)}, bf16[256,768]{1,0:T(8,128)(2,1)S(1)}, u32[]{:S(2)}, u32[]{:S(2)}) collective-permute-start(bf16[256,768]{1,0:T(8,128)(2,1)S(1)} %broadcast_select_fusion.3), channel_id=1, source_target_pairs={{0,16},{1,49},{16,32},{17,1},{32,48},{33,17},{48,0},{49,33},{2,18}... | collective-permute-start | bytes 1179656 | tf_op jit(solution)/shard_map/ppermute | solution.py:329
  92.0 4.5 %shard_map.64.refs_8_ = f32[1024,768]{1,0:T(8,128)S(1)} custom-call(s32[8]{0:T(128)S(1)} %copy-done.13, bf16[1024,4096]{1,0:T(8,128)(2,1)S(1)} %copy-done, bf16[256,768]{1,0:T(8,128)(2,1)S(1)} %collective-permute-done.refs_0_, bf16[256,768]{1,0:T(8,128)(2,1)S(1)} %collective-permute-done.11.refs_1_, bf16[256,768]{1,0:T(8,128)(2,1)S(1)} %collective-permute-done.12.refs_2_, ...), custom_call_target="tpu_custom_call" | custom-call | flops 3221225472 | bytes 8000000 | tf_op jit(solution)/shard_map/pallas_call | solution.py:115
  97.4 5.4 %shard_map.66.into = bf16[1024,512]{1,0:T(8,128)(2,1)S(1)} custom-call(s32[8]{0:T(128)S(1)} %copy-done.15, bf16[1024,768]{1,0:T(8,128)(2,1)S(1)} %convolution_convert_fusion.refs_1_.proj, bf16[176,256]{1,0:T(8,128)(2,1)S(1)} %broadcast_in_dim.99.refs_2_, f32[9,256]{1,0:T(8,128)S(1)} %copy-done.9, bf16[16,256,128]{2,1,0:T(8,128)(2,1)S(1)} %copy-done.17, ...), custom_call_target="tpu_custom_call" | custom-call | flops 6144000000 | bytes 4000000 | tf_op jit(solution)/shard_map/pallas_call | solution.py:231
  103.3 4.5 %shard_map.67.proj = bf16[1024,768]{1,0:T(8,128)(2,1)S(1)} custom-call(s32[8]{0:T(128)S(1)} %copy-done.12, bf16[1024,4096]{1,0:T(8,128)(2,1)S(1)} %copy-done, bf16[256,768]{1,0:T(8,128)(2,1)S(1)} %collective-permute-done.2.refs_0_, bf16[256,768]{1,0:T(8,128)(2,1)S(1)} %collective-permute-done.5.refs_1_, bf16[256,768]{1,0:T(8,128)(2,1)} %collective-permute-done.6.refs_2_, ...), custom_call_target="tpu_custom_call" | custom-call | flops 3221225472 | bytes 8000000 | tf_op jit(solution)/shard_map/pallas_call | solution.py:115
  108.1 6.8 %collective-permute-start.18 = (bf16[176,256]{1,0:T(8,128)(2,1)S(1)}, bf16[176,256]{1,0:T(8,128)(2,1)S(1)}, u32[]{:S(2)}, u32[]{:S(2)}) collective-permute-start(bf16[176,256]{1,0:T(8,128)(2,1)S(1)} %pad_maximum_fusion.1), channel_id=1, source_target_pairs={{0,8},{8,16},{16,24},{24,32},{32,40},{40,48},{48,56},{56,64},{64,7... | collective-permute-start | bytes 270344 | tf_op jit(solution)/shard_map/ppermute | solution.py:309
  114.9 5.2 %shard_map.69.into = bf16[1024,512]{1,0:T(8,128)(2,1)S(1)} custom-call(s32[8]{0:T(128)S(1)} %copy-done.15, bf16[1024,768]{1,0:T(8,128)(2,1)S(1)} %shard_map.67.proj, bf16[176,256]{1,0:T(8,128)(2,1)S(1)} %collective-permute-done.10.halo, f32[9,256]{1,0:T(8,128)S(1)} %slice_convert_fusion.short, ...), custom_call_target="tpu_custom_call", output_to_operand_aliasing={{}: (7, {})} | custom-call | flops 6144000000 | bytes 4000000 | tf_op jit(solution)/shard_map/pallas_call | solution.py:231
  120.2 2.1 %shard_map.70 = bf16[1024,512]{1,0:T(8,128)(2,1)S(1)} custom-call(s32[2]{0:T(128)S(1)} %copy-done.14, bf16[1024,768]{1,0:T(8,128)(2,1)S(1)} %convolution_convert_fusion.refs_1_.proj, bf16[176,256]{1,0:T(8,128)(2,1)S(1)} %collective-permute-done.18.halo, f32[9,256]{1,0:T(8,128)S(1)} %copy-done.9, ...), custom_call_target="tpu_custom_call", output_to_operand_aliasing={{}: (7, {})} | custom-call | flops 1536000000 | bytes 4000000 | tf_op jit(solution)/shard_map/pallas_call | solution.py:231
  122.3 24.3 %all_to_all.11 = bf16[8,128,512]{2,1,0:T(8,128)(2,1)S(1)} all-to-all(bf16[8,128,512]{2,1,0:T(8,128)(2,1)S(1)} %bitcast.48), channel_id=1, replica_groups=mesh['z_lo'=4,'x'=4,'z_hi'=2,'y'=4,'core'=2] {'y','core'}, dimensions={0} | all-to-all | bytes 2097152 | tf_op jit(solution)/shard_map/all_to_all | solution.py:339
  146.6 1.3 shard_map.71
  (151 shorter events, 25.3 us)
Async XLA Ops:
  6.5 59.7 %all-gather.2.cloned.1.call-start = ((), (), s32[]{:S(2)}) async-start(), calls=%async_computation.1 | async-start | bytes 9437184 | tf_op jit(solution)/shard_map/all_gather | solution.py:293
  9.7 25.7 %collective-permute-start = (bf16[256,768]{1,0:T(8,128)(2,1)S(1)}, bf16[256,768]{1,0:T(8,128)(2,1)S(1)}, u32[]{:S(2)}, u32[]{:S(2)}) collective-permute-start(bf16[256,768]{1,0:T(8,128)(2,1)S(1)} %copy.24), channel_id=1, source_target_pairs={{0,136},{8,128},{64,200},{72,192},{128,8},{136,0},{192,72},{200,64... | collective-permute-start | bytes 1179656 | tf_op jit(solution)/shard_map/ppermute | solution.py:55
  16.7 18.7 %collective-permute-start.4 = (bf16[17,256]{1,0:T(8,128)(2,1)S(1)}, bf16[17,256]{1,0:T(8,128)(2,1)S(1)}, u32[]{:S(2)}, u32[]{:S(2)}) collective-permute-start(bf16[17,256]{1,0:T(8,128)(2,1)S(1)} %pad_maximum_fusion.2), channel_id=1, source_target_pairs={{0,8},{8,0},{1,9},{9,1},{2,10},{10,2},{3,11},{11,3},{4,12},{12,4},... | collective-permute-start | bytes 26120 | tf_op jit(solution)/shard_map/ppermute | solution.py:17
  35.4 17.6 %collective-permute-start.11 = (bf16[256,768]{1,0:T(8,128)(2,1)S(1)}, bf16[256,768]{1,0:T(8,128)(2,1)S(1)}, u32[]{:S(2)}, u32[]{:S(2)}) collective-permute-start(bf16[256,768]{1,0:T(8,128)(2,1)S(1)} %collective-permute-done.refs_0_), channel_id=1, source_target_pairs={{0,16},{16,32},{32,48},{48,0},{1,17},{17,33},{33,49},{49,1},{2,18}... | collective-permute-start | bytes 1179656 | tf_op jit(solution)/shard_map/ppermute | solution.py:22
  36.7 16.3 %collective-permute-start.12 = (bf16[256,768]{1,0:T(8,128)(2,1)S(1)}, bf16[256,768]{1,0:T(8,128)(2,1)S(1)}, u32[]{:S(2)}, u32[]{:S(2)}) collective-permute-start(bf16[256,768]{1,0:T(8,128)(2,1)S(1)} %collective-permute-done.refs_0_), channel_id=1, source_target_pairs={{0,48},{16,0},{32,16},{48,32},{1,49},{17,1},{33,17},{49,33},{2,50}... | collective-permute-start | bytes 1179656 | tf_op jit(solution)/shard_map/ppermute | solution.py:22
  39.3 11.0 %collective-permute-start.1 = (bf16[256,768]{1,0:T(8,128)(2,1)}, bf16[256,768]{1,0:T(8,128)(2,1)S(1)}, u32[]{:S(2)}, u32[]{:S(2)}) collective-permute-start(bf16[256,768]{1,0:T(8,128)(2,1)} %get-tuple-element.48), channel_id=1, source_target_pairs={{0,64},{8,72},{64,128},{72,136},{128,192},{136,200},{192,8},{200,0... | collective-permute-start | bytes 1179656 | tf_op jit(solution)/shard_map/ppermute | solution.py:65
  40.8 13.1 %collective-permute-start.2 = (bf16[256,768]{1,0:T(8,128)(2,1)}, bf16[256,768]{1,0:T(8,128)(2,1)S(1)}, u32[]{:S(2)}, u32[]{:S(2)}) collective-permute-start(bf16[256,768]{1,0:T(8,128)(2,1)} %get-tuple-element.47), channel_id=1, source_target_pairs={{0,200},{8,192},{64,0},{72,8},{128,64},{136,72},{192,128},{200,136... | collective-permute-start | bytes 1179656 | tf_op jit(solution)/shard_map/ppermute | solution.py:65
  50.3 9.6 %collective-permute-start.14 = (bf16[256,768]{1,0:T(8,128)(2,1)S(1)}, bf16[256,768]{1,0:T(8,128)(2,1)S(1)}, u32[]{:S(2)}, u32[]{:S(2)}) collective-permute-start(bf16[256,768]{1,0:T(8,128)(2,1)S(1)} %collective-permute-done.1.refs_4_), channel_id=1, source_target_pairs={{0,16},{16,32},{32,48},{48,0},{1,17},{17,33},{33,49},{49,1},{2,18}... | collective-permute-start | bytes 1179656 | tf_op jit(solution)/shard_map/ppermute | solution.py:22
  50.3 9.7 %collective-permute-start.15 = (bf16[256,768]{1,0:T(8,128)(2,1)S(1)}, bf16[256,768]{1,0:T(8,128)(2,1)S(1)}, u32[]{:S(2)}, u32[]{:S(2)}) collective-permute-start(bf16[256,768]{1,0:T(8,128)(2,1)S(1)} %collective-permute-done.1.refs_4_), channel_id=1, source_target_pairs={{0,48},{16,0},{32,16},{48,32},{1,49},{17,1},{33,17},{49,33},{2,50}... | collective-permute-start | bytes 1179656 | tf_op jit(solution)/shard_map/ppermute | solution.py:22
  53.8 38.2 %collective-permute-start.13 = (bf16[256,768]{1,0:T(8,128)(2,1)}, bf16[256,768]{1,0:T(8,128)(2,1)}, u32[]{:S(2)}, u32[]{:S(2)}) collective-permute-start(bf16[256,768]{1,0:T(8,128)(2,1)} %broadcast_select_fusion.1), channel_id=1, source_target_pairs={{0,16},{1,49},{16,32},{17,1},{32,48},{33,17},{48,0},{49,33},{2,18}... | collective-permute-start | bytes 1179656 | tf_op jit(solution)/shard_map/ppermute | solution.py:329
  54.7 22.7 %collective-permute-start.3 = (bf16[256,768]{1,0:T(8,128)(2,1)}, bf16[256,768]{1,0:T(8,128)(2,1)}, u32[]{:S(2)}, u32[]{:S(2)}) collective-permute-start(bf16[256,768]{1,0:T(8,128)(2,1)} %select_select_fusion), channel_id=1, source_target_pairs={{64,128},{128,64},{0,200},{192,8},{72,136},{136,72},{8,192},{200,0... | collective-permute-start | bytes 1179656 | tf_op jit(solution)/shard_map/ppermute | solution.py:79
  55.9 23.1 %collective-permute-start.5 = (bf16[256,768]{1,0:T(8,128)(2,1)S(1)}, bf16[256,768]{1,0:T(8,128)(2,1)S(1)}, u32[]{:S(2)}, u32[]{:S(2)}) collective-permute-start(bf16[256,768]{1,0:T(8,128)(2,1)S(1)} %collective-permute-done.2.refs_0_), channel_id=1, source_target_pairs={{0,16},{16,32},{32,48},{48,0},{1,17},{17,33},{33,49},{49,1},{2,18}... | collective-permute-start | bytes 1179656 | tf_op jit(solution)/shard_map/ppermute | solution.py:22
  59.9 20.7 %collective-permute-start.6 = (bf16[256,768]{1,0:T(8,128)(2,1)S(1)}, bf16[256,768]{1,0:T(8,128)(2,1)}, u32[]{:S(2)}, u32[]{:S(2)}) collective-permute-start(bf16[256,768]{1,0:T(8,128)(2,1)S(1)} %collective-permute-done.2.refs_0_), channel_id=1, source_target_pairs={{0,48},{16,0},{32,16},{48,32},{1,49},{17,1},{33,17},{49,33},{2,50}... | collective-permute-start | bytes 1179656 | tf_op jit(solution)/shard_map/ppermute | solution.py:22
  61.6 30.4 %collective-permute-start.16 = (bf16[256,768]{1,0:T(8,128)(2,1)}, bf16[256,768]{1,0:T(8,128)(2,1)}, u32[]{:S(2)}, u32[]{:S(2)}) collective-permute-start(bf16[256,768]{1,0:T(8,128)(2,1)} %broadcast_select_fusion), channel_id=1, source_target_pairs={{0,16},{1,49},{16,32},{17,1},{32,48},{33,17},{48,0},{49,33},{2,18}... | collective-permute-start | bytes 1179656 | tf_op jit(solution)/shard_map/ppermute | solution.py:329
  66.3 25.7 %copy-start = (bf16[1024,4096]{1,0:T(8,128)(2,1)S(1)}, bf16[1024,4096]{1,0:T(8,128)(2,1)}, u32[]{:S(2)}) copy-start(bf16[1024,4096]{1,0:T(8,128)(2,1)} %all-gather.2.cloned.1.call-done.left) | copy-start | bytes 25165828
  66.3 25.7 %copy-start.13 = (s32[8]{0:T(128)S(1)}, s32[8]{0:T(128)}, u32[]{:S(2)}) copy-start(s32[8]{0:T(128)} %stack.71.places) | copy-start | bytes 100
  77.4 14.6 %copy-start.3 = (bf16[256,768]{1,0:T(8,128)(2,1)S(1)}, bf16[256,768]{1,0:T(8,128)(2,1)}, u32[]{:S(2)}) copy-start(bf16[256,768]{1,0:T(8,128)(2,1)} %copy-done.2) | copy-start | bytes 1179652
  77.5 14.6 %copy-start.5 = (bf16[256,768]{1,0:T(8,128)(2,1)S(1)}, bf16[256,768]{1,0:T(8,128)(2,1)}, u32[]{:S(2)}) copy-start(bf16[256,768]{1,0:T(8,128)(2,1)} %copy-done.4) | copy-start | bytes 1179652
  77.5 19.1 %collective-permute-start.8 = (bf16[256,768]{1,0:T(8,128)(2,1)}, bf16[256,768]{1,0:T(8,128)(2,1)S(1)}, u32[]{:S(2)}, u32[]{:S(2)}) collective-permute-start(bf16[256,768]{1,0:T(8,128)(2,1)} %collective-permute-done.3.refs_4_), channel_id=1, source_target_pairs={{0,16},{16,32},{32,48},{48,0},{1,17},{17,33},{33,49},{49,1},{2,18}... | collective-permute-start | bytes 1179656 | tf_op jit(solution)/shard_map/ppermute | solution.py:22
  79.0 17.5 %collective-permute-start.9 = (bf16[256,768]{1,0:T(8,128)(2,1)}, bf16[256,768]{1,0:T(8,128)(2,1)S(1)}, u32[]{:S(2)}, u32[]{:S(2)}) collective-permute-start(bf16[256,768]{1,0:T(8,128)(2,1)} %collective-permute-done.3.refs_4_), channel_id=1, source_target_pairs={{0,48},{16,0},{32,16},{48,32},{1,49},{17,1},{33,17},{49,33},{2,50}... | collective-permute-start | bytes 1179656 | tf_op jit(solution)/shard_map/ppermute | solution.py:22
  80.6 8.9 %collective-permute-start.10 = (bf16[176,256]{1,0:T(8,128)(2,1)S(1)}, bf16[176,256]{1,0:T(8,128)(2,1)S(1)}, u32[]{:S(2)}, u32[]{:S(2)}) collective-permute-start(bf16[176,256]{1,0:T(8,128)(2,1)S(1)} %pad_maximum_fusion), channel_id=1, source_target_pairs={{0,8},{8,16},{16,24},{24,32},{32,40},{40,48},{48,56},{56,64},{64,7... | collective-permute-start | bytes 270344 | tf_op jit(solution)/shard_map/ppermute | solution.py:309
  89.5 13.4 %collective-permute-start.7 = (bf16[256,768]{1,0:T(8,128)(2,1)S(1)}, bf16[256,768]{1,0:T(8,128)(2,1)S(1)}, u32[]{:S(2)}, u32[]{:S(2)}) collective-permute-start(bf16[256,768]{1,0:T(8,128)(2,1)S(1)} %broadcast_select_fusion.3), channel_id=1, source_target_pairs={{0,16},{1,49},{16,32},{17,1},{32,48},{33,17},{48,0},{49,33},{2,18}... | collective-permute-start | bytes 1179656 | tf_op jit(solution)/shard_map/ppermute | solution.py:329
  96.6 6.7 %collective-permute-start.17 = (bf16[256,768]{1,0:T(8,128)(2,1)S(1)}, bf16[256,768]{1,0:T(8,128)(2,1)S(1)}, u32[]{:S(2)}, u32[]{:S(2)}) collective-permute-start(bf16[256,768]{1,0:T(8,128)(2,1)S(1)} %broadcast_select_fusion.2), channel_id=1, source_target_pairs={{0,16},{1,49},{16,32},{17,1},{32,48},{33,17},{48,0},{49,33},{2,18}... | collective-permute-start | bytes 1179656 | tf_op jit(solution)/shard_map/ppermute | solution.py:329
  108.1 12.0 %collective-permute-start.18 = (bf16[176,256]{1,0:T(8,128)(2,1)S(1)}, bf16[176,256]{1,0:T(8,128)(2,1)S(1)}, u32[]{:S(2)}, u32[]{:S(2)}) collective-permute-start(bf16[176,256]{1,0:T(8,128)(2,1)S(1)} %pad_maximum_fusion.1), channel_id=1, source_target_pairs={{0,8},{8,16},{16,24},{24,32},{32,40},{40,48},{48,56},{56,64},{64,7... | collective-permute-start | bytes 270344 | tf_op jit(solution)/shard_map/ppermute | solution.py:309
  (35 other events, 273.7 us)
Sparse Core Ops, SparseCore 0:
  9.7 56.5 all-gather.1

commit v10 on v9

--- a/solution.py
+++ b/solution.py
@@ -305,9 +305,6 @@
 
     next_half = [(i, i + 1) for i in range(contexts * lax.axis_size("z_hi") - 1)]
 
-    def halo_of(projected, short):
-        return lax.ppermute(tail_of(projected, short, starts), ("z_lo", "x", "z_hi"), next_half)
-
     own_short = short_filter.reshape(3 * taps, channels).astype(jnp.float32)
     other_short = other_short.astype(jnp.float32)
     own_projected = lax.dot_general(
@@ -318,11 +315,9 @@
     columns = (*columns[:3], (columns[3][0], mine))
     rows_of = [spread_rows(mine) for _, mine in columns]
     pieces, places = [], []
-    other_halo = halo_of(own_projected, own_short)
     half = 8
     for n, ((by, mine), (below, above, onward)) in enumerate(zip(columns, rows_of)):
         if n == 2:
-            pieces[0], other_halo = lax.optimization_barrier((pieces[0], other_halo))
             first_sum = add_product(gathered, pieces, places, None, jnp.float32)
         if n == 3:
             onward, first_sum = lax.optimization_barrier((onward, first_sum))
@@ -333,7 +328,11 @@
     gated = mix_conv(own_projected, nothing, own_short, own_band, starts, length, None, 0)
     first_sum, gated = lax.optimization_barrier((first_sum, gated))
     other_projected = add_product(gathered, pieces[half:], places[half:], first_sum, jnp.bfloat16)
-    own_halo = halo_of(other_projected, other_short)
+    tails = jnp.concatenate(
+        [tail_of(other_projected, other_short, starts), tail_of(own_projected, own_short, starts)], axis=0
+    )
+    halos = lax.ppermute(tails, ("z_lo", "x", "z_hi"), next_half)
+    own_halo, other_halo = halos[: SPAN + 3 * RIM], halos[SPAN + 3 * RIM :]
     gated = mix_conv(other_projected, other_halo, other_short, other_band, starts, length, gated, 1)
     gated = mix_conv(own_projected, own_halo, own_short, own_band, starts, 2 * SPAN, gated, 0)
     returned = lax.all_to_all(gated, ("y", "core"), split_axis=0, concat_axis=0, tiled=True)

time: 156 us -> 157 us (level)
  the two profiles are of different devices: /device:TPU:1 before, /device:TPU:32 now
where the time goes in v10:
time: 157 us
  starting transfers between devices  32.4 us (21%)
  waiting for transfers between devices  31.4 us (20%)
  Pallas kernels  21.8 us (14%)
  local copies, waits for them, and re-layouts  19.1 us (12%)
  blocking collectives  19.1 us (12%)
  between operations  14.2 us (9%)
  matrix products  11.1 us (7%)
  other arithmetic  8.35 us (5%)
    all_to_all x1, blocking collectives, per_device(): lax.all_to_all(gated, ('y', 'core'), split_axis=0, concat_axis=0, tiled=T...  19.1 us
    ppermute x8, starting transfers between devices, shift(): lax.ppermute(value, axis, [(i, (i + by) % size) for i in range(size)])  13.3 us
    ppermute x1, waiting for transfers between devices, per_device(): halos = lax.ppermute(tails, ('z_lo', 'x', 'z_hi'), next_half)  12.7 us
    dot_general x1, matrix products, per_device(): lax.dot_general(gathered, weight_t, (((1,), (1,)), ((), ())), preferred_e...  11.1 us
    pallas_call x3, Pallas kernels, mix_conv(): pl.pallas_call(body, out_shape=jax.ShapeDtypeStruct((length, 2 * channels...  10.9 us
    ppermute x8, waiting for transfers between devices, shift(): lax.ppermute(value, axis, [(i, (i + by) % size) for i in range(size)])  10.6 us
    pallas_call x2, Pallas kernels, add_product(): pl.pallas_call(functools.partial(add_product_kernel, count), out_shape=ja...  9.13 us
    optimization_barrier x1, local copies, waits for them, and re-layouts, per_device(): in_weight, normed = lax.optimization_barrier((in_weight, normed))  8.8 us
  transfers between devices with their start and end apart: 19, of which 7 were waited for; matrix products, arithmetic and copies ran while one was open for 21% of the time, Pallas kernels for 6%

profile of v10, /device:TPU:32, one launch (start us, length us, event | category | flops | bytes accessed | tf_op | source)
XLA Modules:
  0.0 157.3 jit_solution(5009523888224391800)
XLA Ops:
  10.4 5.5 %collective-permute-start = (bf16[256,768]{1,0:T(8,128)(2,1)S(1)}, bf16[256,768]{1,0:T(8,128)(2,1)S(1)}, u32[]{:S(2)}, u32[]{:S(2)}) collective-permute-start(bf16[256,768]{1,0:T(8,128)(2,1)S(1)} %copy.24), channel_id=1, source_target_pairs={{0,136},{8,128},{64,200},{72,192},{128,8},{136,0},{192,72},{200,64... | collective-permute-start | bytes 1179656 | tf_op jit(solution)/shard_map/ppermute | solution.py:55
  15.9 1.5 collective-permute-start.4
  21.3 8.8 %copy.25 = bf16[4096,3,256]{0,2,1:T(8,128)(2,1)} copy(bf16[4096,3,256]{2,0,1:T(8,128)(2,1)} %param.8) | data formatting | bytes 12582912 | tf_op jit(solution)/shard_map/optimization_barrier | solution.py:292
  39.6 1.8 %collective-permute-start.11 = (bf16[256,768]{1,0:T(8,128)(2,1)S(1)}, bf16[256,768]{1,0:T(8,128)(2,1)S(1)}, u32[]{:S(2)}, u32[]{:S(2)}) collective-permute-start(bf16[256,768]{1,0:T(8,128)(2,1)S(1)} %collective-permute-done.refs_0_), channel_id=1, source_target_pairs={{0,48},{16,0},{32,16},{48,32},{1,49},{17,1},{33,17},{49,33},{2,50}... | collective-permute-start | bytes 1179656 | tf_op jit(solution)/shard_map/ppermute | solution.py:22
  42.9 3.8 %collective-permute-done.1.refs_4_ = bf16[256,768]{1,0:T(8,128)(2,1)S(1)} collective-permute-done((bf16[256,768]{1,0:T(8,128)(2,1)}, bf16[256,768]{1,0:T(8,128)(2,1)S(1)}, u32[]{:S(2)}, u32[]{:S(2)}) %collective-permute-start.1) | collective-permute-done | bytes 393248 | tf_op jit(solution)/shard_map/ppermute | solution.py:65
  46.7 1.5 collective-permute-start.13
  48.3 1.7 %collective-permute-start.14 = (bf16[256,768]{1,0:T(8,128)(2,1)S(1)}, bf16[256,768]{1,0:T(8,128)(2,1)S(1)}, u32[]{:S(2)}, u32[]{:S(2)}) collective-permute-start(bf16[256,768]{1,0:T(8,128)(2,1)S(1)} %collective-permute-done.1.refs_4_), channel_id=1, source_target_pairs={{0,48},{16,0},{32,16},{48,32},{1,49},{17,1},{33,17},{49,33},{2,50}... | collective-permute-start | bytes 1179656 | tf_op jit(solution)/shard_map/ppermute | solution.py:22
  52.8 1.5 collective-permute-start.5
  54.3 5.3 %collective-permute-done.13.refs_5_ = bf16[256,768]{1,0:T(8,128)(2,1)S(1)} collective-permute-done((bf16[256,768]{1,0:T(8,128)(2,1)S(1)}, bf16[256,768]{1,0:T(8,128)(2,1)S(1)}, u32[]{:S(2)}, u32[]{:S(2)}) %collective-permute-start.13) | collective-permute-done | bytes 393248 | tf_op jit(solution)/shard_map/ppermute | solution.py:22
  59.6 2.0 %collective-permute-start.6 = (bf16[256,768]{1,0:T(8,128)(2,1)S(1)}, bf16[256,768]{1,0:T(8,128)(2,1)}, u32[]{:S(2)}, u32[]{:S(2)}) collective-permute-start(bf16[256,768]{1,0:T(8,128)(2,1)S(1)} %collective-permute-done.2.refs_0_), channel_id=1, source_target_pairs={{0,48},{16,0},{32,16},{48,32},{1,49},{17,1},{33,17},{49,33},{2,50}... | collective-permute-start | bytes 1179656 | tf_op jit(solution)/shard_map/ppermute | solution.py:22
  63.5 1.8 %all-gather.2.cloned.1.call-done.left = bf16[1024,4096]{1,0:T(8,128)(2,1)} async-done(((bf16[128,4096]{1,0:T(8,128)(2,1)}), bf16[1024,4096]{1,0:T(8,128)(2,1)}) %all-gather.2.cloned.1.call-update) | async-done | bytes 8388624 | tf_op jit(solution)/shard_map/all_gather | solution.py:293
  65.3 11.1 %convolution_convert_fusion.refs_1_.proj = bf16[1024,768]{1,0:T(8,128)(2,1)S(1)} fusion(bf16[1024,4096]{1,0:T(8,128)(2,1)} %all-gather.2.cloned.1.call-done.left, bf16[768,4096]{1,0:T(8,128)(2,1)} %bitcast.54), kind=kOutput, calls=%fused_computation.5 | convolution fusion | flops 6443237376 | bytes 16252928 | tf_op jit(solution)/shard_map/dot_general | solution.py:310
  76.4 1.6 collective-permute-start.8
  78.0 1.8 %collective-permute-start.9 = (bf16[256,768]{1,0:T(8,128)(2,1)}, bf16[256,768]{1,0:T(8,128)(2,1)S(1)}, u32[]{:S(2)}, u32[]{:S(2)}) collective-permute-start(bf16[256,768]{1,0:T(8,128)(2,1)} %collective-permute-done.3.refs_4_), channel_id=1, source_target_pairs={{0,48},{16,0},{32,16},{48,32},{1,49},{17,1},{33,17},{49,33},{2,50}... | collective-permute-start | bytes 1179656 | tf_op jit(solution)/shard_map/ppermute | solution.py:22
  80.2 4.6 %shard_map.64.refs_8_ = f32[1024,768]{1,0:T(8,128)S(1)} custom-call(s32[8]{0:T(128)S(1)} %copy-done.14, bf16[1024,4096]{1,0:T(8,128)(2,1)S(1)} %copy-done, bf16[256,768]{1,0:T(8,128)(2,1)S(1)} %collective-permute-done.refs_0_, bf16[256,768]{1,0:T(8,128)(2,1)S(1)} %collective-permute-done.10.refs_1_, bf16[256,768]{1,0:T(8,128)(2,1)S(1)} %collective-permute-done.11.refs_2_, ...), custom_call_target="tpu_custom_call" | custom-call | flops 3221225472 | bytes 8000000 | tf_op jit(solution)/shard_map/pallas_call | solution.py:115
  84.8 4.4 %collective-permute-done.8.refs_5_ = bf16[256,768]{1,0:T(8,128)(2,1)S(1)} collective-permute-done((bf16[256,768]{1,0:T(8,128)(2,1)}, bf16[256,768]{1,0:T(8,128)(2,1)S(1)}, u32[]{:S(2)}, u32[]{:S(2)}) %collective-permute-start.8) | collective-permute-done | bytes 393248 | tf_op jit(solution)/shard_map/ppermute | solution.py:22
  90.2 1.5 collective-permute-start.16
  91.8 4.8 %shard_map.66.into = bf16[1024,512]{1,0:T(8,128)(2,1)S(1)} custom-call(s32[8]{0:T(128)S(1)} %copy-done.16, bf16[1024,768]{1,0:T(8,128)(2,1)S(1)} %convolution_convert_fusion.refs_1_.proj, bf16[176,256]{1,0:T(8,128)(2,1)S(1)} %broadcast_in_dim.96.refs_2_, f32[9,256]{1,0:T(8,128)S(1)} %copy-done.9, bf16[16,256,128]{2,1,0:T(8,128)(2,1)S(1)} %copy-done.18, ...), custom_call_target="tpu_custom_call" | custom-call | flops 6144000000 | bytes 4000000 | tf_op jit(solution)/shard_map/pallas_call | solution.py:231
  96.8 2.5 %collective-permute-done.16.refs_7_ = bf16[256,768]{1,0:T(8,128)(2,1)S(1)} collective-permute-done((bf16[256,768]{1,0:T(8,128)(2,1)S(1)}, bf16[256,768]{1,0:T(8,128)(2,1)S(1)}, u32[]{:S(2)}, u32[]{:S(2)}) %collective-permute-start.16) | collective-permute-done | bytes 393248 | tf_op jit(solution)/shard_map/ppermute | solution.py:324
  99.3 4.5 %shard_map.67.proj = bf16[1024,768]{1,0:T(8,128)(2,1)S(1)} custom-call(s32[8]{0:T(128)S(1)} %copy-done.13, bf16[1024,4096]{1,0:T(8,128)(2,1)S(1)} %copy-done, bf16[256,768]{1,0:T(8,128)(2,1)S(1)} %collective-permute-done.2.refs_0_, bf16[256,768]{1,0:T(8,128)(2,1)S(1)} %collective-permute-done.5.refs_1_, bf16[256,768]{1,0:T(8,128)(2,1)} %collective-permute-done.6.refs_2_, ...), custom_call_target="tpu_custom_call" | custom-call | flops 3221225472 | bytes 8000000 | tf_op jit(solution)/shard_map/pallas_call | solution.py:115
  104.3 6.7 %collective-permute-start.17 = (bf16[352,256]{1,0:T(8,128)(2,1)S(1)}, bf16[352,256]{1,0:T(8,128)(2,1)S(1)}, u32[]{:S(2)}, u32[]{:S(2)}) collective-permute-start(bf16[352,256]{1,0:T(8,128)(2,1)S(1)} %constant_dynamic-update-slice_fusion), channel_id=1, source_target_pairs={{0,8},{8,16},{16,24},{24,32},{32,40},{40,48},{48,56},{56,64},{64,7... | collective-permute-start | bytes 540680 | tf_op jit(solution)/shard_map/ppermute | solution.py:334
  111.3 12.7 %collective-permute-done.17 = bf16[352,256]{1,0:T(8,128)(2,1)S(1)} collective-permute-done((bf16[352,256]{1,0:T(8,128)(2,1)S(1)}, bf16[352,256]{1,0:T(8,128)(2,1)S(1)}, u32[]{:S(2)}, u32[]{:S(2)}) %collective-permute-start.17) | collective-permute-done | bytes 180256 | tf_op jit(solution)/shard_map/ppermute | solution.py:334
  124.0 4.6 %shard_map.69.into = bf16[1024,512]{1,0:T(8,128)(2,1)S(1)} custom-call(s32[8]{0:T(128)S(1)} %copy-done.16, bf16[1024,768]{1,0:T(8,128)(2,1)S(1)} %shard_map.67.proj, bf16[176,256]{1,0:T(8,128)(2,1)S(1)} %get-tuple-element.39.halo, f32[9,256]{1,0:T(8,128)S(1)} %slice_convert_fusion.short, ...), custom_call_target="tpu_custom_call", output_to_operand_aliasing={{}: (7, {})} | custom-call | flops 6144000000 | bytes 4000000 | tf_op jit(solution)/shard_map/pallas_call | solution.py:231
  130.1 19.1 %all_to_all.11 = bf16[8,128,512]{2,1,0:T(8,128)(2,1)S(1)} all-to-all(bf16[8,128,512]{2,1,0:T(8,128)(2,1)S(1)} %bitcast.48), channel_id=1, replica_groups=mesh['z_lo'=4,'x'=4,'z_hi'=2,'y'=4,'core'=2] {'y','core'}, dimensions={0} | all-to-all | bytes 2097152 | tf_op jit(solution)/shard_map/all_to_all | solution.py:338
  (148 shorter events, 28.1 us)
Async XLA Ops:
  6.5 58.7 %all-gather.2.cloned.1.call-start = ((), (), s32[]{:S(2)}) async-start(), calls=%async_computation.1 | async-start | bytes 9437184 | tf_op jit(solution)/shard_map/all_gather | solution.py:293
  10.4 24.6 %collective-permute-start = (bf16[256,768]{1,0:T(8,128)(2,1)S(1)}, bf16[256,768]{1,0:T(8,128)(2,1)S(1)}, u32[]{:S(2)}, u32[]{:S(2)}) collective-permute-start(bf16[256,768]{1,0:T(8,128)(2,1)S(1)} %copy.24), channel_id=1, source_target_pairs={{0,136},{8,128},{64,200},{72,192},{128,8},{136,0},{192,72},{200,64... | collective-permute-start | bytes 1179656 | tf_op jit(solution)/shard_map/ppermute | solution.py:55
  15.9 18.5 %collective-permute-start.4 = (bf16[17,256]{1,0:T(8,128)(2,1)S(1)}, bf16[17,256]{1,0:T(8,128)(2,1)S(1)}, u32[]{:S(2)}, u32[]{:S(2)}) collective-permute-start(bf16[17,256]{1,0:T(8,128)(2,1)S(1)} %pad_maximum_fusion), channel_id=1, source_target_pairs={{0,8},{8,0},{1,9},{9,1},{2,10},{10,2},{3,11},{11,3},{4,12},{12,4},... | collective-permute-start | bytes 26120 | tf_op jit(solution)/shard_map/ppermute | solution.py:17
  17.5 15.5 %copy-start.11 = (s32[256]{0:T(256)}, s32[256]{0:T(256)S(1)}, u32[]{:S(2)}) copy-start(s32[256]{0:T(256)S(1)} %get-tuple-element.53) | copy-start | bytes 3076
  36.1 10.6 %collective-permute-start.1 = (bf16[256,768]{1,0:T(8,128)(2,1)}, bf16[256,768]{1,0:T(8,128)(2,1)S(1)}, u32[]{:S(2)}, u32[]{:S(2)}) collective-permute-start(bf16[256,768]{1,0:T(8,128)(2,1)} %get-tuple-element.38), channel_id=1, source_target_pairs={{0,64},{8,72},{64,128},{72,136},{128,192},{136,200},{192,8},{200,0... | collective-permute-start | bytes 1179656 | tf_op jit(solution)/shard_map/ppermute | solution.py:65
  36.8 13.2 %collective-permute-start.2 = (bf16[256,768]{1,0:T(8,128)(2,1)}, bf16[256,768]{1,0:T(8,128)(2,1)S(1)}, u32[]{:S(2)}, u32[]{:S(2)}) collective-permute-start(bf16[256,768]{1,0:T(8,128)(2,1)} %get-tuple-element.37), channel_id=1, source_target_pairs={{0,200},{8,192},{64,0},{72,8},{128,64},{136,72},{192,128},{200,136... | collective-permute-start | bytes 1179656 | tf_op jit(solution)/shard_map/ppermute | solution.py:65
  38.1 13.2 %collective-permute-start.10 = (bf16[256,768]{1,0:T(8,128)(2,1)S(1)}, bf16[256,768]{1,0:T(8,128)(2,1)S(1)}, u32[]{:S(2)}, u32[]{:S(2)}) collective-permute-start(bf16[256,768]{1,0:T(8,128)(2,1)S(1)} %collective-permute-done.refs_0_), channel_id=1, source_target_pairs={{0,16},{16,32},{32,48},{48,0},{1,17},{17,33},{33,49},{49,1},{2,18}... | collective-permute-start | bytes 1179656 | tf_op jit(solution)/shard_map/ppermute | solution.py:22
  39.6 11.8 %collective-permute-start.11 = (bf16[256,768]{1,0:T(8,128)(2,1)S(1)}, bf16[256,768]{1,0:T(8,128)(2,1)S(1)}, u32[]{:S(2)}, u32[]{:S(2)}) collective-permute-start(bf16[256,768]{1,0:T(8,128)(2,1)S(1)} %collective-permute-done.refs_0_), channel_id=1, source_target_pairs={{0,48},{16,0},{32,16},{48,32},{1,49},{17,1},{33,17},{49,33},{2,50}... | collective-permute-start | bytes 1179656 | tf_op jit(solution)/shard_map/ppermute | solution.py:22
  46.7 12.8 %collective-permute-start.13 = (bf16[256,768]{1,0:T(8,128)(2,1)S(1)}, bf16[256,768]{1,0:T(8,128)(2,1)S(1)}, u32[]{:S(2)}, u32[]{:S(2)}) collective-permute-start(bf16[256,768]{1,0:T(8,128)(2,1)S(1)} %collective-permute-done.1.refs_4_), channel_id=1, source_target_pairs={{0,16},{16,32},{32,48},{48,0},{1,17},{17,33},{33,49},{49,1},{2,18}... | collective-permute-start | bytes 1179656 | tf_op jit(solution)/shard_map/ppermute | solution.py:22
  48.3 13.3 %collective-permute-start.14 = (bf16[256,768]{1,0:T(8,128)(2,1)S(1)}, bf16[256,768]{1,0:T(8,128)(2,1)S(1)}, u32[]{:S(2)}, u32[]{:S(2)}) collective-permute-start(bf16[256,768]{1,0:T(8,128)(2,1)S(1)} %collective-permute-done.1.refs_4_), channel_id=1, source_target_pairs={{0,48},{16,0},{32,16},{48,32},{1,49},{17,1},{33,17},{49,33},{2,50}... | collective-permute-start | bytes 1179656 | tf_op jit(solution)/shard_map/ppermute | solution.py:22
  50.8 25.6 %collective-permute-start.3 = (bf16[256,768]{1,0:T(8,128)(2,1)}, bf16[256,768]{1,0:T(8,128)(2,1)}, u32[]{:S(2)}, u32[]{:S(2)}) collective-permute-start(bf16[256,768]{1,0:T(8,128)(2,1)} %select_select_fusion), channel_id=1, source_target_pairs={{64,128},{128,64},{0,200},{192,8},{72,136},{136,72},{8,192},{200,0... | collective-permute-start | bytes 1179656 | tf_op jit(solution)/shard_map/ppermute | solution.py:79
  52.2 28.0 %collective-permute-start.12 = (bf16[256,768]{1,0:T(8,128)(2,1)}, bf16[256,768]{1,0:T(8,128)(2,1)}, u32[]{:S(2)}, u32[]{:S(2)}) collective-permute-start(bf16[256,768]{1,0:T(8,128)(2,1)} %broadcast_select_fusion.1), channel_id=1, source_target_pairs={{0,16},{1,49},{16,32},{17,1},{32,48},{33,17},{48,0},{49,33},{2,18}... | collective-permute-start | bytes 1179656 | tf_op jit(solution)/shard_map/ppermute | solution.py:324
  52.8 25.1 %collective-permute-start.5 = (bf16[256,768]{1,0:T(8,128)(2,1)S(1)}, bf16[256,768]{1,0:T(8,128)(2,1)S(1)}, u32[]{:S(2)}, u32[]{:S(2)}) collective-permute-start(bf16[256,768]{1,0:T(8,128)(2,1)S(1)} %collective-permute-done.2.refs_0_), channel_id=1, source_target_pairs={{0,16},{16,32},{32,48},{48,0},{1,17},{17,33},{33,49},{49,1},{2,18}... | collective-permute-start | bytes 1179656 | tf_op jit(solution)/shard_map/ppermute | solution.py:22
  59.6 20.1 %collective-permute-start.6 = (bf16[256,768]{1,0:T(8,128)(2,1)S(1)}, bf16[256,768]{1,0:T(8,128)(2,1)}, u32[]{:S(2)}, u32[]{:S(2)}) collective-permute-start(bf16[256,768]{1,0:T(8,128)(2,1)S(1)} %collective-permute-done.2.refs_0_), channel_id=1, source_target_pairs={{0,48},{16,0},{32,16},{48,32},{1,49},{17,1},{33,17},{49,33},{2,50}... | collective-permute-start | bytes 1179656 | tf_op jit(solution)/shard_map/ppermute | solution.py:22
  63.3 16.9 %collective-permute-start.15 = (bf16[256,768]{1,0:T(8,128)(2,1)}, bf16[256,768]{1,0:T(8,128)(2,1)}, u32[]{:S(2)}, u32[]{:S(2)}) collective-permute-start(bf16[256,768]{1,0:T(8,128)(2,1)} %broadcast_select_fusion), channel_id=1, source_target_pairs={{0,16},{1,49},{16,32},{17,1},{32,48},{33,17},{48,0},{49,33},{2,18}... | collective-permute-start | bytes 1179656 | tf_op jit(solution)/shard_map/ppermute | solution.py:324
  65.2 14.9 %copy-start = (bf16[1024,4096]{1,0:T(8,128)(2,1)S(1)}, bf16[1024,4096]{1,0:T(8,128)(2,1)}, u32[]{:S(2)}) copy-start(bf16[1024,4096]{1,0:T(8,128)(2,1)} %all-gather.2.cloned.1.call-done.left) | copy-start | bytes 25165828
  65.2 14.9 %copy-start.3 = (bf16[256,768]{1,0:T(8,128)(2,1)S(1)}, bf16[256,768]{1,0:T(8,128)(2,1)}, u32[]{:S(2)}) copy-start(bf16[256,768]{1,0:T(8,128)(2,1)} %copy-done.2) | copy-start | bytes 1179652
  65.2 14.9 %copy-start.5 = (bf16[256,768]{1,0:T(8,128)(2,1)S(1)}, bf16[256,768]{1,0:T(8,128)(2,1)}, u32[]{:S(2)}) copy-start(bf16[256,768]{1,0:T(8,128)(2,1)} %copy-done.4) | copy-start | bytes 1179652
  65.3 14.9 %copy-start.14 = (s32[8]{0:T(128)S(1)}, s32[8]{0:T(128)}, u32[]{:S(2)}) copy-start(s32[8]{0:T(128)} %stack.71.places) | copy-start | bytes 100
  76.4 12.8 %collective-permute-start.8 = (bf16[256,768]{1,0:T(8,128)(2,1)}, bf16[256,768]{1,0:T(8,128)(2,1)S(1)}, u32[]{:S(2)}, u32[]{:S(2)}) collective-permute-start(bf16[256,768]{1,0:T(8,128)(2,1)} %collective-permute-done.3.refs_4_), channel_id=1, source_target_pairs={{0,16},{16,32},{32,48},{48,0},{1,17},{17,33},{33,49},{49,1},{2,18}... | collective-permute-start | bytes 1179656 | tf_op jit(solution)/shard_map/ppermute | solution.py:22
  78.0 12.2 %collective-permute-start.9 = (bf16[256,768]{1,0:T(8,128)(2,1)}, bf16[256,768]{1,0:T(8,128)(2,1)S(1)}, u32[]{:S(2)}, u32[]{:S(2)}) collective-permute-start(bf16[256,768]{1,0:T(8,128)(2,1)} %collective-permute-done.3.refs_4_), channel_id=1, source_target_pairs={{0,48},{16,0},{32,16},{48,32},{1,49},{17,1},{33,17},{49,33},{2,50}... | collective-permute-start | bytes 1179656 | tf_op jit(solution)/shard_map/ppermute | solution.py:22
  79.8 16.9 %collective-permute-start.7 = (bf16[256,768]{1,0:T(8,128)(2,1)S(1)}, bf16[256,768]{1,0:T(8,128)(2,1)S(1)}, u32[]{:S(2)}, u32[]{:S(2)}) collective-permute-start(bf16[256,768]{1,0:T(8,128)(2,1)S(1)} %broadcast_select_fusion.3), channel_id=1, source_target_pairs={{0,16},{1,49},{16,32},{17,1},{32,48},{33,17},{48,0},{49,33},{2,18}... | collective-permute-start | bytes 1179656 | tf_op jit(solution)/shard_map/ppermute | solution.py:324
  90.2 9.1 %collective-permute-start.16 = (bf16[256,768]{1,0:T(8,128)(2,1)S(1)}, bf16[256,768]{1,0:T(8,128)(2,1)S(1)}, u32[]{:S(2)}, u32[]{:S(2)}) collective-permute-start(bf16[256,768]{1,0:T(8,128)(2,1)S(1)} %broadcast_select_fusion.2), channel_id=1, source_target_pairs={{0,16},{1,49},{16,32},{17,1},{32,48},{33,17},{48,0},{49,33},{2,18}... | collective-permute-start | bytes 1179656 | tf_op jit(solution)/shard_map/ppermute | solution.py:324
  104.3 19.6 %collective-permute-start.17 = (bf16[352,256]{1,0:T(8,128)(2,1)S(1)}, bf16[352,256]{1,0:T(8,128)(2,1)S(1)}, u32[]{:S(2)}, u32[]{:S(2)}) collective-permute-start(bf16[352,256]{1,0:T(8,128)(2,1)S(1)} %constant_dynamic-update-slice_fusion), channel_id=1, source_target_pairs={{0,8},{8,16},{16,24},{24,32},{32,40},{40,48},{48,56},{56,64},{64,7... | collective-permute-start | bytes 540680 | tf_op jit(solution)/shard_map/ppermute | solution.py:334
  (32 other events, 242.0 us)
Sparse Core Ops, SparseCore 0:
  10.3 54.8 all-gather.1
